TPU v7x, 256 devices: a whole 4x4x8 slice. The times are simulated.
256 devices in a mesh: grp: 8 (over x, z_lo), lat: 32 (over y, z_hi, core).
Axes of the slice: x: 4, y: 4, z: 8 (z_hi: 4, z_lo: 2; z = z_hi * 2 + z_lo), core: 2. Of those that a mesh axis runs over, the one named last changes fastest.
Arguments:
- inputs: bfloat16 [512, 8192], P('lat'), may hold values from -6 to 6
- dec_bias: float32 [8192], replicated, may hold values from -3 to 3
- weight: bfloat16 [32768, 8192], P(('grp', 'lat')), may hold values from -0.0625 to 0.0625
- enc_bias: float32 [32768], P(('grp', 'lat')), may hold values from -1 to 0.5
- first_moment: bfloat16 [32768, 8192], P(('grp', 'lat')), may hold values from -0.15625 to 0.15625
- second_moment: bfloat16 [32768, 8192], P(('grp', 'lat')), may hold values from 9.953976e-06 to 0.0009994507
Outputs:
- update: bfloat16 [32768, 8192], P(('grp', 'lat'))
- new_first: bfloat16 [32768, 8192], P(('grp', 'lat'))
- new_second: bfloat16 [32768, 8192], P(('grp', 'lat'))
All inputs are finite; a program needn't handle non-finite values.
Results may differ from a plain program's by a relative error of at most 0.014.
The roundings to bfloat16 on the way count: a program that leaves them out, or rounds other values in their place, can miss the bound.
Values may be sent and summed in bfloat16 or wider, within the bound.
No kernel may reach another device: no remote copies, remote signals or barrier semaphores. Data moves between devices by JAX's collectives and lax.ppermute only.
A program may use at most 128 MiB of HBM per device.

v0:
```python
import jax
import jax.numpy as jnp
from jax import lax
from jax.sharding import PartitionSpec as P

STEP = 100


def body(inputs, dec_bias, weight, enc_bias, first_moment, second_moment):
    local_rows = inputs.shape[0]
    source = inputs.astype(jnp.float32)
    centered_local = (source - dec_bias).astype(jnp.bfloat16)
    centered = lax.all_gather(centered_local, "lat", axis=0, tiled=True)
    contract_last = (((1,), (1,)), ((), ()))
    contract_first = (((0,), (0,)), ((), ()))
    preact = (
        lax.dot_general(centered, weight, contract_last, preferred_element_type=jnp.float32)
        + enc_bias
    )
    activity = jnp.maximum(preact, 0.0).astype(jnp.bfloat16)
    group_part = lax.psum_scatter(
        jnp.dot(activity, weight, preferred_element_type=jnp.float32),
        "lat",
        scatter_dimension=0,
        tiled=True,
    )
    recon = lax.psum(group_part, "grp")
    error_local = (recon + dec_bias - source).astype(jnp.bfloat16)
    error_all = lax.all_gather(error_local, "lat", axis=0, tiled=True)
    back = lax.dot_general(error_all, weight, contract_last, preferred_element_type=jnp.float32)
    pre_grad = jnp.where(preact > 0, back, 0.0).astype(jnp.bfloat16)
    grad_sum = lax.dot_general(
        activity, error_all, contract_first, preferred_element_type=jnp.float32
    )
    grad_sum = grad_sum + lax.dot_general(
        pre_grad, centered, contract_first, preferred_element_type=jnp.float32
    )
    gradient = grad_sum / (local_rows * lax.axis_size("lat"))
    first = 0.9 * first_moment.astype(jnp.float32) + 0.1 * gradient
    second = 0.999 * second_moment.astype(jnp.float32) + 0.001 * gradient * gradient
    update = first / (1.0 - 0.9**STEP) / (jnp.sqrt(second / (1.0 - 0.999**STEP)) + 1e-08)
    return (update.astype(jnp.bfloat16), first.astype(jnp.bfloat16), second.astype(jnp.bfloat16))


def solution(mesh):
    return jax.shard_map(
        body,
        mesh=mesh,
        in_specs=(
            P("lat", None),
            P(),
            P(("grp", "lat"), None),
            P(("grp", "lat")),
            P(("grp", "lat"), None),
            P(("grp", "lat"), None),
        ),
        out_specs=(P(("grp", "lat"), None), P(("grp", "lat"), None), P(("grp", "lat"), None)),
        check_vma=False,
    )
```

profile of v0, /device:TPU:1, one launch (start us, length us, event | category | flops | bytes accessed | tf_op | source)
XLA Modules:
  0.0 465.3 jit_solution(16375666848904786505)
XLA Ops:
  7.2 0.0 copy-start
  7.2 0.0 all-gather.3.cloned.1.call-start
  7.2 1.8 fusion.3
  9.1 0.0 all-gather.3.cloned.1.call-update
  9.1 0.0 reduce-scatter.2.cloned.1.call-start
  9.1 82.4 %all-gather.3.cloned.1.call-done = bf16[512,8192]{1,0:T(8,128)(2,1)} async-done(((bf16[16,8192]{1,0:T(8,128)(2,1)}), bf16[512,8192]{1,0:T(8,128)(2,1)}) %all-gather.3.cloned.1.call-update) | async-done | bytes 8388624 | tf_op jit(solution)/shard_map/all_gather | solution.py:13
  91.5 0.0 copy-done
  91.5 5.7 %convolution_add_fusion.1 = f32[512,128]{1,0:T(8,128)S(1)} fusion(bf16[512,8192]{1,0:T(8,128)(2,1)} %all-gather.3.cloned.1.call-done, bf16[128,8192]{1,0:T(8,128)(2,1)S(1)} %copy-done, f32[128]{0:T(128)} %param.9), kind=kOutput, calls=%fused_computation.7 | convolution fusion | flops 1073807360 | bytes 10748416 | tf_op jit(solution)/shard_map/dot_general | solution.py:17
  97.2 8.1 %fusion.8 = f32[512,8192]{1,0:T(8,128)} fusion(bf16[128,8192]{1,0:T(8,128)(2,1)S(1)} %copy-done, f32[512,128]{1,0:T(8,128)S(1)} %convolution_add_fusion.1), kind=kOutput, calls=%fused_computation.17 | convolution fusion | flops 1073872896 | bytes 19136512 | tf_op jit(solution)/shard_map/dot_general | solution.py:22
  105.3 0.0 copy-start.1
  105.3 0.0 copy-start.2
  105.3 0.0 reduce-scatter.2.cloned.1.call-update
  105.3 0.0 all-reduce.2.cloned.1.call-start
  105.4 167.7 %reduce-scatter.2.cloned.1.call-done = f32[16,8192]{1,0:T(8,128)} async-done(((f32[512,8192]{1,0:T(8,128)}), f32[16,8192]{1,0:T(8,128)}) %reduce-scatter.2.cloned.1.call-update) | async-done | bytes 524304 | tf_op jit(solution)/shard_map/reduce_scatter | solution.py:21
  273.1 0.0 all-reduce.2.cloned.1.call-update
  273.1 0.0 all-gather.5.cloned.1.call-start
  273.2 77.1 %all-reduce.2.cloned.1.call-done = f32[16,8192]{1,0:T(8,128)} async-done(((f32[16,8192]{1,0:T(8,128)}), f32[16,8192]{1,0:T(8,128)}) %all-reduce.2.cloned.1.call-update) | async-done | bytes 524304 | tf_op jit(solution)/shard_map/psum | solution.py:27
  350.3 0.0 copy-done.1
  350.3 0.0 copy-done.2
  350.3 1.8 fusion.4
  352.1 0.0 all-gather.5.cloned.1.call-update
  352.1 81.4 %all-gather.5.cloned.1.call-done = bf16[512,8192]{1,0:T(8,128)(2,1)} async-done(((bf16[16,8192]{1,0:T(8,128)(2,1)}), bf16[512,8192]{1,0:T(8,128)(2,1)}) %all-gather.5.cloned.1.call-update) | async-done | bytes 8388624 | tf_op jit(solution)/shard_map/all_gather | solution.py:29
  433.5 6.7 %fusion.7 = f32[128,8192]{1,0:T(8,128)} fusion(bf16[512,8192]{1,0:T(8,128)(2,1)} %all-gather.5.cloned.1.call-done, f32[512,128]{1,0:T(8,128)S(1)} %convolution_add_fusion.1), kind=kOutput, calls=%fused_computation.16 | convolution fusion | flops 1073872896 | bytes 12845056 | tf_op jit(solution)/shard_map/dot_general | solution.py:32
  440.2 18.6 %fusion.1 = (bf16[128,8192]{1,0:T(8,128)(2,1)}, bf16[128,8192]{1,0:T(8,128)(2,1)}, bf16[128,8192]{1,0:T(8,128)(2,1)}) fusion(bf16[128,8192]{1,0:T(8,128)(2,1)} %param.11, bf16[128,8192]{1,0:T(8,128)(2,1)} %param.10, f32[128,8192]{1,0:T(8,128)} %fusion.7, bf16[512,8192]{1,0:T(8,128)(2,1)} %all-gather.3.cloned.1.call-done, ...), kind=kOutput, calls=%fused_computation.5 | convolution fusion | flops 2166554624 | bytes 33816576 | tf_op jit(solution)/shard_map/dot_general | solution.py:35
Async XLA Ops:
  7.2 84.3 %copy-start = (bf16[128,8192]{1,0:T(8,128)(2,1)S(1)}, bf16[128,8192]{1,0:T(8,128)(2,1)}, u32[]{:S(2)}) copy-start(bf16[128,8192]{1,0:T(8,128)(2,1)} %param.8) | copy-start | bytes 6291460
  7.2 84.3 %all-gather.3.cloned.1.call-start = ((), (), s32[]{:S(2)}) async-start(), calls=%async_computation.1 | async-start | bytes 8650752 | tf_op jit(solution)/shard_map/all_gather | solution.py:13
  9.1 264.0 %reduce-scatter.2.cloned.1.call-start = ((), (), s32[]{:S(2)}) async-start(), calls=%async_computation.2 | async-start | bytes 17301504 | tf_op jit(solution)/shard_map/reduce_scatter | solution.py:21
  105.3 245.0 %copy-start.1 = (bf16[16,8192]{1,0:T(8,128)(2,1)S(1)}, bf16[16,8192]{1,0:T(8,128)(2,1)}, u32[]{:S(2)}) copy-start(bf16[16,8192]{1,0:T(8,128)(2,1)} %param.6) | copy-start | bytes 786436
  105.3 245.0 %copy-start.2 = (f32[8192]{0:T(1024)S(1)}, f32[8192]{0:T(1024)}, u32[]{:S(2)}) copy-start(f32[8192]{0:T(1024)} %param.7) | copy-start | bytes 98308
  105.3 245.0 %all-reduce.2.cloned.1.call-start = ((), (), s32[]{:S(2)}) async-start(), calls=%async_computation.3 | async-start | bytes 1048576 | tf_op jit(solution)/shard_map/psum | solution.py:27
  273.1 160.4 %all-gather.5.cloned.1.call-start = ((), (), s32[]{:S(2)}) async-start(), calls=%async_computation.4 | async-start | bytes 8650752 | tf_op jit(solution)/shard_map/all_gather | solution.py:29
Sparse Core Ops, SparseCore 0:
  11.1 80.3 all-gather.2
  105.5 167.5 reduce-scatter.1
  275.7 74.5 all-reduce.1
  353.6 79.8 all-gather.4
where the time goes:
time: 467 us; the launch traced here: 465 us
  waiting for transfers between devices  409 us (88%)
  matrix products  39 us (8%)
  between operations  13.8 us (3%)
    reduce_scatter x1, waiting for transfers between devices, body(): lax.psum_scatter(jnp.dot(activity, weight, preferred_element_type=jnp.flo...  168 us
    all_gather x1, waiting for transfers between devices, body(): centered = lax.all_gather(centered_local, 'lat', axis=0, tiled=True)  82.4 us
    all_gather x1, waiting for transfers between devices, body(): error_all = lax.all_gather(error_local, 'lat', axis=0, tiled=True)  81.4 us
    psum x1, waiting for transfers between devices, body(): recon = lax.psum(group_part, 'grp')  77.1 us
    dot_general x1, matrix products, body(): lax.dot_general(pre_grad, centered, contract_first, preferred_element_typ...  18.6 us
  transfers between devices with their start and end apart: 4, of which 4 were waited for; matrix products, arithmetic and copies ran while one was open for 0% of the time, Pallas kernels for 0%

commit v1 on v0

v1 whole, which is shorter than its diff:
```python
import functools

import jax
import jax.numpy as jnp
from jax import lax
from jax.experimental import pallas as pl
from jax.experimental.pallas import tpu as pltpu
from jax.sharding import Mesh, PartitionSpec as P

STEP = 100
BF16 = jnp.bfloat16
F32 = jnp.float32
SIDE = 4
ORDER = (0, 2, 1, 3)
PLANE = ("x", "y", "c")
Z = ("zh", "zl")
VMEM = pl.BlockSpec(memory_space=pltpu.VMEM)
SMEM = pl.BlockSpec(memory_space=pltpu.SMEM)
PARAMS = pltpu.CompilerParams(vmem_limit_bytes=48 * 1024 * 1024)


def plane_pairs(by, last):
    pairs = []
    for x in range(SIDE):
        for y in range(SIDE):
            for c in range(2):
                along_x = (c == 0) == last
                to_x = (x + by) % SIDE if along_x else x
                to_y = y if along_x else (y + by) % SIDE
                pairs.append(((x * SIDE + y) * 2 + c, (to_x * SIDE + to_y) * 2 + c))
    return pairs


def shift(value, by, last):
    return lax.ppermute(value, PLANE, plane_pairs(by, last))


def swap(value):
    return lax.ppermute(value, "c", [(0, 1), (1, 0)])


def spread(piece, last):
    return [piece] + [shift(piece, by, last) for by in ORDER[1:]]


def call(kernel, out_shape, args, flops, specs=None, params=PARAMS):
    shapes = jax.tree.leaves(out_shape)
    moved = sum(a.size * a.dtype.itemsize for a in list(args) + shapes)
    return pl.pallas_call(
        kernel,
        out_shape=out_shape,
        in_specs=specs or [VMEM] * len(args),
        out_specs=jax.tree.map(lambda _: VMEM, out_shape),
        compiler_params=params,
        cost_estimate=pl.CostEstimate(flops=flops, bytes_accessed=moved, transcendentals=0),
    )(*args)


def project_kernel(place, weight, extra, *refs, centre):
    pieces, (laid, product) = refs[:4], refs[4:]
    thick, part = pieces[0].shape[1:]
    product[...] = jnp.zeros_like(product)
    for i, piece in enumerate(pieces):

        def step(j, carry, i=i, piece=piece):
            row = pl.multiple_of(place[0, i * SIDE + j] * thick, thick)
            column = pl.multiple_of(place[1, i * SIDE + j] * part, part)
            block = piece[j]
            if centre:
                block = (block.astype(F32) - extra[:, pl.ds(column, part)]).astype(BF16)
            laid[pl.ds(row, thick), pl.ds(column, part)] = block
            product[pl.ds(row, thick), :] += lax.dot_general(
                block,
                weight[:, pl.ds(column, part)],
                (((1,), (1,)), ((), ())),
                preferred_element_type=F32,
            )
            return carry

        lax.fori_loop(0, SIDE, step, 0)


def project(place, weight, extra, pieces, centre):
    thick, part = pieces[0].shape[1:]
    rows, width = thick * SIDE, part * SIDE
    return call(
        functools.partial(project_kernel, centre=centre),
        (jax.ShapeDtypeStruct((rows, width), BF16), jax.ShapeDtypeStruct((rows, weight.shape[0]), F32)),
        (place, weight, extra, *pieces),
        2 * rows * width * weight.shape[0],
        [SMEM] + [VMEM] * (2 + SIDE),
    )


def join(own, other, latents):
    return jnp.concatenate([own[:, :latents] + other[:, latents:], own[:, latents:] + other[:, :latents]], 1)


def activate_kernel(own, other, bias, preact, activity, flat):
    latents = bias.shape[1] // 2
    value = join(own[...], other[...], latents) + bias[...]
    preact[...] = value
    positive = jnp.maximum(value, 0.0)
    activity[...] = positive.astype(BF16)
    flat[...] = positive.T.astype(BF16)


def recon_kernel(place, activity, weight, block, *, slot):
    _, thick, part = block.shape

    def step(j, carry):
        row = pl.multiple_of(place[0, slot * SIDE + j] * thick, thick)
        column = pl.multiple_of(place[1, slot * SIDE + j] * part, part)
        block[j] = jnp.dot(
            activity[pl.ds(row, thick), :], weight[:, pl.ds(column, part)], preferred_element_type=F32
        ).astype(BF16)
        return carry

    lax.fori_loop(0, SIDE, step, 0)


def gradient_kernel(own, other, preact, flat, error, centered, mine, theirs, slope, *, chunk):
    latents = mine.shape[0]
    value = jnp.where(preact[...] > 0, join(own[...], other[...], latents), 0.0)
    slope[...] = value.T.astype(BF16)

    def step(j, carry):
        columns = pl.ds(pl.multiple_of(j * chunk, chunk), chunk)
        total = jnp.dot(flat[...], error[:, columns], preferred_element_type=F32)
        total += jnp.dot(slope[...], centered[:, columns], preferred_element_type=F32)
        mine[:, columns] = total[:latents]
        theirs[:, columns] = total[latents:].astype(BF16)
        return carry

    lax.fori_loop(0, mine.shape[1] // chunk, step, 0)


def adam_kernel(at, gradient_ref, first_ref, second_ref, *refs, rows):
    update_out, first_out, second_out = refs[-3:]
    gradient = gradient_ref[...].astype(F32) * (1.0 / rows)
    first = 0.9 * first_ref[...].astype(F32) + 0.1 * gradient
    second = 0.999 * second_ref[...].astype(F32) + 0.001 * gradient * gradient
    update = first * (1.0 / (1.0 - 0.9**STEP)) / (jnp.sqrt(second * (1.0 / (1.0 - 0.999**STEP))) + 1e-08)
    update_out[...] = update.astype(BF16)
    first_out[...] = first.astype(BF16)
    second_out[...] = second.astype(BF16)


def adam(at, gradient, first_moment, second_moment, outs, rows, chunk=512):
    latents, width = gradient.shape
    count = width // chunk
    here = pl.BlockSpec((latents, chunk), lambda i, at: (0, i))
    there = pl.BlockSpec((latents, chunk), lambda i, at: (0, at[0] * count + i))
    held = [pl.BlockSpec(memory_space=pl.ANY)] * len(outs)
    return pl.pallas_call(
        functools.partial(adam_kernel, rows=rows),
        out_shape=(jax.ShapeDtypeStruct(first_moment.shape, BF16),) * 3,
        grid_spec=pltpu.PrefetchScalarGridSpec(
            num_scalar_prefetch=1,
            grid=(count,),
            in_specs=[here, there, there] + held,
            out_specs=(there,) * 3,
        ),
        input_output_aliases={4 + i: i for i in range(len(outs))},
        compiler_params=pltpu.CompilerParams(vmem_limit_bytes=32 * 1024 * 1024),
        cost_estimate=pl.CostEstimate(flops=20 * gradient.size, bytes_accessed=14 * gradient.size, transcendentals=0),
    )(at, gradient, first_moment, second_moment, *outs)


def body(inputs, dec_bias, weight, enc_bias, first_moment, second_moment):
    latents, width = weight.shape
    half = width // 2
    part = half // SIDE
    x, y, c = lax.axis_index("x"), lax.axis_index("y"), lax.axis_index("c")
    zh, z = lax.axis_index("zh"), lax.axis_index(Z)
    last_me, first_me = jnp.where(c == 0, x, y), jnp.where(c == 0, y, x)
    order = jnp.array(ORDER, jnp.int32)
    behind_last = jnp.repeat((last_me - order) % SIDE, SIDE)
    behind_first = jnp.tile((first_me - order) % SIDE, SIDE)
    ahead_last = jnp.repeat((last_me + order) % SIDE, SIDE)

    def places(last):
        return jnp.stack([jnp.where(c == 0, behind_first, last), jnp.where(c == 0, last, behind_first)])

    gather_place, send_place = places(behind_last), places(ahead_last)

    kept = lax.dynamic_slice_in_dim(inputs, c * half + x * part, part, 1)
    given = swap(lax.dynamic_slice_in_dim(inputs, (1 - c) * half + x * part, part, 1))
    both = jnp.concatenate([jnp.where(c == 0, kept, given), jnp.where(c == 0, given, kept)], 0)
    count = both.shape[0]
    block = jnp.zeros((SIDE * count, part), BF16)
    block = lax.dynamic_update_slice_in_dim(block, both, zh * count, 0)
    for by in ORDER[1:]:
        arrived = lax.ppermute(both, "zh", [(i, (i + by) % SIDE) for i in range(SIDE)])
        block = lax.dynamic_update_slice_in_dim(block, arrived, (zh - by) % SIDE * count, 0)
    source = block
    thick = source.shape[0]
    rows = thick * SIDE
    pieces = spread(jnp.stack(spread(source, False)), True)

    taken = swap(lax.dynamic_slice_in_dim(weight, (1 - c) * half, half, 1))
    pair = jnp.concatenate([lax.dynamic_slice_in_dim(weight, c * half, half, 1), taken], 0)
    decoder = lax.dynamic_slice_in_dim(dec_bias, c * half, half, 0)[None, :]
    bias = jnp.concatenate([enc_bias, swap(enc_bias)])[None, :]

    centered, own = project(gather_place, pair, decoder, pieces, True)
    preact, activity, flat = call(
        activate_kernel,
        (
            jax.ShapeDtypeStruct(own.shape, F32),
            jax.ShapeDtypeStruct(own.shape, BF16),
            jax.ShapeDtypeStruct(own.shape[::-1], BF16),
        ),
        (own, swap(own), bias),
        own.size * 4,
    )

    def recon_block(slot):
        return call(
            functools.partial(recon_kernel, slot=slot),
            jax.ShapeDtypeStruct((SIDE, thick, part), BF16),
            (send_place, activity, pair),
            2 * rows * part * 2 * latents,
            [SMEM, VMEM, VMEM],
        )

    total = 0.0
    for slot in (1, 2, 3):
        total = total + shift(recon_block(slot), ORDER[slot], True).astype(F32)
    total = (total + recon_block(0).astype(F32)).astype(BF16)
    strip = total[0].astype(F32)
    for by in ORDER[1:]:
        strip = strip + shift(total[ORDER.index(SIDE - by)], by, False).astype(F32)
    thin = thick // 8
    parts = lax.all_to_all(strip.astype(BF16).reshape(8, thin, part), Z, 0, 0, tiled=True)
    recon = jnp.sum(parts.astype(F32), 0)
    here = lax.dynamic_slice_in_dim(source, z * thin, thin, 0).astype(F32)
    error = (recon + lax.dynamic_slice_in_dim(decoder, x * part, part, 1) - here).astype(BF16)
    error = lax.all_to_all(jnp.broadcast_to(error, (8, thin, part)), Z, 0, 0, tiled=True)
    pieces = spread(jnp.stack(spread(error.reshape(thick, part), False)), True)

    error, own = project(gather_place, pair, decoder, pieces, False)
    mine, theirs, _ = call(
        functools.partial(gradient_kernel, chunk=512),
        (
            jax.ShapeDtypeStruct((latents, half), F32),
            jax.ShapeDtypeStruct((latents, half), BF16),
            jax.ShapeDtypeStruct(flat.shape, BF16),
        ),
        (own, swap(own), preact, flat, error, centered),
        8 * rows * half * latents,
    )
    arrived = swap(theirs)
    at = c.astype(jnp.int32)[None]
    outs = adam(at, mine, first_moment, second_moment, (), rows)
    return tuple(adam(1 - at, arrived, first_moment, second_moment, outs, rows))


def solution(mesh):
    fine = Mesh(mesh.devices.reshape(4, 2, 4, 4, 2), ("x", "zl", "y", "zh", "c"))
    lat = ("y", "zh", "c")
    everything = ("x", "zl", "y", "zh", "c")
    return jax.shard_map(
        body,
        mesh=fine,
        in_specs=(P(lat, None), P(), P(everything, None), P(everything), P(everything, None), P(everything, None)),
        out_specs=(P(everything, None),) * 3,
        check_vma=False,
    )
```

time: 467 us -> 230 us (0.49)
  the two profiles are of different devices: /device:TPU:1 before, /device:TPU:9 now
where the time goes in v1:
time: 230 us
  waiting for transfers between devices  97 us (42%)
  starting transfers between devices  63.4 us (28%)
  Pallas kernels  41 us (18%)
  blocking collectives  11.9 us (5%)
  local copies, waits for them, and re-layouts  8.79 us (4%)
  other arithmetic  6.85 us (3%)
    ppermute x18, waiting for transfers between devices, shift(): return lax.ppermute(value, PLANE, plane_pairs(by, last))  80 us
    pallas_call x8, Pallas kernels, call(): pl.pallas_call(kernel, out_shape=out_shape, in_specs=specs or [VMEM] * le...  32.3 us
    ppermute x18, starting transfers between devices, shift(): return lax.ppermute(value, PLANE, plane_pairs(by, last))  24.2 us
    ppermute x6, starting transfers between devices, swap(): return lax.ppermute(value, 'c', [(0, 1), (1, 0)])  23.6 us
    all_to_all x1, blocking collectives, body(): lax.all_to_all(jnp.broadcast_to(error, (8, thin, part)), Z, 0, 0, tiled=T...  11.9 us
    ppermute x3, starting transfers between devices, body(): lax.ppermute(both, 'zh', [(i, (i + by) % SIDE) for i in range(SIDE)])  10.6 us
    all_to_all x1, waiting for transfers between devices, body(): lax.all_to_all(strip.astype(BF16).reshape(8, thin, part), Z, 0, 0, tiled=...  9.32 us
    pallas_call x2, Pallas kernels, adam(): pl.pallas_call(functools.partial(adam_kernel, rows=rows), out_shape=(jax....  8.72 us
  transfers between devices with their start and end apart: 28, of which 21 were waited for; matrix products, arithmetic and copies ran while one was open for 3% of the time, Pallas kernels for 3%

profile of v1, /device:TPU:9, one launch (start us, length us, event | category | flops | bytes accessed | tf_op | source)
XLA Modules:
  0.0 229.8 jit_solution(15646423580997883334)
XLA Ops:
  3.8 7.0 %collective-permute-start.2 = (bf16[32,1024]{1,0:T(8,128)(2,1)S(1)}, bf16[32,1024]{1,0:T(8,128)(2,1)S(1)}, u32[]{:S(2)}, u32[]{:S(2)}) collective-permute-start(bf16[32,1024]{1,0:T(8,128)(2,1)S(1)} %get-tuple-element.34), channel_id=1, source_target_pairs={{0,4},{2,6},{4,0},{6,2},{1,5},{3,7},{5,1},{7,3},{8,12},{10,14},{12... | collective-permute-start | bytes 196616 | tf_op jit(solution)/shard_map/ppermute | solution.py:194
  10.8 3.1 %constant_dynamic-slice_fusion.2 = (bf16[128,4096]{1,0:T(8,128)(2,1)}, bf16[128,4096]{1,0:T(8,128)(2,1)}) fusion(bf16[128,8192]{1,0:T(8,128)(2,1)} %param.9, s32[]{:T(128)S(6)} %select_n.151, s32[]{:T(128)S(6)} %select_n.152), kind=kLoop, calls=%fused_computation.23 | loop fusion | bytes 4194312 | tf_op jit(solution)/shard_map/dynamic_slice | solution.py:202
  14.6 1.2 collective-permute-start.3
  15.8 2.4 %collective-permute-start.4 = (bf16[32,1024]{1,0:T(8,128)(2,1)S(1)}, bf16[32,1024]{1,0:T(8,128)(2,1)S(1)}, u32[]{:S(2)}, u32[]{:S(2)}) collective-permute-start(bf16[32,1024]{1,0:T(8,128)(2,1)S(1)} %get-tuple-element.34), channel_id=1, source_target_pairs={{0,6},{2,0},{4,2},{6,4},{1,7},{3,1},{5,3},{7,5},{8,14},{10,8},{12,... | collective-permute-start | bytes 196616 | tf_op jit(solution)/shard_map/ppermute | solution.py:194
  18.2 3.8 %collective-permute-done.3 = bf16[32,1024]{1,0:T(8,128)(2,1)S(1)} collective-permute-done((bf16[32,1024]{1,0:T(8,128)(2,1)S(1)}, bf16[32,1024]{1,0:T(8,128)(2,1)S(1)}, u32[]{:S(2)}, u32[]{:S(2)}) %collective-permute-start.3) | collective-permute-done | bytes 65568 | tf_op jit(solution)/shard_map/ppermute | solution.py:194
  22.0 2.8 %collective-permute-start.5 = (bf16[128,1024]{1,0:T(8,128)(2,1)S(1)}, bf16[128,1024]{1,0:T(8,128)(2,1)S(1)}, u32[]{:S(2)}, u32[]{:S(2)}) collective-permute-start(bf16[128,1024]{1,0:T(8,128)(2,1)S(1)} %constant_dynamic-update-slice_fusion), channel_id=1, source_target_pairs={{0,16},{1,129},{8,24},{9,137},{16,0},{17,145},{24,8},{25,153},{64,... | collective-permute-start | bytes 786440 | tf_op jit(solution)/shard_map/ppermute | solution.py:35
  25.1 2.4 %collective-permute-start.7 = (bf16[128,1024]{1,0:T(8,128)(2,1)S(1)}, bf16[128,1024]{1,0:T(8,128)(2,1)S(1)}, u32[]{:S(2)}, u32[]{:S(2)}) collective-permute-start(bf16[128,1024]{1,0:T(8,128)(2,1)S(1)} %constant_dynamic-update-slice_fusion), channel_id=1, source_target_pairs={{0,24},{1,193},{8,0},{9,201},{16,8},{17,209},{24,16},{25,217},{64,... | collective-permute-start | bytes 786440 | tf_op jit(solution)/shard_map/ppermute | solution.py:35
  27.5 1.3 collective-permute-done.5
  28.8 2.8 %collective-permute-done.6 = bf16[128,1024]{1,0:T(8,128)(2,1)S(1)} collective-permute-done((bf16[128,1024]{1,0:T(8,128)(2,1)S(1)}, bf16[128,1024]{1,0:T(8,128)(2,1)S(1)}, u32[]{:S(2)}, u32[]{:S(2)}) %collective-permute-start.6) | collective-permute-done | bytes 262176 | tf_op jit(solution)/shard_map/ppermute | solution.py:35
  32.4 2.3 %collective-permute-start.8 = (bf16[4,128,1024]{2,1,0:T(8,128)(2,1)S(1)}, bf16[4,128,1024]{2,1,0:T(8,128)(2,1)S(1)}, u32[]{:S(2)}, u32[]{:S(2)}) collective-permute-start(bf16[4,128,1024]{2,1,0:T(8,128)(2,1)S(1)} %pad_maximum_fusion.1.refs_0_), channel_id=1, source_target_pairs={{0,128},{1,17},{8,136},{9,25},{16,144},{17,1},{24,152},{25,9},{64,... | collective-permute-start | bytes 3145736 | tf_op jit(solution)/shard_map/ppermute | solution.py:35
  34.7 1.6 collective-permute-start.9
  36.6 3.1 %pad_maximum_fusion.weight = bf16[256,4096]{1,0:T(8,128)(2,1)} fusion(bf16[128,4096]{1,0:T(8,128)(2,1)} %collective-permute-done, bf16[128,4096]{1,0:T(8,128)(2,1)} %get-tuple-element.27), kind=kLoop, calls=%fused_computation | loop fusion | flops 4194304 | bytes 4194304 | tf_op jit(solution)/shard_map/concatenate | solution.py:202
  39.7 6.6 %collective-permute-done.10.refs_3_ = bf16[4,128,1024]{2,1,0:T(8,128)(2,1)S(1)} collective-permute-done((bf16[4,128,1024]{2,1,0:T(8,128)(2,1)S(1)}, bf16[4,128,1024]{2,1,0:T(8,128)(2,1)S(1)}, u32[]{:S(2)}, u32[]{:S(2)}) %collective-permute-start.10) | collective-permute-done | bytes 1048608 | tf_op jit(solution)/shard_map/ppermute | solution.py:35
  47.2 11.3 %collective-permute-done.8.refs_1_ = bf16[4,128,1024]{2,1,0:T(8,128)(2,1)S(1)} collective-permute-done((bf16[4,128,1024]{2,1,0:T(8,128)(2,1)S(1)}, bf16[4,128,1024]{2,1,0:T(8,128)(2,1)S(1)}, u32[]{:S(2)}, u32[]{:S(2)}) %collective-permute-start.8) | collective-permute-done | bytes 1048608 | tf_op jit(solution)/shard_map/ppermute | solution.py:35
  59.5 1.2 copy-done.4
  60.7 1.2 copy-done.6
  61.9 9.1 %shard_map.94 = (bf16[512,4096]{1,0:T(8,128)(2,1)}, f32[512,256]{1,0:T(8,128)}) custom-call(s32[2,16]{1,0:T(2,128)S(1)} %pad_add_fusion.place, bf16[256,4096]{1,0:T(8,128)(2,1)} %pad_maximum_fusion.weight, f32[1,4096]{1,0:T(1,128)S(1)} %bitcast.24, bf16[4,128,1024]{2,1,0:T(8,128)(2,1)S(1)} %pad_maximum_fusion.1.refs_0_, bf16[4,128,1024]{2,1,0:T(8,128)(2,1)S(1)} %copy-done.6, ...), custom_call_target="tpu_custom_call" | custom-call | flops 1073741824 | bytes 11026560 | tf_op jit(solution)/shard_map/pallas_call | solution.py:49
  71.0 4.5 %collective-permute-start.11 = (f32[512,256]{1,0:T(8,128)}, f32[512,256]{1,0:T(8,128)S(1)}, u32[]{:S(2)}, u32[]{:S(2)}) collective-permute-start(f32[512,256]{1,0:T(8,128)} %get-tuple-element.15.own), channel_id=1, source_target_pairs={{0,1},{1,0},{2,3},{3,2},{4,5},{5,4},{6,7},{7,6},{8,9},{9,8},{10,11... | collective-permute-start | bytes 1572872 | tf_op jit(solution)/shard_map/ppermute | solution.py:39
  75.8 1.3 collective-permute-done.12
  77.3 1.2 shard_map.95
  78.5 1.5 shard_map.96
  80.0 1.5 shard_map.97
  81.5 1.5 shard_map.98
  83.0 2.3 collective-permute-start.13
  85.3 1.5 collective-permute-start.15
  86.8 1.5 shard_map.99
  88.3 10.3 %collective-permute-done.13 = bf16[4,128,1024]{2,1,0:T(8,128)(2,1)S(1)} collective-permute-done((bf16[4,128,1024]{2,1,0:T(8,128)(2,1)S(1)}, bf16[4,128,1024]{2,1,0:T(8,128)(2,1)S(1)}, u32[]{:S(2)}, u32[]{:S(2)}) %collective-permute-start.13) | collective-permute-done | bytes 1048608 | tf_op jit(solution)/shard_map/ppermute | solution.py:35
  98.6 10.4 %collective-permute-done.14 = bf16[4,128,1024]{2,1,0:T(8,128)(2,1)S(1)} collective-permute-done((bf16[4,128,1024]{2,1,0:T(8,128)(2,1)S(1)}, bf16[4,128,1024]{2,1,0:T(8,128)(2,1)S(1)}, u32[]{:S(2)}, u32[]{:S(2)}) %collective-permute-start.14) | collective-permute-done | bytes 1048608 | tf_op jit(solution)/shard_map/ppermute | solution.py:35
  111.4 1.3 collective-permute-start.17
  112.7 1.3 collective-permute-start.18
  114.1 3.6 %collective-permute-done.16 = bf16[128,1024]{1,0:T(8,128)(2,1)S(1)} collective-permute-done((bf16[128,1024]{1,0:T(8,128)(2,1)S(1)}, bf16[128,1024]{1,0:T(8,128)(2,1)S(1)}, u32[]{:S(2)}, u32[]{:S(2)}) %collective-permute-start.16) | collective-permute-done | bytes 262176 | tf_op jit(solution)/shard_map/ppermute | solution.py:35
  117.7 2.7 %collective-permute-done.17 = bf16[128,1024]{1,0:T(8,128)(2,1)S(1)} collective-permute-done((bf16[128,1024]{1,0:T(8,128)(2,1)S(1)}, bf16[128,1024]{1,0:T(8,128)(2,1)S(1)}, u32[]{:S(2)}, u32[]{:S(2)}) %collective-permute-start.17) | collective-permute-done | bytes 262176 | tf_op jit(solution)/shard_map/ppermute | solution.py:35
  121.3 5.0 %all-to-all-start = ((bf16[8,16,1024]{2,1,0:T(8,128)(2,1)}), bf16[8,16,1024]{2,1,0:T(8,128)(2,1)S(1)}, u32[]{:S(2)}, u32[]{:S(2)}) async-start(bf16[8,16,1024]{2,1,0:T(8,128)(2,1)} %bitcast.11), calls=%async_computation | async-start | bytes 524288 | tf_op jit(solution)/shard_map/all_to_all | solution.py:235
  126.4 9.3 %all-to-all-done = bf16[8,16,1024]{2,1,0:T(8,128)(2,1)S(1)} async-done(((bf16[8,16,1024]{2,1,0:T(8,128)(2,1)}), bf16[8,16,1024]{2,1,0:T(8,128)(2,1)S(1)}, u32[]{:S(2)}, u32[]{:S(2)}) %all-to-all-start) | async-done | bytes 262176 | tf_op jit(solution)/shard_map/all_to_all | solution.py:235
  136.6 11.9 %all_to_all.10 = bf16[8,16,1024]{2,1,0:T(8,128)(2,1)S(1)} all-to-all(bf16[8,16,1024]{2,1,0:T(8,128)(2,1)S(1)} %broadcast_in_dim.27), channel_id=1, replica_groups=mesh['x'=4,'zl'=2,'y'=4,'zh'=4,'c'=2] {'zh','zl'}, dimensions={0} | all-to-all | bytes 524288 | tf_op jit(solution)/shard_map/all_to_all | solution.py:239
  150.3 1.6 collective-permute-start.21
  151.9 3.4 %collective-permute-done.19 = bf16[128,1024]{1,0:T(8,128)(2,1)S(1)} collective-permute-done((bf16[128,1024]{1,0:T(8,128)(2,1)S(1)}, bf16[128,1024]{1,0:T(8,128)(2,1)S(1)}, u32[]{:S(2)}, u32[]{:S(2)}) %collective-permute-start.19) | collective-permute-done | bytes 262176 | tf_op jit(solution)/shard_map/ppermute | solution.py:35
  155.3 2.8 %collective-permute-done.20 = bf16[128,1024]{1,0:T(8,128)(2,1)S(1)} collective-permute-done((bf16[128,1024]{1,0:T(8,128)(2,1)S(1)}, bf16[128,1024]{1,0:T(8,128)(2,1)S(1)}, u32[]{:S(2)}, u32[]{:S(2)}) %collective-permute-start.20) | collective-permute-done | bytes 262176 | tf_op jit(solution)/shard_map/ppermute | solution.py:35
  158.3 2.6 %collective-permute-start.22 = (bf16[4,128,1024]{2,1,0:T(8,128)(2,1)S(1)}, bf16[4,128,1024]{2,1,0:T(8,128)(2,1)S(1)}, u32[]{:S(2)}, u32[]{:S(2)}) collective-permute-start(bf16[4,128,1024]{2,1,0:T(8,128)(2,1)S(1)} %pad_maximum_fusion.2.refs_0_), channel_id=1, source_target_pairs={{0,128},{1,17},{8,136},{9,25},{16,144},{17,1},{24,152},{25,9},{64,... | collective-permute-start | bytes 3145736 | tf_op jit(solution)/shard_map/ppermute | solution.py:35
  160.9 1.5 collective-permute-start.24
  162.4 12.2 %collective-permute-done.22.refs_1_ = bf16[4,128,1024]{2,1,0:T(8,128)(2,1)S(1)} collective-permute-done((bf16[4,128,1024]{2,1,0:T(8,128)(2,1)S(1)}, bf16[4,128,1024]{2,1,0:T(8,128)(2,1)S(1)}, u32[]{:S(2)}, u32[]{:S(2)}) %collective-permute-start.22) | collective-permute-done | bytes 1048608 | tf_op jit(solution)/shard_map/ppermute | solution.py:35
  174.6 10.6 %collective-permute-done.23.refs_2_ = bf16[4,128,1024]{2,1,0:T(8,128)(2,1)S(1)} collective-permute-done((bf16[4,128,1024]{2,1,0:T(8,128)(2,1)S(1)}, bf16[4,128,1024]{2,1,0:T(8,128)(2,1)S(1)}, u32[]{:S(2)}, u32[]{:S(2)}) %collective-permute-start.23) | collective-permute-done | bytes 1048608 | tf_op jit(solution)/shard_map/ppermute | solution.py:35
  185.9 8.4 %shard_map.100 = (bf16[512,4096]{1,0:T(8,128)(2,1)}, f32[512,256]{1,0:T(8,128)S(1)}) custom-call(s32[2,16]{1,0:T(2,128)S(1)} %pad_add_fusion.place, bf16[256,4096]{1,0:T(8,128)(2,1)} %pad_maximum_fusion.weight, f32[1,4096]{1,0:T(1,128)S(1)} %bitcast.25, bf16[4,128,1024]{2,1,0:T(8,128)(2,1)S(1)} %pad_maximum_fusion.2.refs_0_, ...), custom_call_target="tpu_custom_call" | custom-call | flops 1073741824 | bytes 11026560 | tf_op jit(solution)/shard_map/pallas_call | solution.py:49
  194.4 17.2 %collective-permute-start.25 = (f32[512,256]{1,0:T(8,128)S(1)}, f32[512,256]{1,0:T(8,128)S(1)}, u32[]{:S(2)}, u32[]{:S(2)}) collective-permute-start(f32[512,256]{1,0:T(8,128)S(1)} %get-tuple-element.17.own), channel_id=1, source_target_pairs={{0,1},{1,0},{2,3},{3,2},{4,5},{5,4},{6,7},{7,6},{8,9},{9,8},{10,11... | collective-permute-start | bytes 1572872 | tf_op jit(solution)/shard_map/ppermute | solution.py:39
  211.6 1.5 collective-permute-done.25.other
  213.1 7.6 %shard_map.101 = (f32[128,4096]{1,0:T(8,128)S(1)}, bf16[128,4096]{1,0:T(8,128)(2,1)S(1)}, bf16[256,512]{1,0:T(8,128)(2,1)}) custom-call(f32[512,256]{1,0:T(8,128)S(1)} %get-tuple-element.17.own, f32[512,256]{1,0:T(8,128)S(1)} %collective-permute-done.25.other, f32[512,256]{1,0:T(8,128)S(1)} %get-tuple-element.18.preact, ...), custom_call_target="tpu_custom_call" | custom-call | flops 2147483648 | bytes 13631488 | tf_op jit(solution)/shard_map/pallas_call | solution.py:49
  221.1 4.3 %shard_map.102 = (bf16[128,8192]{1,0:T(8,128)(2,1)}, bf16[128,8192]{1,0:T(8,128)(2,1)}, bf16[128,8192]{1,0:T(8,128)(2,1)}) custom-call(s32[1]{0:T(128)} %bitcast.at, f32[128,4096]{1,0:T(8,128)S(1)} %get-tuple-element.23.gradient_ref, bf16[128,8192]{1,0:T(8,128)(2,1)S(1)} %copy-done.1, bf16[128,8192]{1,0:T(8,128)(2,1)S(1)} %copy-done.2), custom_call_target="tpu_custom_call" | custom-call | flops 10485760 | bytes 7340032 | tf_op jit(solution)/shard_map/pallas_call | solution.py:155
  225.4 4.4 %shard_map.103 = (bf16[128,8192]{1,0:T(8,128)(2,1)}, bf16[128,8192]{1,0:T(8,128)(2,1)}, bf16[128,8192]{1,0:T(8,128)(2,1)}) custom-call(s32[1]{0:T(128)S(6)} %sub.31.at, bf16[128,4096]{1,0:T(8,128)(2,1)S(1)} %collective-permute-done.26.gradient_ref, bf16[128,8192]{1,0:T(8,128)(2,1)S(1)} %copy-done.1, ...), custom_call_target="tpu_custom_call", output_to_operand_aliasing={{0}: (4, {}), {1}: (5, {}), {2}: (6, {})} | custom-call | flops 10485760 | bytes 7340032 | tf_op jit(solution)/shard_map/pallas_call | solution.py:155
  (71 shorter events, 14.9 us)
Async XLA Ops:
  1.4 1.5 collective-permute-start.1
  3.8 14.4 %collective-permute-start.2 = (bf16[32,1024]{1,0:T(8,128)(2,1)S(1)}, bf16[32,1024]{1,0:T(8,128)(2,1)S(1)}, u32[]{:S(2)}, u32[]{:S(2)}) collective-permute-start(bf16[32,1024]{1,0:T(8,128)(2,1)S(1)} %get-tuple-element.34), channel_id=1, source_target_pairs={{0,4},{2,6},{4,0},{6,2},{1,5},{3,7},{5,1},{7,3},{8,12},{10,14},{12... | collective-permute-start | bytes 196616 | tf_op jit(solution)/shard_map/ppermute | solution.py:194
  13.8 22.4 %copy-start.9 = (s32[4]{0:T(128)S(1)}, s32[4]{0:T(128)}, u32[]{:S(2)}) copy-start(s32[4]{0:T(128)} %constant.101) | copy-start | bytes 52
  13.8 22.4 %copy-start.10 = (s32[4]{0:T(128)S(1)}, s32[4]{0:T(128)}, u32[]{:S(2)}) copy-start(s32[4]{0:T(128)} %constant.95.clone) | copy-start | bytes 52
  13.8 22.7 %copy-start.8 = (f32[8192]{0:T(1024)S(1)}, f32[8192]{0:T(1024)}, u32[]{:S(2)}) copy-start(f32[8192]{0:T(1024)} %param.8) | copy-start | bytes 98308
  13.8 22.7 %collective-permute-start = (bf16[128,4096]{1,0:T(8,128)(2,1)}, bf16[128,4096]{1,0:T(8,128)(2,1)}, u32[]{:S(2)}, u32[]{:S(2)}) collective-permute-start(bf16[128,4096]{1,0:T(8,128)(2,1)} %get-tuple-element.28), channel_id=1, source_target_pairs={{0,1},{1,0},{2,3},{3,2},{4,5},{5,4},{6,7},{7,6},{8,9},{9,8},{10,11... | collective-permute-start | bytes 3145736 | tf_op jit(solution)/shard_map/ppermute | solution.py:39
  14.6 7.4 %collective-permute-start.3 = (bf16[32,1024]{1,0:T(8,128)(2,1)S(1)}, bf16[32,1024]{1,0:T(8,128)(2,1)S(1)}, u32[]{:S(2)}, u32[]{:S(2)}) collective-permute-start(bf16[32,1024]{1,0:T(8,128)(2,1)S(1)} %get-tuple-element.34), channel_id=1, source_target_pairs={{0,2},{2,4},{4,6},{6,0},{1,3},{3,5},{5,7},{7,1},{8,10},{10,12},{12... | collective-permute-start | bytes 196616 | tf_op jit(solution)/shard_map/ppermute | solution.py:194
  15.8 6.2 %collective-permute-start.4 = (bf16[32,1024]{1,0:T(8,128)(2,1)S(1)}, bf16[32,1024]{1,0:T(8,128)(2,1)S(1)}, u32[]{:S(2)}, u32[]{:S(2)}) collective-permute-start(bf16[32,1024]{1,0:T(8,128)(2,1)S(1)} %get-tuple-element.34), channel_id=1, source_target_pairs={{0,6},{2,0},{4,2},{6,4},{1,7},{3,1},{5,3},{7,5},{8,14},{10,8},{12,... | collective-permute-start | bytes 196616 | tf_op jit(solution)/shard_map/ppermute | solution.py:194
  22.0 10.0 %copy-start.7 = (bf16[128,1024]{1,0:T(8,128)(2,1)}, bf16[128,1024]{1,0:T(8,128)(2,1)S(1)}, u32[]{:S(2)}) copy-start(bf16[128,1024]{1,0:T(8,128)(2,1)S(1)} %constant_dynamic-update-slice_fusion) | copy-start | bytes 786436
  22.0 6.9 %collective-permute-start.5 = (bf16[128,1024]{1,0:T(8,128)(2,1)S(1)}, bf16[128,1024]{1,0:T(8,128)(2,1)S(1)}, u32[]{:S(2)}, u32[]{:S(2)}) collective-permute-start(bf16[128,1024]{1,0:T(8,128)(2,1)S(1)} %constant_dynamic-update-slice_fusion), channel_id=1, source_target_pairs={{0,16},{1,129},{8,24},{9,137},{16,0},{17,145},{24,8},{25,153},{64,... | collective-permute-start | bytes 786440 | tf_op jit(solution)/shard_map/ppermute | solution.py:35
  24.8 6.8 %collective-permute-start.6 = (bf16[128,1024]{1,0:T(8,128)(2,1)S(1)}, bf16[128,1024]{1,0:T(8,128)(2,1)S(1)}, u32[]{:S(2)}, u32[]{:S(2)}) collective-permute-start(bf16[128,1024]{1,0:T(8,128)(2,1)S(1)} %constant_dynamic-update-slice_fusion), channel_id=1, source_target_pairs={{0,8},{1,65},{8,16},{9,73},{16,24},{17,81},{24,0},{25,89},{64,72},... | collective-permute-start | bytes 786440 | tf_op jit(solution)/shard_map/ppermute | solution.py:35
  25.1 6.9 %collective-permute-start.7 = (bf16[128,1024]{1,0:T(8,128)(2,1)S(1)}, bf16[128,1024]{1,0:T(8,128)(2,1)S(1)}, u32[]{:S(2)}, u32[]{:S(2)}) collective-permute-start(bf16[128,1024]{1,0:T(8,128)(2,1)S(1)} %constant_dynamic-update-slice_fusion), channel_id=1, source_target_pairs={{0,24},{1,193},{8,0},{9,201},{16,8},{17,209},{24,16},{25,217},{64,... | collective-permute-start | bytes 786440 | tf_op jit(solution)/shard_map/ppermute | solution.py:35
  32.1 14.1 %collective-permute-start.10 = (bf16[4,128,1024]{2,1,0:T(8,128)(2,1)S(1)}, bf16[4,128,1024]{2,1,0:T(8,128)(2,1)S(1)}, u32[]{:S(2)}, u32[]{:S(2)}) collective-permute-start(bf16[4,128,1024]{2,1,0:T(8,128)(2,1)S(1)} %pad_maximum_fusion.1.refs_0_), channel_id=1, source_target_pairs={{0,192},{1,25},{8,200},{9,1},{16,208},{17,9},{24,216},{25,17},{64,... | collective-permute-start | bytes 3145736 | tf_op jit(solution)/shard_map/ppermute | solution.py:35
  32.4 26.1 %collective-permute-start.8 = (bf16[4,128,1024]{2,1,0:T(8,128)(2,1)S(1)}, bf16[4,128,1024]{2,1,0:T(8,128)(2,1)S(1)}, u32[]{:S(2)}, u32[]{:S(2)}) collective-permute-start(bf16[4,128,1024]{2,1,0:T(8,128)(2,1)S(1)} %pad_maximum_fusion.1.refs_0_), channel_id=1, source_target_pairs={{0,128},{1,17},{8,136},{9,25},{16,144},{17,1},{24,152},{25,9},{64,... | collective-permute-start | bytes 3145736 | tf_op jit(solution)/shard_map/ppermute | solution.py:35
  34.7 24.8 %collective-permute-start.9 = (bf16[4,128,1024]{2,1,0:T(8,128)(2,1)S(1)}, bf16[4,128,1024]{2,1,0:T(8,128)(2,1)}, u32[]{:S(2)}, u32[]{:S(2)}) collective-permute-start(bf16[4,128,1024]{2,1,0:T(8,128)(2,1)S(1)} %pad_maximum_fusion.1.refs_0_), channel_id=1, source_target_pairs={{0,64},{1,9},{8,72},{9,17},{16,80},{17,25},{24,88},{25,1},{64,128}... | collective-permute-start | bytes 3145736 | tf_op jit(solution)/shard_map/ppermute | solution.py:35
  46.2 1.0 copy-start.3
  58.5 1.0 copy-start.5
  59.5 1.2 copy-start.4
  60.7 1.2 copy-start.6
  61.9 13.6 %copy-start.11 = (f32[128]{0:T(128)S(1)}, f32[128]{0:T(128)}, u32[]{:S(2)}) copy-start(f32[128]{0:T(128)} %param.10) | copy-start | bytes 1540
  61.9 16.6 %copy-start = (bf16[256,4096]{1,0:T(8,128)(2,1)S(1)}, bf16[256,4096]{1,0:T(8,128)(2,1)}, u32[]{:S(2)}) copy-start(bf16[256,4096]{1,0:T(8,128)(2,1)} %pad_maximum_fusion.weight) | copy-start | bytes 6291460
  71.0 6.3 %collective-permute-start.11 = (f32[512,256]{1,0:T(8,128)}, f32[512,256]{1,0:T(8,128)S(1)}, u32[]{:S(2)}, u32[]{:S(2)}) collective-permute-start(f32[512,256]{1,0:T(8,128)} %get-tuple-element.15.own), channel_id=1, source_target_pairs={{0,1},{1,0},{2,3},{3,2},{4,5},{5,4},{6,7},{7,6},{8,9},{9,8},{10,11... | collective-permute-start | bytes 1572872 | tf_op jit(solution)/shard_map/ppermute | solution.py:39
  75.6 1.5 collective-permute-start.12
  83.0 15.6 %collective-permute-start.13 = (bf16[4,128,1024]{2,1,0:T(8,128)(2,1)S(1)}, bf16[4,128,1024]{2,1,0:T(8,128)(2,1)S(1)}, u32[]{:S(2)}, u32[]{:S(2)}) collective-permute-start(bf16[4,128,1024]{2,1,0:T(8,128)(2,1)S(1)} %shard_map.96), channel_id=1, source_target_pairs={{0,128},{1,17},{8,136},{9,25},{16,144},{17,1},{24,152},{25,9},{64,... | collective-permute-start | bytes 3145736 | tf_op jit(solution)/shard_map/ppermute | solution.py:35
  85.3 23.7 %collective-permute-start.14 = (bf16[4,128,1024]{2,1,0:T(8,128)(2,1)S(1)}, bf16[4,128,1024]{2,1,0:T(8,128)(2,1)S(1)}, u32[]{:S(2)}, u32[]{:S(2)}) collective-permute-start(bf16[4,128,1024]{2,1,0:T(8,128)(2,1)S(1)} %shard_map.97), channel_id=1, source_target_pairs={{0,64},{1,9},{8,72},{9,17},{16,80},{17,25},{24,88},{25,1},{64,128}... | collective-permute-start | bytes 3145736 | tf_op jit(solution)/shard_map/ppermute | solution.py:35
  85.3 24.5 %collective-permute-start.15 = (bf16[4,128,1024]{2,1,0:T(8,128)(2,1)S(1)}, bf16[4,128,1024]{2,1,0:T(8,128)(2,1)S(1)}, u32[]{:S(2)}, u32[]{:S(2)}) collective-permute-start(bf16[4,128,1024]{2,1,0:T(8,128)(2,1)S(1)} %shard_map.98), channel_id=1, source_target_pairs={{0,192},{1,25},{8,200},{9,1},{16,208},{17,9},{24,216},{25,17},{64,... | collective-permute-start | bytes 3145736 | tf_op jit(solution)/shard_map/ppermute | solution.py:35
  110.8 6.9 %collective-permute-start.16 = (bf16[128,1024]{1,0:T(8,128)(2,1)S(1)}, bf16[128,1024]{1,0:T(8,128)(2,1)S(1)}, u32[]{:S(2)}, u32[]{:S(2)}) collective-permute-start(bf16[128,1024]{1,0:T(8,128)(2,1)S(1)} %get-tuple-element.29), channel_id=1, source_target_pairs={{0,16},{1,129},{8,24},{9,137},{16,0},{17,145},{24,8},{25,153},{64,... | collective-permute-start | bytes 786440 | tf_op jit(solution)/shard_map/ppermute | solution.py:35
  111.4 9.0 %collective-permute-start.17 = (bf16[128,1024]{1,0:T(8,128)(2,1)S(1)}, bf16[128,1024]{1,0:T(8,128)(2,1)S(1)}, u32[]{:S(2)}, u32[]{:S(2)}) collective-permute-start(bf16[128,1024]{1,0:T(8,128)(2,1)S(1)} %get-tuple-element.31), channel_id=1, source_target_pairs={{0,8},{1,65},{8,16},{9,73},{16,24},{17,81},{24,0},{25,89},{64,72},... | collective-permute-start | bytes 786440 | tf_op jit(solution)/shard_map/ppermute | solution.py:35
  112.7 7.7 %collective-permute-start.18 = (bf16[128,1024]{1,0:T(8,128)(2,1)S(1)}, bf16[128,1024]{1,0:T(8,128)(2,1)S(1)}, u32[]{:S(2)}, u32[]{:S(2)}) collective-permute-start(bf16[128,1024]{1,0:T(8,128)(2,1)S(1)} %get-tuple-element.30), channel_id=1, source_target_pairs={{0,24},{1,193},{8,0},{9,201},{16,8},{17,209},{24,16},{25,217},{64,... | collective-permute-start | bytes 786440 | tf_op jit(solution)/shard_map/ppermute | solution.py:35
  121.3 14.4 %all-to-all-start = ((bf16[8,16,1024]{2,1,0:T(8,128)(2,1)}), bf16[8,16,1024]{2,1,0:T(8,128)(2,1)S(1)}, u32[]{:S(2)}, u32[]{:S(2)}) async-start(bf16[8,16,1024]{2,1,0:T(8,128)(2,1)} %bitcast.11), calls=%async_computation | async-start | bytes 524288 | tf_op jit(solution)/shard_map/all_to_all | solution.py:235
  148.4 6.8 %collective-permute-start.19 = (bf16[128,1024]{1,0:T(8,128)(2,1)S(1)}, bf16[128,1024]{1,0:T(8,128)(2,1)S(1)}, u32[]{:S(2)}, u32[]{:S(2)}) collective-permute-start(bf16[128,1024]{1,0:T(8,128)(2,1)S(1)} %bitcast.28), channel_id=1, source_target_pairs={{0,16},{1,129},{8,24},{9,137},{16,0},{17,145},{24,8},{25,153},{64,... | collective-permute-start | bytes 786440 | tf_op jit(solution)/shard_map/ppermute | solution.py:35
  149.3 8.9 %collective-permute-start.20 = (bf16[128,1024]{1,0:T(8,128)(2,1)S(1)}, bf16[128,1024]{1,0:T(8,128)(2,1)S(1)}, u32[]{:S(2)}, u32[]{:S(2)}) collective-permute-start(bf16[128,1024]{1,0:T(8,128)(2,1)S(1)} %bitcast.29), channel_id=1, source_target_pairs={{0,8},{1,65},{8,16},{9,73},{16,24},{17,81},{24,0},{25,89},{64,72},... | collective-permute-start | bytes 786440 | tf_op jit(solution)/shard_map/ppermute | solution.py:35
  150.3 7.8 %collective-permute-start.21 = (bf16[128,1024]{1,0:T(8,128)(2,1)S(1)}, bf16[128,1024]{1,0:T(8,128)(2,1)S(1)}, u32[]{:S(2)}, u32[]{:S(2)}) collective-permute-start(bf16[128,1024]{1,0:T(8,128)(2,1)S(1)} %bitcast.30), channel_id=1, source_target_pairs={{0,24},{1,193},{8,0},{9,201},{16,8},{17,209},{24,16},{25,217},{64,... | collective-permute-start | bytes 786440 | tf_op jit(solution)/shard_map/ppermute | solution.py:35
  158.3 16.3 %collective-permute-start.22 = (bf16[4,128,1024]{2,1,0:T(8,128)(2,1)S(1)}, bf16[4,128,1024]{2,1,0:T(8,128)(2,1)S(1)}, u32[]{:S(2)}, u32[]{:S(2)}) collective-permute-start(bf16[4,128,1024]{2,1,0:T(8,128)(2,1)S(1)} %pad_maximum_fusion.2.refs_0_), channel_id=1, source_target_pairs={{0,128},{1,17},{8,136},{9,25},{16,144},{17,1},{24,152},{25,9},{64,... | collective-permute-start | bytes 3145736 | tf_op jit(solution)/shard_map/ppermute | solution.py:35
  160.9 24.3 %collective-permute-start.23 = (bf16[4,128,1024]{2,1,0:T(8,128)(2,1)S(1)}, bf16[4,128,1024]{2,1,0:T(8,128)(2,1)S(1)}, u32[]{:S(2)}, u32[]{:S(2)}) collective-permute-start(bf16[4,128,1024]{2,1,0:T(8,128)(2,1)S(1)} %pad_maximum_fusion.2.refs_0_), channel_id=1, source_target_pairs={{0,64},{1,9},{8,72},{9,17},{16,80},{17,25},{24,88},{25,1},{64,128}... | collective-permute-start | bytes 3145736 | tf_op jit(solution)/shard_map/ppermute | solution.py:35
  160.9 25.1 %collective-permute-start.24 = (bf16[4,128,1024]{2,1,0:T(8,128)(2,1)S(1)}, bf16[4,128,1024]{2,1,0:T(8,128)(2,1)S(1)}, u32[]{:S(2)}, u32[]{:S(2)}) collective-permute-start(bf16[4,128,1024]{2,1,0:T(8,128)(2,1)S(1)} %pad_maximum_fusion.2.refs_0_), channel_id=1, source_target_pairs={{0,192},{1,25},{8,200},{9,1},{16,208},{17,9},{24,216},{25,17},{64,... | collective-permute-start | bytes 3145736 | tf_op jit(solution)/shard_map/ppermute | solution.py:35
  194.4 18.8 %collective-permute-start.25 = (f32[512,256]{1,0:T(8,128)S(1)}, f32[512,256]{1,0:T(8,128)S(1)}, u32[]{:S(2)}, u32[]{:S(2)}) collective-permute-start(f32[512,256]{1,0:T(8,128)S(1)} %get-tuple-element.17.own), channel_id=1, source_target_pairs={{0,1},{1,0},{2,3},{3,2},{4,5},{5,4},{6,7},{7,6},{8,9},{9,8},{10,11... | collective-permute-start | bytes 1572872 | tf_op jit(solution)/shard_map/ppermute | solution.py:39
  213.1 7.9 %copy-start.1 = (bf16[128,8192]{1,0:T(8,128)(2,1)S(1)}, bf16[128,8192]{1,0:T(8,128)(2,1)}, u32[]{:S(2)}) copy-start(bf16[128,8192]{1,0:T(8,128)(2,1)} %first_ref.3) | copy-start | bytes 6291460
  213.1 7.9 %copy-start.2 = (bf16[128,8192]{1,0:T(8,128)(2,1)S(1)}, bf16[128,8192]{1,0:T(8,128)(2,1)}, u32[]{:S(2)}) copy-start(bf16[128,8192]{1,0:T(8,128)(2,1)} %second_ref.3) | copy-start | bytes 6291460
  220.7 4.7 %collective-permute-start.26 = (bf16[128,4096]{1,0:T(8,128)(2,1)S(1)}, bf16[128,4096]{1,0:T(8,128)(2,1)S(1)}, u32[]{:S(2)}, u32[]{:S(2)}) collective-permute-start(bf16[128,4096]{1,0:T(8,128)(2,1)S(1)} %get-tuple-element.22), channel_id=1, source_target_pairs={{0,1},{1,0},{2,3},{3,2},{4,5},{5,4},{6,7},{7,6},{8,9},{9,8},{10,11... | collective-permute-start | bytes 3145736 | tf_op jit(solution)/shard_map/ppermute | solution.py:39

commit v2 on v1

--- a/solution.py
+++ b/solution.py
@@ -11,6 +11,7 @@
 BF16 = jnp.bfloat16
 F32 = jnp.float32
 SIDE = 4
+CHUNKS = 2
 ORDER = (0, 2, 1, 3)
 PLANE = ("x", "y", "c")
 Z = ("zh", "zl")
@@ -57,9 +58,8 @@
 
 
 def project_kernel(place, weight, extra, *refs, centre):
-    pieces, (laid, product) = refs[:4], refs[4:]
+    pieces, (laid, product) = refs[:SIDE], refs[SIDE:]
     thick, part = pieces[0].shape[1:]
-    product[...] = jnp.zeros_like(product)
     for i, piece in enumerate(pieces):
 
         def step(j, carry, i=i, piece=piece):
@@ -69,15 +69,17 @@
             if centre:
                 block = (block.astype(F32) - extra[:, pl.ds(column, part)]).astype(BF16)
             laid[pl.ds(row, thick), pl.ds(column, part)] = block
-            product[pl.ds(row, thick), :] += lax.dot_general(
-                block,
-                weight[:, pl.ds(column, part)],
-                (((1,), (1,)), ((), ())),
-                preferred_element_type=F32,
-            )
             return carry
 
         lax.fori_loop(0, SIDE, step, 0)
+    total = None
+    for q in range(SIDE):
+        columns = pl.ds(q * part, part)
+        term = lax.dot_general(
+            laid[:, columns], weight[:, columns], (((1,), (1,)), ((), ())), preferred_element_type=F32
+        )
+        total = term if total is None else total + term
+    product[...] = total
 
 
 def project(place, weight, extra, pieces, centre):
@@ -96,31 +98,48 @@
     return jnp.concatenate([own[:, :latents] + other[:, latents:], own[:, latents:] + other[:, :latents]], 1)
 
 
-def activate_kernel(own, other, bias, preact, activity, flat):
-    latents = bias.shape[1] // 2
-    value = join(own[...], other[...], latents) + bias[...]
+def recon_kernel(place, own, other, bias, weight, preact, flat, *refs):
+    blocks, (activity, laid) = refs[:SIDE], refs[SIDE:]
+    _, thick, part = blocks[0].shape
+    value = join(own[...], other[...], bias.shape[1] // 2) + bias[...]
     preact[...] = value
     positive = jnp.maximum(value, 0.0)
     activity[...] = positive.astype(BF16)
     flat[...] = positive.T.astype(BF16)
-
-
-def recon_kernel(place, activity, weight, block, *, slot):
-    _, thick, part = block.shape
-
-    def step(j, carry):
-        row = pl.multiple_of(place[0, slot * SIDE + j] * thick, thick)
-        column = pl.multiple_of(place[1, slot * SIDE + j] * part, part)
-        block[j] = jnp.dot(
-            activity[pl.ds(row, thick), :], weight[:, pl.ds(column, part)], preferred_element_type=F32
-        ).astype(BF16)
-        return carry
-
-    lax.fori_loop(0, SIDE, step, 0)
-
-
-def gradient_kernel(own, other, preact, flat, error, centered, mine, theirs, slope, *, chunk):
-    latents = mine.shape[0]
+    for q in range(SIDE):
+        columns = pl.ds(q * part, part)
+        laid[:, columns] = jnp.dot(activity[...], weight[:, columns], preferred_element_type=F32).astype(BF16)
+    for i, block in enumerate(blocks):
+
+        def step(j, carry, i=i, block=block):
+            row = pl.multiple_of(place[0, i * SIDE + j] * thick, thick)
+            column = pl.multiple_of(place[1, i * SIDE + j] * part, part)
+            block[j] = laid[pl.ds(row, thick), pl.ds(column, part)]
+            return carry
+
+        lax.fori_loop(0, SIDE, step, 0)
+
+
+def recon(place, own, other, bias, weight):
+    rows, wide = own.shape
+    width = weight.shape[1]
+    blocks = jax.ShapeDtypeStruct((SIDE, rows // SIDE, width // SIDE), BF16)
+    args = (place, own, other, bias, weight)
+    shapes = (jax.ShapeDtypeStruct((rows, wide), F32), jax.ShapeDtypeStruct((wide, rows), BF16)) + (blocks,) * SIDE
+    return pl.pallas_call(
+        recon_kernel,
+        out_shape=shapes,
+        in_specs=[SMEM] + [VMEM] * 4,
+        out_specs=(VMEM,) * len(shapes),
+        scratch_shapes=[pltpu.VMEM((rows, wide), BF16), pltpu.VMEM((rows, width), BF16)],
+        compiler_params=PARAMS,
+        cost_estimate=pl.CostEstimate(flops=2 * rows * wide * width, bytes_accessed=4 * rows * width, transcendentals=0),
+    )(*args)
+
+
+def gradient_kernel(own, other, preact, flat, error, centered, *refs, chunk, final):
+    slope = refs[-1]
+    latents = preact.shape[1] // 2
     value = jnp.where(preact[...] > 0, join(own[...], other[...], latents), 0.0)
     slope[...] = value.T.astype(BF16)
 
@@ -128,11 +147,35 @@
         columns = pl.ds(pl.multiple_of(j * chunk, chunk), chunk)
         total = jnp.dot(flat[...], error[:, columns], preferred_element_type=F32)
         total += jnp.dot(slope[...], centered[:, columns], preferred_element_type=F32)
-        mine[:, columns] = total[:latents]
-        theirs[:, columns] = total[latents:].astype(BF16)
+        if final:
+            before, mine, theirs = refs[:3]
+            total += before[:, columns]
+            mine[:, columns] = total[:latents]
+            theirs[:, columns] = total[latents:].astype(BF16)
+        else:
+            refs[0][:, columns] = total
         return carry
 
-    lax.fori_loop(0, mine.shape[1] // chunk, step, 0)
+    lax.fori_loop(0, error.shape[1] // chunk, step, 0)
+
+
+def gradient(args, before, chunk=1024):
+    flat, error = args[3], args[4]
+    wide, width = flat.shape[0], error.shape[1]
+    if before is None:
+        shapes = jax.ShapeDtypeStruct((wide, width), F32)
+    else:
+        args = args + (before,)
+        shapes = (jax.ShapeDtypeStruct((wide // 2, width), F32), jax.ShapeDtypeStruct((wide // 2, width), BF16))
+    return pl.pallas_call(
+        functools.partial(gradient_kernel, chunk=chunk, final=before is not None),
+        out_shape=shapes,
+        in_specs=[VMEM] * len(args),
+        out_specs=jax.tree.map(lambda _: VMEM, shapes),
+        scratch_shapes=[pltpu.VMEM(flat.shape, BF16)],
+        compiler_params=PARAMS,
+        cost_estimate=pl.CostEstimate(flops=4 * flat.size * width, bytes_accessed=12 * error.size, transcendentals=0),
+    )(*args)
 
 
 def adam_kernel(at, gradient_ref, first_ref, second_ref, *refs, rows):
@@ -194,62 +237,46 @@
         arrived = lax.ppermute(both, "zh", [(i, (i + by) % SIDE) for i in range(SIDE)])
         block = lax.dynamic_update_slice_in_dim(block, arrived, (zh - by) % SIDE * count, 0)
     source = block
-    thick = source.shape[0]
-    rows = thick * SIDE
-    pieces = spread(jnp.stack(spread(source, False)), True)
+    split = source.shape[0] // CHUNKS
+    gathered = spread(source, False)
 
     taken = swap(lax.dynamic_slice_in_dim(weight, (1 - c) * half, half, 1))
     pair = jnp.concatenate([lax.dynamic_slice_in_dim(weight, c * half, half, 1), taken], 0)
     decoder = lax.dynamic_slice_in_dim(dec_bias, c * half, half, 0)[None, :]
     bias = jnp.concatenate([enc_bias, swap(enc_bias)])[None, :]
-
-    centered, own = project(gather_place, pair, decoder, pieces, True)
-    preact, activity, flat = call(
-        activate_kernel,
-        (
-            jax.ShapeDtypeStruct(own.shape, F32),
-            jax.ShapeDtypeStruct(own.shape, BF16),
-            jax.ShapeDtypeStruct(own.shape[::-1], BF16),
-        ),
-        (own, swap(own), bias),
-        own.size * 4,
-    )
-
-    def recon_block(slot):
-        return call(
-            functools.partial(recon_kernel, slot=slot),
-            jax.ShapeDtypeStruct((SIDE, thick, part), BF16),
-            (send_place, activity, pair),
-            2 * rows * part * 2 * latents,
-            [SMEM, VMEM, VMEM],
-        )
-
-    total = 0.0
-    for slot in (1, 2, 3):
-        total = total + shift(recon_block(slot), ORDER[slot], True).astype(F32)
-    total = (total + recon_block(0).astype(F32)).astype(BF16)
-    strip = total[0].astype(F32)
-    for by in ORDER[1:]:
-        strip = strip + shift(total[ORDER.index(SIDE - by)], by, False).astype(F32)
-    thin = thick // 8
-    parts = lax.all_to_all(strip.astype(BF16).reshape(8, thin, part), Z, 0, 0, tiled=True)
-    recon = jnp.sum(parts.astype(F32), 0)
-    here = lax.dynamic_slice_in_dim(source, z * thin, thin, 0).astype(F32)
-    error = (recon + lax.dynamic_slice_in_dim(decoder, x * part, part, 1) - here).astype(BF16)
-    error = lax.all_to_all(jnp.broadcast_to(error, (8, thin, part)), Z, 0, 0, tiled=True)
-    pieces = spread(jnp.stack(spread(error.reshape(thick, part), False)), True)
-
-    error, own = project(gather_place, pair, decoder, pieces, False)
-    mine, theirs, _ = call(
-        functools.partial(gradient_kernel, chunk=512),
-        (
-            jax.ShapeDtypeStruct((latents, half), F32),
-            jax.ShapeDtypeStruct((latents, half), BF16),
-            jax.ShapeDtypeStruct(flat.shape, BF16),
-        ),
-        (own, swap(own), preact, flat, error, centered),
-        8 * rows * half * latents,
-    )
+    rows = source.shape[0] * SIDE
+    thin = split // 8
+    share = lax.dynamic_slice_in_dim(decoder, x * part, part, 1)
+
+    def reduce(blocks):
+        total = blocks[0].astype(F32)
+        for slot in (1, 2, 3):
+            total = total + shift(blocks[slot], ORDER[slot], True).astype(F32)
+        total = total.astype(BF16)
+        strip = total[0].astype(F32)
+        for by in ORDER[1:]:
+            strip = strip + shift(total[ORDER.index(SIDE - by)], by, False).astype(F32)
+        return lax.all_to_all(strip.astype(BF16).reshape(8, thin, part), Z, 0, 0, tiled=True)
+
+    def expand(parts, k):
+        recon_sum = jnp.sum(parts.astype(F32), 0)
+        here = lax.dynamic_slice_in_dim(source, k * split + z * thin, thin, 0).astype(F32)
+        error = (recon_sum + share - here).astype(BF16)
+        error = lax.all_to_all(jnp.broadcast_to(error, (8, thin, part)), Z, 0, 0, tiled=True)
+        return spread(jnp.stack(spread(error.reshape(split, part), False)), True)
+
+    chunks = range(CHUNKS)
+    pieces = [spread(jnp.stack([g[k * split : (k + 1) * split] for g in gathered]), True) for k in chunks]
+    first = [project(gather_place, pair, decoder, pieces[k], True) for k in chunks]
+    made = [recon(send_place, first[k][1], swap(first[k][1]), bias, pair) for k in chunks]
+    parts = [reduce(made[k][2:]) for k in chunks]
+    pieces = [expand(parts[k], k) for k in chunks]
+    second = [project(gather_place, pair, decoder, pieces[k], False) for k in chunks]
+    total = None
+    for k in chunks:
+        error, own = second[k]
+        total = gradient((own, swap(own), made[k][0], made[k][1], error, first[k][0]), total)
+    mine, theirs = total
     arrived = swap(theirs)
     at = c.astype(jnp.int32)[None]
     outs = adam(at, mine, first_moment, second_moment, (), rows)

time: 230 us -> 232 us (level)
  the two profiles are of different devices: /device:TPU:9 before, /device:TPU:1 now
where the time goes in v2:
time: 232 us; the launch traced here: 227 us
  starting transfers between devices  97.8 us (42%)
  waiting for transfers between devices  59.4 us (26%)
  Pallas kernels  32.2 us (14%)
  blocking collectives  20.6 us (9%)
  local copies, waits for them, and re-layouts  9.14 us (4%)
  other arithmetic  6.88 us (3%)
    ppermute x33, starting transfers between devices, shift(): return lax.ppermute(value, PLANE, plane_pairs(by, last))  41 us
    ppermute x33, waiting for transfers between devices, shift(): return lax.ppermute(value, PLANE, plane_pairs(by, last))  40 us
    ppermute x8, starting transfers between devices, swap(): return lax.ppermute(value, 'c', [(0, 1), (1, 0)])  30.2 us
    all_to_all x2, blocking collectives, expand(): lax.all_to_all(jnp.broadcast_to(error, (8, thin, part)), Z, 0, 0, tiled=T...  20.6 us
    all_to_all x2, starting transfers between devices, reduce(): lax.all_to_all(strip.astype(BF16).reshape(8, thin, part), Z, 0, 0, tiled=...  17.7 us
    all_to_all x2, waiting for transfers between devices, reduce(): lax.all_to_all(strip.astype(BF16).reshape(8, thin, part), Z, 0, 0, tiled=...  14.3 us
    pallas_call x4, Pallas kernels, call(): pl.pallas_call(kernel, out_shape=out_shape, in_specs=specs or [VMEM] * le...  11.2 us
    ppermute x3, starting transfers between devices, body(): lax.ppermute(both, 'zh', [(i, (i + by) % SIDE) for i in range(SIDE)])  8.86 us
  transfers between devices with their start and end apart: 46, of which 18 were waited for; matrix products, arithmetic and copies ran while one was open for 4% of the time, Pallas kernels for 10%

profile of v2, /device:TPU:1, one launch (start us, length us, event | category | flops | bytes accessed | tf_op | source)
XLA Modules:
  0.0 227.2 jit_solution(9798678330984575281)
XLA Ops:
  1.4 3.2 %collective-permute-start.1 = (bf16[16,1024]{1,0:T(8,128)(2,1)S(1)}, bf16[16,1024]{1,0:T(8,128)(2,1)S(1)}, u32[]{:S(2)}, u32[]{:S(2)}) collective-permute-start(bf16[16,1024]{1,0:T(8,128)(2,1)S(1)} %constant_dynamic-slice_fusion), channel_id=1, source_target_pairs={{0,1},{1,0},{2,3},{3,2},{4,5},{5,4},{6,7},{7,6},{8,9},{9,8},{10,11... | collective-permute-start | bytes 98312 | tf_op jit(solution)/shard_map/ppermute | solution.py:40
  4.7 2.7 %constant_dynamic-slice_fusion.2 = (bf16[128,4096]{1,0:T(8,128)(2,1)S(1)}, bf16[128,4096]{1,0:T(8,128)(2,1)}) fusion(bf16[128,8192]{1,0:T(8,128)(2,1)} %param.9, s32[]{:T(128)S(6)} %select_n.154, s32[]{:T(128)S(6)} %select_n.155), kind=kLoop, calls=%fused_computation.46 | loop fusion | bytes 4194312 | tf_op jit(solution)/shard_map/dynamic_slice | solution.py:244
  8.3 5.3 %collective-permute-start.2 = (bf16[32,1024]{1,0:T(8,128)(2,1)S(1)}, bf16[32,1024]{1,0:T(8,128)(2,1)S(1)}, u32[]{:S(2)}, u32[]{:S(2)}) collective-permute-start(bf16[32,1024]{1,0:T(8,128)(2,1)S(1)} %get-tuple-element.73), channel_id=1, source_target_pairs={{0,4},{2,6},{4,0},{6,2},{1,5},{3,7},{5,1},{7,3},{8,12},{10,14},{12... | collective-permute-start | bytes 196616 | tf_op jit(solution)/shard_map/ppermute | solution.py:237
  15.0 2.4 %collective-permute-start.4 = (bf16[32,1024]{1,0:T(8,128)(2,1)S(1)}, bf16[32,1024]{1,0:T(8,128)(2,1)S(1)}, u32[]{:S(2)}, u32[]{:S(2)}) collective-permute-start(bf16[32,1024]{1,0:T(8,128)(2,1)S(1)} %get-tuple-element.73), channel_id=1, source_target_pairs={{0,6},{2,0},{4,2},{6,4},{1,7},{3,1},{5,3},{7,5},{8,14},{10,8},{12,... | collective-permute-start | bytes 196616 | tf_op jit(solution)/shard_map/ppermute | solution.py:237
  17.4 2.1 collective-permute-done.3
  20.0 2.8 %collective-permute-start.5 = (bf16[128,1024]{1,0:T(8,128)(2,1)S(1)}, bf16[128,1024]{1,0:T(8,128)(2,1)S(1)}, u32[]{:S(2)}, u32[]{:S(2)}) collective-permute-start(bf16[128,1024]{1,0:T(8,128)(2,1)S(1)} %constant_dynamic-update-slice_fusion), channel_id=1, source_target_pairs={{0,16},{1,129},{8,24},{9,137},{16,0},{17,145},{24,8},{25,153},{64,... | collective-permute-start | bytes 786440 | tf_op jit(solution)/shard_map/ppermute | solution.py:36
  23.2 2.4 %collective-permute-start.7 = (bf16[128,1024]{1,0:T(8,128)(2,1)S(1)}, bf16[128,1024]{1,0:T(8,128)(2,1)S(1)}, u32[]{:S(2)}, u32[]{:S(2)}) collective-permute-start(bf16[128,1024]{1,0:T(8,128)(2,1)S(1)} %constant_dynamic-update-slice_fusion), channel_id=1, source_target_pairs={{0,24},{1,193},{8,0},{9,201},{16,8},{17,209},{24,16},{25,217},{64,... | collective-permute-start | bytes 786440 | tf_op jit(solution)/shard_map/ppermute | solution.py:36
  25.6 1.5 collective-permute-done.5
  27.1 2.8 %collective-permute-done.6 = bf16[128,1024]{1,0:T(8,128)(2,1)S(1)} collective-permute-done((bf16[128,1024]{1,0:T(8,128)(2,1)S(1)}, bf16[128,1024]{1,0:T(8,128)(2,1)S(1)}, u32[]{:S(2)}, u32[]{:S(2)}) %collective-permute-start.6) | collective-permute-done | bytes 262176 | tf_op jit(solution)/shard_map/ppermute | solution.py:36
  30.1 2.8 %collective-permute-start.10 = (bf16[4,64,1024]{2,1,0:T(8,128)(2,1)S(1)}, bf16[4,64,1024]{2,1,0:T(8,128)(2,1)S(1)}, u32[]{:S(2)}, u32[]{:S(2)}) collective-permute-start(bf16[4,64,1024]{2,1,0:T(8,128)(2,1)S(1)} %pad_maximum_fusion.1.refs_0_), channel_id=1, source_target_pairs={{0,192},{1,25},{8,200},{9,1},{16,208},{17,9},{24,216},{25,17},{64,... | collective-permute-start | bytes 1572872 | tf_op jit(solution)/shard_map/ppermute | solution.py:36
  34.0 2.0 collective-permute-start.26
  36.7 2.7 %pad_maximum_fusion.weight = bf16[256,4096]{1,0:T(8,128)(2,1)} fusion(bf16[128,4096]{1,0:T(8,128)(2,1)} %collective-permute-done, bf16[128,4096]{1,0:T(8,128)(2,1)S(1)} %get-tuple-element.53), kind=kLoop, calls=%fused_computation | loop fusion | flops 4194304 | bytes 4194304 | tf_op jit(solution)/shard_map/concatenate | solution.py:244
  39.4 10.9 %collective-permute-done.10.refs_3_ = bf16[4,64,1024]{2,1,0:T(8,128)(2,1)S(1)} collective-permute-done((bf16[4,64,1024]{2,1,0:T(8,128)(2,1)S(1)}, bf16[4,64,1024]{2,1,0:T(8,128)(2,1)S(1)}, u32[]{:S(2)}, u32[]{:S(2)}) %collective-permute-start.10) | collective-permute-done | bytes 524320 | tf_op jit(solution)/shard_map/ppermute | solution.py:36
  50.2 3.4 %collective-permute-start.28 = (bf16[4,64,1024]{2,1,0:T(8,128)(2,1)S(1)}, bf16[4,64,1024]{2,1,0:T(8,128)(2,1)}, u32[]{:S(2)}, u32[]{:S(2)}) collective-permute-start(bf16[4,64,1024]{2,1,0:T(8,128)(2,1)S(1)} %pad_maximum_fusion.3.refs_0_), channel_id=1, source_target_pairs={{0,192},{1,25},{8,200},{9,1},{16,208},{17,9},{24,216},{25,17},{64,... | collective-permute-start | bytes 1572872 | tf_op jit(solution)/shard_map/ppermute | solution.py:36
  53.7 2.9 %shard_map.94 = (bf16[256,4096]{1,0:T(8,128)(2,1)S(1)}, f32[256,256]{1,0:T(8,128)S(1)}) custom-call(s32[2,16]{1,0:T(2,128)S(1)} %pad_add_fusion.place, bf16[256,4096]{1,0:T(8,128)(2,1)} %pad_maximum_fusion.weight, f32[1,4096]{1,0:T(1,128)S(1)} %bitcast.55, bf16[4,64,1024]{2,1,0:T(8,128)(2,1)S(1)} %pad_maximum_fusion.1.refs_0_, ...), custom_call_target="tpu_custom_call" | custom-call | flops 536870912 | bytes 6570112 | tf_op jit(solution)/shard_map/pallas_call | solution.py:50
  58.0 3.7 %collective-permute-start.11 = (f32[256,256]{1,0:T(8,128)S(1)}, f32[256,256]{1,0:T(8,128)}, u32[]{:S(2)}, u32[]{:S(2)}) collective-permute-start(f32[256,256]{1,0:T(8,128)S(1)} %get-tuple-element.28.own), channel_id=1, source_target_pairs={{0,1},{1,0},{2,3},{3,2},{4,5},{5,4},{6,7},{7,6},{8,9},{9,8},{10,11... | collective-permute-start | bytes 786440 | tf_op jit(solution)/shard_map/ppermute | solution.py:40
  64.7 2.0 shard_map.95
  66.7 2.0 collective-permute-start.13
  68.7 1.4 collective-permute-start.14
  71.4 3.0 %shard_map.97 = (bf16[256,4096]{1,0:T(8,128)(2,1)S(1)}, f32[256,256]{1,0:T(8,128)S(1)}) custom-call(s32[2,16]{1,0:T(2,128)S(1)} %copy-done.10, bf16[256,4096]{1,0:T(8,128)(2,1)} %pad_maximum_fusion.weight, f32[1,4096]{1,0:T(1,128)S(1)} %bitcast.56, bf16[4,64,1024]{2,1,0:T(8,128)(2,1)S(1)} %pad_maximum_fusion.3.refs_0_, ...), custom_call_target="tpu_custom_call" | custom-call | flops 536870912 | bytes 6570112 | tf_op jit(solution)/shard_map/pallas_call | solution.py:50
  75.7 1.5 collective-permute-done.29.other
  77.3 1.6 shard_map.98
  83.1 1.5 collective-permute-start.16
  84.5 4.5 %collective-permute-done.30 = bf16[4,64,1024]{2,1,0:T(8,128)(2,1)S(1)} collective-permute-done((bf16[4,64,1024]{2,1,0:T(8,128)(2,1)S(1)}, bf16[4,64,1024]{2,1,0:T(8,128)(2,1)S(1)}, u32[]{:S(2)}, u32[]{:S(2)}) %collective-permute-start.30) | collective-permute-done | bytes 524320 | tf_op jit(solution)/shard_map/ppermute | solution.py:36
  89.0 8.1 %collective-permute-done.31 = bf16[4,64,1024]{2,1,0:T(8,128)(2,1)S(1)} collective-permute-done((bf16[4,64,1024]{2,1,0:T(8,128)(2,1)S(1)}, bf16[4,64,1024]{2,1,0:T(8,128)(2,1)S(1)}, u32[]{:S(2)}, u32[]{:S(2)}) %collective-permute-start.31) | collective-permute-done | bytes 524320 | tf_op jit(solution)/shard_map/ppermute | solution.py:36
  98.6 2.7 %collective-permute-start.35 = (bf16[64,1024]{1,0:T(8,128)(2,1)S(1)}, bf16[64,1024]{1,0:T(8,128)(2,1)S(1)}, u32[]{:S(2)}, u32[]{:S(2)}) collective-permute-start(bf16[64,1024]{1,0:T(8,128)(2,1)S(1)} %get-tuple-element.56), channel_id=1, source_target_pairs={{0,24},{1,193},{8,0},{9,201},{16,8},{17,209},{24,16},{25,217},{64,... | collective-permute-start | bytes 393224 | tf_op jit(solution)/shard_map/ppermute | solution.py:36
  102.0 14.4 %all-to-all-start = ((bf16[8,8,1024]{2,1,0:T(8,128)(2,1)}), bf16[8,8,1024]{2,1,0:T(8,128)(2,1)S(1)}, u32[]{:S(2)}, u32[]{:S(2)}) async-start(bf16[8,8,1024]{2,1,0:T(8,128)(2,1)} %fusion.6), calls=%async_computation | async-start | bytes 262144 | tf_op jit(solution)/shard_map/all_to_all | solution.py:259
  117.2 7.2 %all-to-all-done = bf16[8,8,1024]{2,1,0:T(8,128)(2,1)S(1)} async-done(((bf16[8,8,1024]{2,1,0:T(8,128)(2,1)}), bf16[8,8,1024]{2,1,0:T(8,128)(2,1)S(1)}, u32[]{:S(2)}, u32[]{:S(2)}) %all-to-all-start) | async-done | bytes 131104 | tf_op jit(solution)/shard_map/all_to_all | solution.py:259
  124.4 3.4 %all-to-all-start.2 = ((bf16[8,8,1024]{2,1,0:T(8,128)(2,1)}), bf16[8,8,1024]{2,1,0:T(8,128)(2,1)S(1)}, u32[]{:S(2)}, u32[]{:S(2)}) async-start(bf16[8,8,1024]{2,1,0:T(8,128)(2,1)} %fusion.7), calls=%async_computation.2 | async-start | bytes 262144 | tf_op jit(solution)/shard_map/all_to_all | solution.py:259
  128.6 7.1 %all-to-all-done.2 = bf16[8,8,1024]{2,1,0:T(8,128)(2,1)S(1)} async-done(((bf16[8,8,1024]{2,1,0:T(8,128)(2,1)}), bf16[8,8,1024]{2,1,0:T(8,128)(2,1)S(1)}, u32[]{:S(2)}, u32[]{:S(2)}) %all-to-all-start.2) | async-done | bytes 131104 | tf_op jit(solution)/shard_map/all_to_all | solution.py:259
  136.5 10.3 %all_to_all.20 = bf16[8,8,1024]{2,1,0:T(8,128)(2,1)S(1)} all-to-all(bf16[8,8,1024]{2,1,0:T(8,128)(2,1)S(1)} %broadcast_in_dim.31), channel_id=1, replica_groups=mesh['x'=4,'zl'=2,'y'=4,'zh'=4,'c'=2] {'zh','zl'}, dimensions={0} | all-to-all | bytes 262144 | tf_op jit(solution)/shard_map/all_to_all | solution.py:265
  147.5 2.7 %collective-permute-start.38 = (bf16[64,1024]{1,0:T(8,128)(2,1)S(1)}, bf16[64,1024]{1,0:T(8,128)(2,1)S(1)}, u32[]{:S(2)}, u32[]{:S(2)}) collective-permute-start(bf16[64,1024]{1,0:T(8,128)(2,1)S(1)} %bitcast.67), channel_id=1, source_target_pairs={{0,24},{1,193},{8,0},{9,201},{16,8},{17,209},{24,16},{25,217},{64,... | collective-permute-start | bytes 393224 | tf_op jit(solution)/shard_map/ppermute | solution.py:36
  150.2 2.0 collective-permute-done.36
  153.6 1.7 collective-permute-start.39
  155.3 10.3 %all_to_all.21 = bf16[8,8,1024]{2,1,0:T(8,128)(2,1)S(1)} all-to-all(bf16[8,8,1024]{2,1,0:T(8,128)(2,1)S(1)} %broadcast_in_dim.30), channel_id=1, replica_groups=mesh['x'=4,'zl'=2,'y'=4,'zh'=4,'c'=2] {'zh','zl'}, dimensions={0} | all-to-all | bytes 262144 | tf_op jit(solution)/shard_map/all_to_all | solution.py:265
  166.0 1.6 collective-permute-start.20
  168.7 4.1 %collective-permute-done.19 = bf16[64,1024]{1,0:T(8,128)(2,1)S(1)} collective-permute-done((bf16[64,1024]{1,0:T(8,128)(2,1)S(1)}, bf16[64,1024]{1,0:T(8,128)(2,1)S(1)}, u32[]{:S(2)}, u32[]{:S(2)}) %collective-permute-start.19) | collective-permute-done | bytes 131104 | tf_op jit(solution)/shard_map/ppermute | solution.py:36
  172.8 2.7 %collective-permute-done.20 = bf16[64,1024]{1,0:T(8,128)(2,1)S(1)} collective-permute-done((bf16[64,1024]{1,0:T(8,128)(2,1)S(1)}, bf16[64,1024]{1,0:T(8,128)(2,1)S(1)}, u32[]{:S(2)}, u32[]{:S(2)}) %collective-permute-start.20) | collective-permute-done | bytes 131104 | tf_op jit(solution)/shard_map/ppermute | solution.py:36
  176.9 2.7 %collective-permute-start.24 = (bf16[4,64,1024]{2,1,0:T(8,128)(2,1)S(1)}, bf16[4,64,1024]{2,1,0:T(8,128)(2,1)S(1)}, u32[]{:S(2)}, u32[]{:S(2)}) collective-permute-start(bf16[4,64,1024]{2,1,0:T(8,128)(2,1)S(1)} %pad_maximum_fusion.2.refs_0_), channel_id=1, source_target_pairs={{0,192},{1,25},{8,200},{9,1},{16,208},{17,9},{24,216},{25,17},{64,... | collective-permute-start | bytes 1572872 | tf_op jit(solution)/shard_map/ppermute | solution.py:36
  179.6 1.7 collective-permute-done.41.refs_3_
  181.2 2.6 %shard_map.99 = (bf16[256,4096]{1,0:T(8,128)(2,1)S(1)}, f32[256,256]{1,0:T(8,128)S(1)}) custom-call(s32[2,16]{1,0:T(2,128)S(1)} %copy-done.11, bf16[256,4096]{1,0:T(8,128)(2,1)} %pad_maximum_fusion.weight, f32[1,4096]{1,0:T(1,128)S(1)} %bitcast.57, bf16[4,64,1024]{2,1,0:T(8,128)(2,1)S(1)} %pad_maximum_fusion.4.refs_0_, ...), custom_call_target="tpu_custom_call" | custom-call | flops 536870912 | bytes 6570112 | tf_op jit(solution)/shard_map/pallas_call | solution.py:50
  183.9 13.2 %collective-permute-start.42 = (f32[256,256]{1,0:T(8,128)S(1)}, f32[256,256]{1,0:T(8,128)S(1)}, u32[]{:S(2)}, u32[]{:S(2)}) collective-permute-start(f32[256,256]{1,0:T(8,128)S(1)} %get-tuple-element.43.own), channel_id=1, source_target_pairs={{0,1},{1,0},{2,3},{3,2},{4,5},{5,4},{6,7},{7,6},{8,9},{9,8},{10,11... | collective-permute-start | bytes 786440 | tf_op jit(solution)/shard_map/ppermute | solution.py:40
  197.1 2.6 %shard_map.96 = (bf16[256,4096]{1,0:T(8,128)(2,1)S(1)}, f32[256,256]{1,0:T(8,128)S(1)}) custom-call(s32[2,16]{1,0:T(2,128)S(1)} %copy-done.11, bf16[256,4096]{1,0:T(8,128)(2,1)} %pad_maximum_fusion.weight, f32[1,4096]{1,0:T(1,128)S(1)} %bitcast.58, bf16[4,64,1024]{2,1,0:T(8,128)(2,1)S(1)} %pad_maximum_fusion.2.refs_0_, ...), custom_call_target="tpu_custom_call" | custom-call | flops 536870912 | bytes 6570112 | tf_op jit(solution)/shard_map/pallas_call | solution.py:50
  199.7 9.7 %collective-permute-start.25 = (f32[256,256]{1,0:T(8,128)S(1)}, f32[256,256]{1,0:T(8,128)S(1)}, u32[]{:S(2)}, u32[]{:S(2)}) collective-permute-start(f32[256,256]{1,0:T(8,128)S(1)} %get-tuple-element.33.own), channel_id=1, source_target_pairs={{0,1},{1,0},{2,3},{3,2},{4,5},{5,4},{6,7},{7,6},{8,9},{9,8},{10,11... | collective-permute-start | bytes 786440 | tf_op jit(solution)/shard_map/ppermute | solution.py:40
  209.4 3.9 %shard_map.100.refs_0_ = f32[256,4096]{1,0:T(8,128)} custom-call(f32[256,256]{1,0:T(8,128)S(1)} %get-tuple-element.43.own, f32[256,256]{1,0:T(8,128)S(1)} %collective-permute-done.42.other, f32[256,256]{1,0:T(8,128)S(1)} %get-tuple-element.44.preact, bf16[256,256]{1,0:T(8,128)(2,1)S(1)} %get-tuple-element.45.flat, ...), custom_call_target="tpu_custom_call" | custom-call | flops 1073741824 | bytes 12582912 | tf_op jit(solution)/shard_map/pallas_call | solution.py:170
  213.3 4.9 %shard_map.101 = (f32[128,4096]{1,0:T(8,128)S(1)}, bf16[128,4096]{1,0:T(8,128)(2,1)S(1)}) custom-call(f32[256,256]{1,0:T(8,128)S(1)} %get-tuple-element.33.own, f32[256,256]{1,0:T(8,128)S(1)} %collective-permute-done.25.other, f32[256,256]{1,0:T(8,128)S(1)} %get-tuple-element.34.preact, bf16[256,256]{1,0:T(8,128)(2,1)S(1)} %get-tuple-element.35.flat, ...), custom_call_target="tpu_custom_call" | custom-call | flops 1073741824 | bytes 12582912 | tf_op jit(solution)/shard_map/pallas_call | solution.py:170
  218.3 4.4 %shard_map.102 = (bf16[128,8192]{1,0:T(8,128)(2,1)}, bf16[128,8192]{1,0:T(8,128)(2,1)}, bf16[128,8192]{1,0:T(8,128)(2,1)}) custom-call(s32[1]{0:T(128)} %bitcast.at, f32[128,4096]{1,0:T(8,128)S(1)} %get-tuple-element.49.gradient_ref, bf16[128,8192]{1,0:T(8,128)(2,1)S(1)} %copy-done.2, bf16[128,8192]{1,0:T(8,128)(2,1)S(1)} %copy-done.3), custom_call_target="tpu_custom_call" | custom-call | flops 10485760 | bytes 7340032 | tf_op jit(solution)/shard_map/pallas_call | solution.py:198
  222.7 4.4 %shard_map.103 = (bf16[128,8192]{1,0:T(8,128)(2,1)}, bf16[128,8192]{1,0:T(8,128)(2,1)}, bf16[128,8192]{1,0:T(8,128)(2,1)}) custom-call(s32[1]{0:T(128)S(6)} %sub.34.at, bf16[128,4096]{1,0:T(8,128)(2,1)S(1)} %collective-permute-done.43.gradient_ref, bf16[128,8192]{1,0:T(8,128)(2,1)S(1)} %copy-done.2, ...), custom_call_target="tpu_custom_call", output_to_operand_aliasing={{0}: (4, {}), {1}: (5, {}), {2}: (6, {})} | custom-call | flops 10485760 | bytes 7340032 | tf_op jit(solution)/shard_map/pallas_call | solution.py:198
  (129 shorter events, 26.6 us)
Async XLA Ops:
  1.4 6.0 %collective-permute-start.1 = (bf16[16,1024]{1,0:T(8,128)(2,1)S(1)}, bf16[16,1024]{1,0:T(8,128)(2,1)S(1)}, u32[]{:S(2)}, u32[]{:S(2)}) collective-permute-start(bf16[16,1024]{1,0:T(8,128)(2,1)S(1)} %constant_dynamic-slice_fusion), channel_id=1, source_target_pairs={{0,1},{1,0},{2,3},{3,2},{4,5},{5,4},{6,7},{7,6},{8,9},{9,8},{10,11... | collective-permute-start | bytes 98312 | tf_op jit(solution)/shard_map/ppermute | solution.py:40
  7.4 28.7 %collective-permute-start = (bf16[128,4096]{1,0:T(8,128)(2,1)}, bf16[128,4096]{1,0:T(8,128)(2,1)}, u32[]{:S(2)}, u32[]{:S(2)}) collective-permute-start(bf16[128,4096]{1,0:T(8,128)(2,1)} %get-tuple-element.54), channel_id=1, source_target_pairs={{0,1},{1,0},{2,3},{3,2},{4,5},{5,4},{6,7},{7,6},{8,9},{9,8},{10,11... | collective-permute-start | bytes 3145736 | tf_op jit(solution)/shard_map/ppermute | solution.py:40
  8.3 9.1 %collective-permute-start.2 = (bf16[32,1024]{1,0:T(8,128)(2,1)S(1)}, bf16[32,1024]{1,0:T(8,128)(2,1)S(1)}, u32[]{:S(2)}, u32[]{:S(2)}) collective-permute-start(bf16[32,1024]{1,0:T(8,128)(2,1)S(1)} %get-tuple-element.73), channel_id=1, source_target_pairs={{0,4},{2,6},{4,0},{6,2},{1,5},{3,7},{5,1},{7,3},{8,12},{10,14},{12... | collective-permute-start | bytes 196616 | tf_op jit(solution)/shard_map/ppermute | solution.py:237
  13.8 5.8 %collective-permute-start.3 = (bf16[32,1024]{1,0:T(8,128)(2,1)S(1)}, bf16[32,1024]{1,0:T(8,128)(2,1)S(1)}, u32[]{:S(2)}, u32[]{:S(2)}) collective-permute-start(bf16[32,1024]{1,0:T(8,128)(2,1)S(1)} %get-tuple-element.73), channel_id=1, source_target_pairs={{0,2},{2,4},{4,6},{6,0},{1,3},{3,5},{5,7},{7,1},{8,10},{10,12},{12... | collective-permute-start | bytes 196616 | tf_op jit(solution)/shard_map/ppermute | solution.py:237
  15.0 5.0 %collective-permute-start.4 = (bf16[32,1024]{1,0:T(8,128)(2,1)S(1)}, bf16[32,1024]{1,0:T(8,128)(2,1)S(1)}, u32[]{:S(2)}, u32[]{:S(2)}) collective-permute-start(bf16[32,1024]{1,0:T(8,128)(2,1)S(1)} %get-tuple-element.73), channel_id=1, source_target_pairs={{0,6},{2,0},{4,2},{6,4},{1,7},{3,1},{5,3},{7,5},{8,14},{10,8},{12,... | collective-permute-start | bytes 196616 | tf_op jit(solution)/shard_map/ppermute | solution.py:237
  20.0 7.1 %collective-permute-start.5 = (bf16[128,1024]{1,0:T(8,128)(2,1)S(1)}, bf16[128,1024]{1,0:T(8,128)(2,1)S(1)}, u32[]{:S(2)}, u32[]{:S(2)}) collective-permute-start(bf16[128,1024]{1,0:T(8,128)(2,1)S(1)} %constant_dynamic-update-slice_fusion), channel_id=1, source_target_pairs={{0,16},{1,129},{8,24},{9,137},{16,0},{17,145},{24,8},{25,153},{64,... | collective-permute-start | bytes 786440 | tf_op jit(solution)/shard_map/ppermute | solution.py:36
  22.8 30.9 %copy-start.9 = (s32[2,16]{1,0:T(2,128)}, s32[2,16]{1,0:T(2,128)S(1)}, u32[]{:S(2)}) copy-start(s32[2,16]{1,0:T(2,128)S(1)} %pad_add_fusion.place) | copy-start | bytes 388
  22.8 7.0 %collective-permute-start.6 = (bf16[128,1024]{1,0:T(8,128)(2,1)S(1)}, bf16[128,1024]{1,0:T(8,128)(2,1)S(1)}, u32[]{:S(2)}, u32[]{:S(2)}) collective-permute-start(bf16[128,1024]{1,0:T(8,128)(2,1)S(1)} %constant_dynamic-update-slice_fusion), channel_id=1, source_target_pairs={{0,8},{1,65},{8,16},{9,73},{16,24},{17,81},{24,0},{25,89},{64,72},... | collective-permute-start | bytes 786440 | tf_op jit(solution)/shard_map/ppermute | solution.py:36
  23.2 6.7 %collective-permute-start.7 = (bf16[128,1024]{1,0:T(8,128)(2,1)S(1)}, bf16[128,1024]{1,0:T(8,128)(2,1)S(1)}, u32[]{:S(2)}, u32[]{:S(2)}) collective-permute-start(bf16[128,1024]{1,0:T(8,128)(2,1)S(1)} %constant_dynamic-update-slice_fusion), channel_id=1, source_target_pairs={{0,24},{1,193},{8,0},{9,201},{16,8},{17,209},{24,16},{25,217},{64,... | collective-permute-start | bytes 786440 | tf_op jit(solution)/shard_map/ppermute | solution.py:36
  30.1 20.2 %collective-permute-start.10 = (bf16[4,64,1024]{2,1,0:T(8,128)(2,1)S(1)}, bf16[4,64,1024]{2,1,0:T(8,128)(2,1)S(1)}, u32[]{:S(2)}, u32[]{:S(2)}) collective-permute-start(bf16[4,64,1024]{2,1,0:T(8,128)(2,1)S(1)} %pad_maximum_fusion.1.refs_0_), channel_id=1, source_target_pairs={{0,192},{1,25},{8,200},{9,1},{16,208},{17,9},{24,216},{25,17},{64,... | collective-permute-start | bytes 1572872 | tf_op jit(solution)/shard_map/ppermute | solution.py:36
  32.9 20.8 %collective-permute-start.8 = (bf16[4,64,1024]{2,1,0:T(8,128)(2,1)S(1)}, bf16[4,64,1024]{2,1,0:T(8,128)(2,1)S(1)}, u32[]{:S(2)}, u32[]{:S(2)}) collective-permute-start(bf16[4,64,1024]{2,1,0:T(8,128)(2,1)S(1)} %pad_maximum_fusion.1.refs_0_), channel_id=1, source_target_pairs={{0,128},{1,17},{8,136},{9,25},{16,144},{17,1},{24,152},{25,9},{64,... | collective-permute-start | bytes 1572872 | tf_op jit(solution)/shard_map/ppermute | solution.py:36
  33.2 20.4 %collective-permute-start.9 = (bf16[4,64,1024]{2,1,0:T(8,128)(2,1)S(1)}, bf16[4,64,1024]{2,1,0:T(8,128)(2,1)S(1)}, u32[]{:S(2)}, u32[]{:S(2)}) collective-permute-start(bf16[4,64,1024]{2,1,0:T(8,128)(2,1)S(1)} %pad_maximum_fusion.1.refs_0_), channel_id=1, source_target_pairs={{0,64},{1,9},{8,72},{9,17},{16,80},{17,25},{24,88},{25,1},{64,128}... | collective-permute-start | bytes 1572872 | tf_op jit(solution)/shard_map/ppermute | solution.py:36
  34.0 36.1 %collective-permute-start.26 = (bf16[4,64,1024]{2,1,0:T(8,128)(2,1)S(1)}, bf16[4,64,1024]{2,1,0:T(8,128)(2,1)S(1)}, u32[]{:S(2)}, u32[]{:S(2)}) collective-permute-start(bf16[4,64,1024]{2,1,0:T(8,128)(2,1)S(1)} %pad_maximum_fusion.3.refs_0_), channel_id=1, source_target_pairs={{0,128},{1,17},{8,136},{9,25},{16,144},{17,1},{24,152},{25,9},{64,... | collective-permute-start | bytes 1572872 | tf_op jit(solution)/shard_map/ppermute | solution.py:36
  36.0 35.3 %collective-permute-start.27 = (bf16[4,64,1024]{2,1,0:T(8,128)(2,1)S(1)}, bf16[4,64,1024]{2,1,0:T(8,128)(2,1)}, u32[]{:S(2)}, u32[]{:S(2)}) collective-permute-start(bf16[4,64,1024]{2,1,0:T(8,128)(2,1)S(1)} %pad_maximum_fusion.3.refs_0_), channel_id=1, source_target_pairs={{0,64},{1,9},{8,72},{9,17},{16,80},{17,25},{24,88},{25,1},{64,128}... | collective-permute-start | bytes 1572872 | tf_op jit(solution)/shard_map/ppermute | solution.py:36
  50.2 21.1 %collective-permute-start.28 = (bf16[4,64,1024]{2,1,0:T(8,128)(2,1)S(1)}, bf16[4,64,1024]{2,1,0:T(8,128)(2,1)}, u32[]{:S(2)}, u32[]{:S(2)}) collective-permute-start(bf16[4,64,1024]{2,1,0:T(8,128)(2,1)S(1)} %pad_maximum_fusion.3.refs_0_), channel_id=1, source_target_pairs={{0,192},{1,25},{8,200},{9,1},{16,208},{17,9},{24,216},{25,17},{64,... | collective-permute-start | bytes 1572872 | tf_op jit(solution)/shard_map/ppermute | solution.py:36
  58.0 5.8 %collective-permute-start.11 = (f32[256,256]{1,0:T(8,128)S(1)}, f32[256,256]{1,0:T(8,128)}, u32[]{:S(2)}, u32[]{:S(2)}) collective-permute-start(f32[256,256]{1,0:T(8,128)S(1)} %get-tuple-element.28.own), channel_id=1, source_target_pairs={{0,1},{1,0},{2,3},{3,2},{4,5},{5,4},{6,7},{7,6},{8,9},{9,8},{10,11... | collective-permute-start | bytes 786440 | tf_op jit(solution)/shard_map/ppermute | solution.py:40
  62.3 1.4 collective-permute-start.12
  66.7 14.2 %collective-permute-start.13 = (bf16[4,64,1024]{2,1,0:T(8,128)(2,1)S(1)}, bf16[4,64,1024]{2,1,0:T(8,128)(2,1)S(1)}, u32[]{:S(2)}, u32[]{:S(2)}) collective-permute-start(bf16[4,64,1024]{2,1,0:T(8,128)(2,1)S(1)} %get-tuple-element.30), channel_id=1, source_target_pairs={{0,128},{1,17},{8,136},{9,25},{16,144},{17,1},{24,152},{25,9},{64,... | collective-permute-start | bytes 1572872 | tf_op jit(solution)/shard_map/ppermute | solution.py:36
  68.7 13.6 %collective-permute-start.14 = (bf16[4,64,1024]{2,1,0:T(8,128)(2,1)S(1)}, bf16[4,64,1024]{2,1,0:T(8,128)(2,1)S(1)}, u32[]{:S(2)}, u32[]{:S(2)}) collective-permute-start(bf16[4,64,1024]{2,1,0:T(8,128)(2,1)S(1)} %get-tuple-element.31), channel_id=1, source_target_pairs={{0,64},{1,9},{8,72},{9,17},{16,80},{17,25},{24,88},{25,1},{64,128}... | collective-permute-start | bytes 1572872 | tf_op jit(solution)/shard_map/ppermute | solution.py:36
  70.1 12.5 %collective-permute-start.15 = (bf16[4,64,1024]{2,1,0:T(8,128)(2,1)S(1)}, bf16[4,64,1024]{2,1,0:T(8,128)(2,1)S(1)}, u32[]{:S(2)}, u32[]{:S(2)}) collective-permute-start(bf16[4,64,1024]{2,1,0:T(8,128)(2,1)S(1)} %get-tuple-element.32), channel_id=1, source_target_pairs={{0,192},{1,25},{8,200},{9,1},{16,208},{17,9},{24,216},{25,17},{64,... | collective-permute-start | bytes 1572872 | tf_op jit(solution)/shard_map/ppermute | solution.py:36
  75.7 1.5 collective-permute-start.29
  78.8 10.2 %collective-permute-start.30 = (bf16[4,64,1024]{2,1,0:T(8,128)(2,1)S(1)}, bf16[4,64,1024]{2,1,0:T(8,128)(2,1)S(1)}, u32[]{:S(2)}, u32[]{:S(2)}) collective-permute-start(bf16[4,64,1024]{2,1,0:T(8,128)(2,1)S(1)} %get-tuple-element.40), channel_id=1, source_target_pairs={{0,128},{1,17},{8,136},{9,25},{16,144},{17,1},{24,152},{25,9},{64,... | collective-permute-start | bytes 1572872 | tf_op jit(solution)/shard_map/ppermute | solution.py:36
  79.6 17.5 %collective-permute-start.31 = (bf16[4,64,1024]{2,1,0:T(8,128)(2,1)S(1)}, bf16[4,64,1024]{2,1,0:T(8,128)(2,1)S(1)}, u32[]{:S(2)}, u32[]{:S(2)}) collective-permute-start(bf16[4,64,1024]{2,1,0:T(8,128)(2,1)S(1)} %get-tuple-element.41), channel_id=1, source_target_pairs={{0,64},{1,9},{8,72},{9,17},{16,80},{17,25},{24,88},{25,1},{64,128}... | collective-permute-start | bytes 1572872 | tf_op jit(solution)/shard_map/ppermute | solution.py:36
  80.9 16.3 %collective-permute-start.32 = (bf16[4,64,1024]{2,1,0:T(8,128)(2,1)S(1)}, bf16[4,64,1024]{2,1,0:T(8,128)(2,1)S(1)}, u32[]{:S(2)}, u32[]{:S(2)}) collective-permute-start(bf16[4,64,1024]{2,1,0:T(8,128)(2,1)S(1)} %get-tuple-element.42), channel_id=1, source_target_pairs={{0,192},{1,25},{8,200},{9,1},{16,208},{17,9},{24,216},{25,17},{64,... | collective-permute-start | bytes 1572872 | tf_op jit(solution)/shard_map/ppermute | solution.py:36
  83.1 15.6 %collective-permute-start.16 = (bf16[64,1024]{1,0:T(8,128)(2,1)S(1)}, bf16[64,1024]{1,0:T(8,128)(2,1)S(1)}, u32[]{:S(2)}, u32[]{:S(2)}) collective-permute-start(bf16[64,1024]{1,0:T(8,128)(2,1)S(1)} %get-tuple-element.58), channel_id=1, source_target_pairs={{0,16},{1,129},{8,24},{9,137},{16,0},{17,145},{24,8},{25,153},{64,... | collective-permute-start | bytes 393224 | tf_op jit(solution)/shard_map/ppermute | solution.py:36
  84.5 16.8 %collective-permute-start.17 = (bf16[64,1024]{1,0:T(8,128)(2,1)S(1)}, bf16[64,1024]{1,0:T(8,128)(2,1)S(1)}, u32[]{:S(2)}, u32[]{:S(2)}) collective-permute-start(bf16[64,1024]{1,0:T(8,128)(2,1)S(1)} %get-tuple-element.60), channel_id=1, source_target_pairs={{0,8},{1,65},{8,16},{9,73},{16,24},{17,81},{24,0},{25,89},{64,72},... | collective-permute-start | bytes 393224 | tf_op jit(solution)/shard_map/ppermute | solution.py:36
  89.0 12.3 %collective-permute-start.18 = (bf16[64,1024]{1,0:T(8,128)(2,1)S(1)}, bf16[64,1024]{1,0:T(8,128)(2,1)S(1)}, u32[]{:S(2)}, u32[]{:S(2)}) collective-permute-start(bf16[64,1024]{1,0:T(8,128)(2,1)S(1)} %get-tuple-element.59), channel_id=1, source_target_pairs={{0,24},{1,193},{8,0},{9,201},{16,8},{17,209},{24,16},{25,217},{64,... | collective-permute-start | bytes 393224 | tf_op jit(solution)/shard_map/ppermute | solution.py:36
  97.6 18.8 %collective-permute-start.33 = (bf16[64,1024]{1,0:T(8,128)(2,1)S(1)}, bf16[64,1024]{1,0:T(8,128)(2,1)S(1)}, u32[]{:S(2)}, u32[]{:S(2)}) collective-permute-start(bf16[64,1024]{1,0:T(8,128)(2,1)S(1)} %get-tuple-element.55), channel_id=1, source_target_pairs={{0,16},{1,129},{8,24},{9,137},{16,0},{17,145},{24,8},{25,153},{64,... | collective-permute-start | bytes 393224 | tf_op jit(solution)/shard_map/ppermute | solution.py:36
  98.6 17.8 %collective-permute-start.34 = (bf16[64,1024]{1,0:T(8,128)(2,1)S(1)}, bf16[64,1024]{1,0:T(8,128)(2,1)S(1)}, u32[]{:S(2)}, u32[]{:S(2)}) collective-permute-start(bf16[64,1024]{1,0:T(8,128)(2,1)S(1)} %get-tuple-element.57), channel_id=1, source_target_pairs={{0,8},{1,65},{8,16},{9,73},{16,24},{17,81},{24,0},{25,89},{64,72},... | collective-permute-start | bytes 393224 | tf_op jit(solution)/shard_map/ppermute | solution.py:36
  98.6 17.8 %collective-permute-start.35 = (bf16[64,1024]{1,0:T(8,128)(2,1)S(1)}, bf16[64,1024]{1,0:T(8,128)(2,1)S(1)}, u32[]{:S(2)}, u32[]{:S(2)}) collective-permute-start(bf16[64,1024]{1,0:T(8,128)(2,1)S(1)} %get-tuple-element.56), channel_id=1, source_target_pairs={{0,24},{1,193},{8,0},{9,201},{16,8},{17,209},{24,16},{25,217},{64,... | collective-permute-start | bytes 393224 | tf_op jit(solution)/shard_map/ppermute | solution.py:36
  102.0 22.4 %all-to-all-start = ((bf16[8,8,1024]{2,1,0:T(8,128)(2,1)}), bf16[8,8,1024]{2,1,0:T(8,128)(2,1)S(1)}, u32[]{:S(2)}, u32[]{:S(2)}) async-start(bf16[8,8,1024]{2,1,0:T(8,128)(2,1)} %fusion.6), calls=%async_computation | async-start | bytes 262144 | tf_op jit(solution)/shard_map/all_to_all | solution.py:259
  116.4 64.8 %copy-start.11 = (s32[2,16]{1,0:T(2,128)S(1)}, s32[2,16]{1,0:T(2,128)}, u32[]{:S(2)}) copy-start(s32[2,16]{1,0:T(2,128)} %copy-done.9) | copy-start | bytes 388
  124.4 11.3 %all-to-all-start.2 = ((bf16[8,8,1024]{2,1,0:T(8,128)(2,1)}), bf16[8,8,1024]{2,1,0:T(8,128)(2,1)S(1)}, u32[]{:S(2)}, u32[]{:S(2)}) async-start(bf16[8,8,1024]{2,1,0:T(8,128)(2,1)} %fusion.7), calls=%async_computation.2 | async-start | bytes 262144 | tf_op jit(solution)/shard_map/all_to_all | solution.py:259
  146.8 5.4 %collective-permute-start.36 = (bf16[64,1024]{1,0:T(8,128)(2,1)S(1)}, bf16[64,1024]{1,0:T(8,128)(2,1)S(1)}, u32[]{:S(2)}, u32[]{:S(2)}) collective-permute-start(bf16[64,1024]{1,0:T(8,128)(2,1)S(1)} %bitcast.65), channel_id=1, source_target_pairs={{0,16},{1,129},{8,24},{9,137},{16,0},{17,145},{24,8},{25,153},{64,... | collective-permute-start | bytes 393224 | tf_op jit(solution)/shard_map/ppermute | solution.py:36
  147.5 6.0 %collective-permute-start.37 = (bf16[64,1024]{1,0:T(8,128)(2,1)S(1)}, bf16[64,1024]{1,0:T(8,128)(2,1)S(1)}, u32[]{:S(2)}, u32[]{:S(2)}) collective-permute-start(bf16[64,1024]{1,0:T(8,128)(2,1)S(1)} %bitcast.66), channel_id=1, source_target_pairs={{0,8},{1,65},{8,16},{9,73},{16,24},{17,81},{24,0},{25,89},{64,72},... | collective-permute-start | bytes 393224 | tf_op jit(solution)/shard_map/ppermute | solution.py:36
  147.5 6.0 %collective-permute-start.38 = (bf16[64,1024]{1,0:T(8,128)(2,1)S(1)}, bf16[64,1024]{1,0:T(8,128)(2,1)S(1)}, u32[]{:S(2)}, u32[]{:S(2)}) collective-permute-start(bf16[64,1024]{1,0:T(8,128)(2,1)S(1)} %bitcast.67), channel_id=1, source_target_pairs={{0,24},{1,193},{8,0},{9,201},{16,8},{17,209},{24,16},{25,217},{64,... | collective-permute-start | bytes 393224 | tf_op jit(solution)/shard_map/ppermute | solution.py:36
  153.6 23.2 %collective-permute-start.39 = (bf16[4,64,1024]{2,1,0:T(8,128)(2,1)S(1)}, bf16[4,64,1024]{2,1,0:T(8,128)(2,1)S(1)}, u32[]{:S(2)}, u32[]{:S(2)}) collective-permute-start(bf16[4,64,1024]{2,1,0:T(8,128)(2,1)S(1)} %pad_maximum_fusion.4.refs_0_), channel_id=1, source_target_pairs={{0,128},{1,17},{8,136},{9,25},{16,144},{17,1},{24,152},{25,9},{64,... | collective-permute-start | bytes 1572872 | tf_op jit(solution)/shard_map/ppermute | solution.py:36
  165.6 7.1 %collective-permute-start.19 = (bf16[64,1024]{1,0:T(8,128)(2,1)S(1)}, bf16[64,1024]{1,0:T(8,128)(2,1)S(1)}, u32[]{:S(2)}, u32[]{:S(2)}) collective-permute-start(bf16[64,1024]{1,0:T(8,128)(2,1)S(1)} %bitcast.61), channel_id=1, source_target_pairs={{0,16},{1,129},{8,24},{9,137},{16,0},{17,145},{24,8},{25,153},{64,... | collective-permute-start | bytes 393224 | tf_op jit(solution)/shard_map/ppermute | solution.py:36
  166.0 9.5 %collective-permute-start.20 = (bf16[64,1024]{1,0:T(8,128)(2,1)S(1)}, bf16[64,1024]{1,0:T(8,128)(2,1)S(1)}, u32[]{:S(2)}, u32[]{:S(2)}) collective-permute-start(bf16[64,1024]{1,0:T(8,128)(2,1)S(1)} %bitcast.62), channel_id=1, source_target_pairs={{0,8},{1,65},{8,16},{9,73},{16,24},{17,81},{24,0},{25,89},{64,72},... | collective-permute-start | bytes 393224 | tf_op jit(solution)/shard_map/ppermute | solution.py:36
  167.6 7.9 %collective-permute-start.21 = (bf16[64,1024]{1,0:T(8,128)(2,1)S(1)}, bf16[64,1024]{1,0:T(8,128)(2,1)S(1)}, u32[]{:S(2)}, u32[]{:S(2)}) collective-permute-start(bf16[64,1024]{1,0:T(8,128)(2,1)S(1)} %bitcast.63), channel_id=1, source_target_pairs={{0,24},{1,193},{8,0},{9,201},{16,8},{17,209},{24,16},{25,217},{64,... | collective-permute-start | bytes 393224 | tf_op jit(solution)/shard_map/ppermute | solution.py:36
  168.7 10.9 %collective-permute-start.40 = (bf16[4,64,1024]{2,1,0:T(8,128)(2,1)S(1)}, bf16[4,64,1024]{2,1,0:T(8,128)(2,1)S(1)}, u32[]{:S(2)}, u32[]{:S(2)}) collective-permute-start(bf16[4,64,1024]{2,1,0:T(8,128)(2,1)S(1)} %pad_maximum_fusion.4.refs_0_), channel_id=1, source_target_pairs={{0,64},{1,9},{8,72},{9,17},{16,80},{17,25},{24,88},{25,1},{64,128}... | collective-permute-start | bytes 1572872 | tf_op jit(solution)/shard_map/ppermute | solution.py:36
  172.8 8.5 %collective-permute-start.41 = (bf16[4,64,1024]{2,1,0:T(8,128)(2,1)S(1)}, bf16[4,64,1024]{2,1,0:T(8,128)(2,1)S(1)}, u32[]{:S(2)}, u32[]{:S(2)}) collective-permute-start(bf16[4,64,1024]{2,1,0:T(8,128)(2,1)S(1)} %pad_maximum_fusion.4.refs_0_), channel_id=1, source_target_pairs={{0,192},{1,25},{8,200},{9,1},{16,208},{17,9},{24,216},{25,17},{64,... | collective-permute-start | bytes 1572872 | tf_op jit(solution)/shard_map/ppermute | solution.py:36
  175.6 21.5 %collective-permute-start.22 = (bf16[4,64,1024]{2,1,0:T(8,128)(2,1)S(1)}, bf16[4,64,1024]{2,1,0:T(8,128)(2,1)S(1)}, u32[]{:S(2)}, u32[]{:S(2)}) collective-permute-start(bf16[4,64,1024]{2,1,0:T(8,128)(2,1)S(1)} %pad_maximum_fusion.2.refs_0_), channel_id=1, source_target_pairs={{0,128},{1,17},{8,136},{9,25},{16,144},{17,1},{24,152},{25,9},{64,... | collective-permute-start | bytes 1572872 | tf_op jit(solution)/shard_map/ppermute | solution.py:36
  176.9 20.2 %collective-permute-start.23 = (bf16[4,64,1024]{2,1,0:T(8,128)(2,1)S(1)}, bf16[4,64,1024]{2,1,0:T(8,128)(2,1)S(1)}, u32[]{:S(2)}, u32[]{:S(2)}) collective-permute-start(bf16[4,64,1024]{2,1,0:T(8,128)(2,1)S(1)} %pad_maximum_fusion.2.refs_0_), channel_id=1, source_target_pairs={{0,64},{1,9},{8,72},{9,17},{16,80},{17,25},{24,88},{25,1},{64,128}... | collective-permute-start | bytes 1572872 | tf_op jit(solution)/shard_map/ppermute | solution.py:36
  176.9 20.2 %collective-permute-start.24 = (bf16[4,64,1024]{2,1,0:T(8,128)(2,1)S(1)}, bf16[4,64,1024]{2,1,0:T(8,128)(2,1)S(1)}, u32[]{:S(2)}, u32[]{:S(2)}) collective-permute-start(bf16[4,64,1024]{2,1,0:T(8,128)(2,1)S(1)} %pad_maximum_fusion.2.refs_0_), channel_id=1, source_target_pairs={{0,192},{1,25},{8,200},{9,1},{16,208},{17,9},{24,216},{25,17},{64,... | collective-permute-start | bytes 1572872 | tf_op jit(solution)/shard_map/ppermute | solution.py:36
  183.9 25.5 %collective-permute-start.42 = (f32[256,256]{1,0:T(8,128)S(1)}, f32[256,256]{1,0:T(8,128)S(1)}, u32[]{:S(2)}, u32[]{:S(2)}) collective-permute-start(f32[256,256]{1,0:T(8,128)S(1)} %get-tuple-element.43.own), channel_id=1, source_target_pairs={{0,1},{1,0},{2,3},{3,2},{4,5},{5,4},{6,7},{7,6},{8,9},{9,8},{10,11... | collective-permute-start | bytes 786440 | tf_op jit(solution)/shard_map/ppermute | solution.py:40
  199.7 13.6 %collective-permute-start.25 = (f32[256,256]{1,0:T(8,128)S(1)}, f32[256,256]{1,0:T(8,128)S(1)}, u32[]{:S(2)}, u32[]{:S(2)}) collective-permute-start(f32[256,256]{1,0:T(8,128)S(1)} %get-tuple-element.33.own), channel_id=1, source_target_pairs={{0,1},{1,0},{2,3},{3,2},{4,5},{5,4},{6,7},{7,6},{8,9},{9,8},{10,11... | collective-permute-start | bytes 786440 | tf_op jit(solution)/shard_map/ppermute | solution.py:40
  218.2 4.5 %collective-permute-start.43 = (bf16[128,4096]{1,0:T(8,128)(2,1)S(1)}, bf16[128,4096]{1,0:T(8,128)(2,1)S(1)}, u32[]{:S(2)}, u32[]{:S(2)}) collective-permute-start(bf16[128,4096]{1,0:T(8,128)(2,1)S(1)} %get-tuple-element.48), channel_id=1, source_target_pairs={{0,1},{1,0},{2,3},{3,2},{4,5},{5,4},{6,7},{7,6},{8,9},{9,8},{10,11... | collective-permute-start | bytes 3145736 | tf_op jit(solution)/shard_map/ppermute | solution.py:40
  (15 other events, 112.0 us)

commit v3 on v2

--- a/solution.py
+++ b/solution.py
@@ -17,7 +17,7 @@
 Z = ("zh", "zl")
 VMEM = pl.BlockSpec(memory_space=pltpu.VMEM)
 SMEM = pl.BlockSpec(memory_space=pltpu.SMEM)
-PARAMS = pltpu.CompilerParams(vmem_limit_bytes=48 * 1024 * 1024)
+PARAMS = pltpu.CompilerParams(vmem_limit_bytes=16 * 1024 * 1024)
 
 
 def plane_pairs(by, last):
@@ -44,21 +44,8 @@
     return [piece] + [shift(piece, by, last) for by in ORDER[1:]]
 
 
-def call(kernel, out_shape, args, flops, specs=None, params=PARAMS):
-    shapes = jax.tree.leaves(out_shape)
-    moved = sum(a.size * a.dtype.itemsize for a in list(args) + shapes)
-    return pl.pallas_call(
-        kernel,
-        out_shape=out_shape,
-        in_specs=specs or [VMEM] * len(args),
-        out_specs=jax.tree.map(lambda _: VMEM, out_shape),
-        compiler_params=params,
-        cost_estimate=pl.CostEstimate(flops=flops, bytes_accessed=moved, transcendentals=0),
-    )(*args)
-
-
-def project_kernel(place, weight, extra, *refs, centre):
-    pieces, (laid, product) = refs[:SIDE], refs[SIDE:]
+def project_kernel(place, weight, extra, lift, *refs, centre):
+    pieces, (laid, product) = refs[:SIDE], refs[-2:]
     thick, part = pieces[0].shape[1:]
     for i, piece in enumerate(pieces):
 
@@ -72,7 +59,7 @@
             return carry
 
         lax.fori_loop(0, SIDE, step, 0)
-    total = None
+    total = lift[...] if centre else None
     for q in range(SIDE):
         columns = pl.ds(q * part, part)
         term = lax.dot_general(
@@ -82,26 +69,30 @@
     product[...] = total
 
 
-def project(place, weight, extra, pieces, centre):
+def project(place, weight, extra, lift, pieces, centre, after=()):
     thick, part = pieces[0].shape[1:]
     rows, width = thick * SIDE, part * SIDE
-    return call(
+    args = (place, weight, extra, lift, *pieces, *after)
+    return pl.pallas_call(
         functools.partial(project_kernel, centre=centre),
-        (jax.ShapeDtypeStruct((rows, width), BF16), jax.ShapeDtypeStruct((rows, weight.shape[0]), F32)),
-        (place, weight, extra, *pieces),
-        2 * rows * width * weight.shape[0],
-        [SMEM] + [VMEM] * (2 + SIDE),
-    )
+        out_shape=(jax.ShapeDtypeStruct((rows, width), BF16), jax.ShapeDtypeStruct((rows, weight.shape[0]), F32)),
+        in_specs=[SMEM] + [VMEM] * (3 + SIDE) + [pl.BlockSpec(memory_space=pl.ANY)] * len(after),
+        out_specs=(VMEM, VMEM),
+        compiler_params=PARAMS,
+        cost_estimate=pl.CostEstimate(
+            flops=2 * rows * width * weight.shape[0], bytes_accessed=4 * rows * width, transcendentals=0
+        ),
+    )(*args)
 
 
 def join(own, other, latents):
     return jnp.concatenate([own[:, :latents] + other[:, latents:], own[:, latents:] + other[:, :latents]], 1)
 
 
-def recon_kernel(place, own, other, bias, weight, preact, flat, *refs):
+def recon_kernel(place, own, other, weight, preact, flat, *refs):
     blocks, (activity, laid) = refs[:SIDE], refs[SIDE:]
     _, thick, part = blocks[0].shape
-    value = join(own[...], other[...], bias.shape[1] // 2) + bias[...]
+    value = join(own[...], other[...], own.shape[1] // 2)
     preact[...] = value
     positive = jnp.maximum(value, 0.0)
     activity[...] = positive.astype(BF16)
@@ -120,16 +111,16 @@
         lax.fori_loop(0, SIDE, step, 0)
 
 
-def recon(place, own, other, bias, weight):
+def recon(place, own, other, weight):
     rows, wide = own.shape
     width = weight.shape[1]
     blocks = jax.ShapeDtypeStruct((SIDE, rows // SIDE, width // SIDE), BF16)
-    args = (place, own, other, bias, weight)
+    args = (place, own, other, weight)
     shapes = (jax.ShapeDtypeStruct((rows, wide), F32), jax.ShapeDtypeStruct((wide, rows), BF16)) + (blocks,) * SIDE
     return pl.pallas_call(
         recon_kernel,
         out_shape=shapes,
-        in_specs=[SMEM] + [VMEM] * 4,
+        in_specs=[SMEM] + [VMEM] * 3,
         out_specs=(VMEM,) * len(shapes),
         scratch_shapes=[pltpu.VMEM((rows, wide), BF16), pltpu.VMEM((rows, width), BF16)],
         compiler_params=PARAMS,
@@ -189,7 +180,7 @@
     second_out[...] = second.astype(BF16)
 
 
-def adam(at, gradient, first_moment, second_moment, outs, rows, chunk=512):
+def adam(at, gradient, first_moment, second_moment, outs, rows, chunk=1024):
     latents, width = gradient.shape
     count = width // chunk
     here = pl.BlockSpec((latents, chunk), lambda i, at: (0, i))
@@ -215,7 +206,7 @@
     half = width // 2
     part = half // SIDE
     x, y, c = lax.axis_index("x"), lax.axis_index("y"), lax.axis_index("c")
-    zh, z = lax.axis_index("zh"), lax.axis_index(Z)
+    z = lax.axis_index(Z)
     last_me, first_me = jnp.where(c == 0, x, y), jnp.where(c == 0, y, x)
     order = jnp.array(ORDER, jnp.int32)
     behind_last = jnp.repeat((last_me - order) % SIDE, SIDE)
@@ -227,15 +218,10 @@
 
     gather_place, send_place = places(behind_last), places(ahead_last)
 
-    kept = lax.dynamic_slice_in_dim(inputs, c * half + x * part, part, 1)
-    given = swap(lax.dynamic_slice_in_dim(inputs, (1 - c) * half + x * part, part, 1))
-    both = jnp.concatenate([jnp.where(c == 0, kept, given), jnp.where(c == 0, given, kept)], 0)
-    count = both.shape[0]
-    block = jnp.zeros((SIDE * count, part), BF16)
-    block = lax.dynamic_update_slice_in_dim(block, both, zh * count, 0)
-    for by in ORDER[1:]:
-        arrived = lax.ppermute(both, "zh", [(i, (i + by) % SIDE) for i in range(SIDE)])
-        block = lax.dynamic_update_slice_in_dim(block, arrived, (zh - by) % SIDE * count, 0)
+    own_columns = [lax.dynamic_slice_in_dim(inputs, core * half + x * part, part, 1) for core in range(2)]
+    block = jnp.broadcast_to(jnp.stack(own_columns), (SIDE, 2) + own_columns[0].shape)
+    block = lax.all_to_all(block.reshape((8,) + own_columns[0].shape), ("zh", "c"), 0, 0, tiled=True)
+    block = block.reshape(-1, part)
     source = block
     split = source.shape[0] // CHUNKS
     gathered = spread(source, False)
@@ -243,7 +229,7 @@
     taken = swap(lax.dynamic_slice_in_dim(weight, (1 - c) * half, half, 1))
     pair = jnp.concatenate([lax.dynamic_slice_in_dim(weight, c * half, half, 1), taken], 0)
     decoder = lax.dynamic_slice_in_dim(dec_bias, c * half, half, 0)[None, :]
-    bias = jnp.concatenate([enc_bias, swap(enc_bias)])[None, :]
+    lift = jnp.concatenate([enc_bias, jnp.zeros_like(enc_bias)])[None, :]
     rows = source.shape[0] * SIDE
     thin = split // 8
     share = lax.dynamic_slice_in_dim(decoder, x * part, part, 1)
@@ -256,26 +242,24 @@
         strip = total[0].astype(F32)
         for by in ORDER[1:]:
             strip = strip + shift(total[ORDER.index(SIDE - by)], by, False).astype(F32)
-        return lax.all_to_all(strip.astype(BF16).reshape(8, thin, part), Z, 0, 0, tiled=True)
-
-    def expand(parts, k):
-        recon_sum = jnp.sum(parts.astype(F32), 0)
-        here = lax.dynamic_slice_in_dim(source, k * split + z * thin, thin, 0).astype(F32)
-        error = (recon_sum + share - here).astype(BF16)
-        error = lax.all_to_all(jnp.broadcast_to(error, (8, thin, part)), Z, 0, 0, tiled=True)
-        return spread(jnp.stack(spread(error.reshape(split, part), False)), True)
+        return strip.astype(BF16).reshape(8, thin, part)
 
     chunks = range(CHUNKS)
     pieces = [spread(jnp.stack([g[k * split : (k + 1) * split] for g in gathered]), True) for k in chunks]
-    first = [project(gather_place, pair, decoder, pieces[k], True) for k in chunks]
-    made = [recon(send_place, first[k][1], swap(first[k][1]), bias, pair) for k in chunks]
-    parts = [reduce(made[k][2:]) for k in chunks]
-    pieces = [expand(parts[k], k) for k in chunks]
-    second = [project(gather_place, pair, decoder, pieces[k], False) for k in chunks]
+    ahead = [project(gather_place, pair, decoder, lift, pieces[k], True) for k in chunks]
+    made = [recon(send_place, ahead[k][1], swap(ahead[k][1]), pair) for k in chunks]
+    parts = jnp.concatenate([reduce(made[k][2:]) for k in chunks], 1)
+    recon_sum = jnp.sum(lax.all_to_all(parts, Z, 0, 0, tiled=True).astype(F32), 0)
+    here = [lax.dynamic_slice_in_dim(source, k * split + z * thin, thin, 0) for k in chunks]
+    error = (recon_sum + share - jnp.concatenate(here, 0).astype(F32)).astype(BF16)
+    error = lax.all_to_all(jnp.broadcast_to(error, (8,) + error.shape), Z, 0, 0, tiled=True)
+    error = [error[:, k * thin : (k + 1) * thin].reshape(split, part) for k in chunks]
+    pieces = [spread(jnp.stack(spread(error[k], False)), True) for k in chunks]
     total = None
     for k in chunks:
-        error, own = second[k]
-        total = gradient((own, swap(own), made[k][0], made[k][1], error, first[k][0]), total)
+        after = () if total is None else (total,)
+        laid, own = project(gather_place, pair, decoder, lift, pieces[k], False, after)
+        total = gradient((own, swap(own), made[k][0], made[k][1], laid, ahead[k][0]), total)
     mine, theirs = total
     arrived = swap(theirs)
     at = c.astype(jnp.int32)[None]

time: 232 us -> 193 us (0.83); the launches traced: 227 us -> 192 us
  Pallas kernels: 32.2 us -> 21.3 us
  blocking collectives: 20.6 us -> 11.8 us
  starting transfers between devices: 97.8 us -> 89.5 us
  waiting for transfers between devices: 59.4 us -> 54.6 us
  other arithmetic: 6.88 us -> 3.44 us
    all_to_all x2 -> x1, blocking collectives: 20.6 us -> 11.8 us  [body(): lax.all_to_all(jnp.broadcast_to(error, (8,) + error.shape), Z, 0, 0, tile...]
    ppermute x3 -> x0, starting transfers between devices: 8.86 us -> none  [body(): lax.ppermute(both, 'zh', [(i, (i + by) % SIDE) for i in range(SIDE)])]
    ppermute x33, starting transfers between devices: 41 us -> 48.6 us  [shift(): return lax.ppermute(value, PLANE, plane_pairs(by, last))]
    pallas_call x2, Pallas kernels: 8.74 us -> 3.74 us  [gradient(): pl.pallas_call(functools.partial(gradient_kernel, chunk=chunk, final=befo...]
    all_to_all x2, starting transfers between devices: 17.7 us -> 13.4 us  [the longest x1 9.97 us: body(): lax.all_to_all(block.reshape((8,) + own_columns[0].shape), ('zh', 'c'), 0...]
    ppermute x33, waiting for transfers between devices: 40 us -> 35.9 us  [shift(): return lax.ppermute(value, PLANE, plane_pairs(by, last))]
    pallas_call x4, Pallas kernels: 11.2 us -> 7.22 us  [project(): pl.pallas_call(functools.partial(project_kernel, centre=centre), out_shap...]
    ppermute x8 -> x6, starting transfers between devices: 30.2 us -> 27.5 us  [swap(): return lax.ppermute(value, 'c', [(0, 1), (1, 0)])]
  transfers between devices with their start and end apart: 46 -> 41, of which waited for: 18 -> 21; matrix products, arithmetic and copies ran while one was open for 4% -> 4% of each run, Pallas kernels for 10% -> 8%
where the time goes in v3:
time: 193 us; the launch traced here: 192 us
  starting transfers between devices  89.5 us (46%)
  waiting for transfers between devices  54.6 us (28%)
  Pallas kernels  21.3 us (11%)
  blocking collectives  11.8 us (6%)
  local copies, waits for them, and re-layouts  10.7 us (6%)
  other arithmetic  3.44 us (2%)
    ppermute x33, starting transfers between devices, shift(): return lax.ppermute(value, PLANE, plane_pairs(by, last))  48.6 us
    ppermute x33, waiting for transfers between devices, shift(): return lax.ppermute(value, PLANE, plane_pairs(by, last))  35.9 us
    ppermute x6, starting transfers between devices, swap(): return lax.ppermute(value, 'c', [(0, 1), (1, 0)])  27.5 us
    all_to_all x1, blocking collectives, body(): lax.all_to_all(jnp.broadcast_to(error, (8,) + error.shape), Z, 0, 0, tile...  11.8 us
    all_to_all x1, starting transfers between devices, body(): lax.all_to_all(block.reshape((8,) + own_columns[0].shape), ('zh', 'c'), 0...  9.97 us
    all_to_all x1, waiting for transfers between devices, body(): lax.all_to_all(parts, Z, 0, 0, tiled=True).astype(F32)  7.76 us
    pallas_call x4, Pallas kernels, project(): pl.pallas_call(functools.partial(project_kernel, centre=centre), out_shap...  7.22 us
    all_to_all x1, waiting for transfers between devices, body(): lax.all_to_all(block.reshape((8,) + own_columns[0].shape), ('zh', 'c'), 0...  7.04 us
  transfers between devices with their start and end apart: 41, of which 21 were waited for; matrix products, arithmetic and copies ran while one was open for 4% of the time, Pallas kernels for 8%

profile of v3, /device:TPU:1, one launch (start us, length us, event | category | flops | bytes accessed | tf_op | source)
XLA Modules:
  0.0 192.4 jit_solution(11993606213399990459)
XLA Ops:
  2.2 10.0 %all-to-all-start = ((bf16[8,16,1024]{2,1,0:T(8,128)(2,1)}), bf16[8,16,1024]{2,1,0:T(8,128)(2,1)S(1)}, u32[]{:S(2)}, u32[]{:S(2)}) async-start(bf16[8,16,1024]{2,1,0:T(8,128)(2,1)} %bitcast.5), calls=%async_computation | async-start | bytes 524288 | tf_op jit(solution)/shard_map/all_to_all | solution.py:223
  12.2 2.8 %constant_dynamic-slice_fusion.3 = (bf16[128,4096]{1,0:T(8,128)(2,1)}, bf16[128,4096]{1,0:T(8,128)(2,1)S(1)}) fusion(bf16[128,8192]{1,0:T(8,128)(2,1)} %param.9, s32[]{:T(128)S(6)} %select_n.116, s32[]{:T(128)S(6)} %select_n.117), kind=kLoop, calls=%fused_computation.53 | loop fusion | bytes 4194312 | tf_op jit(solution)/shard_map/dynamic_slice | solution.py:230
  15.2 7.0 %all-to-all-done = bf16[8,16,1024]{2,1,0:T(8,128)(2,1)S(1)} async-done(((bf16[8,16,1024]{2,1,0:T(8,128)(2,1)}), bf16[8,16,1024]{2,1,0:T(8,128)(2,1)S(1)}, u32[]{:S(2)}, u32[]{:S(2)}) %all-to-all-start) | async-done | bytes 262176 | tf_op jit(solution)/shard_map/all_to_all | solution.py:223
  22.2 2.7 %collective-permute-start.1 = (bf16[128,1024]{1,0:T(8,128)(2,1)S(1)}, bf16[128,1024]{1,0:T(8,128)(2,1)S(1)}, u32[]{:S(2)}, u32[]{:S(2)}) collective-permute-start(bf16[128,1024]{1,0:T(8,128)(2,1)S(1)} %bitcast.71), channel_id=1, source_target_pairs={{0,16},{1,129},{8,24},{9,137},{16,0},{17,145},{24,8},{25,153},{64,... | collective-permute-start | bytes 786440 | tf_op jit(solution)/shard_map/ppermute | solution.py:36
  25.5 2.4 %collective-permute-start.3 = (bf16[128,1024]{1,0:T(8,128)(2,1)S(1)}, bf16[128,1024]{1,0:T(8,128)(2,1)S(1)}, u32[]{:S(2)}, u32[]{:S(2)}) collective-permute-start(bf16[128,1024]{1,0:T(8,128)(2,1)S(1)} %bitcast.73), channel_id=1, source_target_pairs={{0,24},{1,193},{8,0},{9,201},{16,8},{17,209},{24,16},{25,217},{64,... | collective-permute-start | bytes 786440 | tf_op jit(solution)/shard_map/ppermute | solution.py:36
  29.0 3.1 %collective-permute-done.2 = bf16[128,1024]{1,0:T(8,128)(2,1)S(1)} collective-permute-done((bf16[128,1024]{1,0:T(8,128)(2,1)S(1)}, bf16[128,1024]{1,0:T(8,128)(2,1)S(1)}, u32[]{:S(2)}, u32[]{:S(2)}) %collective-permute-start.2) | collective-permute-done | bytes 262176 | tf_op jit(solution)/shard_map/ppermute | solution.py:36
  32.2 3.0 %collective-permute-start.4 = (bf16[4,64,1024]{2,1,0:T(8,128)(2,1)S(1)}, bf16[4,64,1024]{2,1,0:T(8,128)(2,1)S(1)}, u32[]{:S(2)}, u32[]{:S(2)}) collective-permute-start(bf16[4,64,1024]{2,1,0:T(8,128)(2,1)S(1)} %pad_maximum_fusion.1.refs_0_), channel_id=1, source_target_pairs={{0,128},{1,17},{8,136},{9,25},{16,144},{17,1},{24,152},{25,9},{64,... | collective-permute-start | bytes 1572872 | tf_op jit(solution)/shard_map/ppermute | solution.py:36
  35.6 2.3 %collective-permute-start.6 = (bf16[4,64,1024]{2,1,0:T(8,128)(2,1)S(1)}, bf16[4,64,1024]{2,1,0:T(8,128)(2,1)S(1)}, u32[]{:S(2)}, u32[]{:S(2)}) collective-permute-start(bf16[4,64,1024]{2,1,0:T(8,128)(2,1)S(1)} %pad_maximum_fusion.1.refs_0_), channel_id=1, source_target_pairs={{0,192},{1,25},{8,200},{9,1},{16,208},{17,9},{24,216},{25,17},{64,... | collective-permute-start | bytes 1572872 | tf_op jit(solution)/shard_map/ppermute | solution.py:36
  38.7 1.4 pad_maximum_fusion.weight
  40.1 2.1 %collective-permute-done.4.refs_1_ = bf16[4,64,1024]{2,1,0:T(8,128)(2,1)S(1)} collective-permute-done((bf16[4,64,1024]{2,1,0:T(8,128)(2,1)S(1)}, bf16[4,64,1024]{2,1,0:T(8,128)(2,1)S(1)}, u32[]{:S(2)}, u32[]{:S(2)}) %collective-permute-start.4) | collective-permute-done | bytes 524320 | tf_op jit(solution)/shard_map/ppermute | solution.py:36
  42.2 2.8 %collective-permute-start.16 = (bf16[4,64,1024]{2,1,0:T(8,128)(2,1)S(1)}, bf16[4,64,1024]{2,1,0:T(8,128)(2,1)}, u32[]{:S(2)}, u32[]{:S(2)}) collective-permute-start(bf16[4,64,1024]{2,1,0:T(8,128)(2,1)S(1)} %pad_maximum_fusion.2.refs_0_), channel_id=1, source_target_pairs={{0,192},{1,25},{8,200},{9,1},{16,208},{17,9},{24,216},{25,17},{64,... | collective-permute-start | bytes 1572872 | tf_op jit(solution)/shard_map/ppermute | solution.py:36
  44.9 2.8 %collective-permute-done.5.refs_2_ = bf16[4,64,1024]{2,1,0:T(8,128)(2,1)S(1)} collective-permute-done((bf16[4,64,1024]{2,1,0:T(8,128)(2,1)S(1)}, bf16[4,64,1024]{2,1,0:T(8,128)(2,1)S(1)}, u32[]{:S(2)}, u32[]{:S(2)}) %collective-permute-start.5) | collective-permute-done | bytes 524320 | tf_op jit(solution)/shard_map/ppermute | solution.py:36
  48.2 1.7 shard_map.94
  49.9 1.3 copy-done.2
  51.2 4.1 %collective-permute-start.7 = (f32[256,256]{1,0:T(8,128)S(1)}, f32[256,256]{1,0:T(8,128)}, u32[]{:S(2)}, u32[]{:S(2)}) collective-permute-start(f32[256,256]{1,0:T(8,128)S(1)} %get-tuple-element.28.own), channel_id=1, source_target_pairs={{0,1},{1,0},{2,3},{3,2},{4,5},{5,4},{6,7},{7,6},{8,9},{9,8},{10,11... | collective-permute-start | bytes 786440 | tf_op jit(solution)/shard_map/ppermute | solution.py:40
  57.5 2.0 %shard_map.95 = (f32[256,256]{1,0:T(8,128)S(1)}, bf16[256,256]{1,0:T(8,128)(2,1)S(1)}, bf16[4,64,1024]{2,1,0:T(8,128)(2,1)S(1)}, bf16[4,64,1024]{2,1,0:T(8,128)(...) custom-call(s32[2,16]{1,0:T(2,128)S(1)} %pad_add_fusion.1.place, f32[256,256]{1,0:T(8,128)S(1)} %copy-done.7, ...), custom_call_target="tpu_custom_call" | custom-call | flops 536870912 | bytes 4194304 | tf_op jit(solution)/shard_map/pallas_call | solution.py:120
  59.5 2.9 %collective-permute-start.10 = (bf16[4,64,1024]{2,1,0:T(8,128)(2,1)S(1)}, bf16[4,64,1024]{2,1,0:T(8,128)(2,1)S(1)}, u32[]{:S(2)}, u32[]{:S(2)}) collective-permute-start(bf16[4,64,1024]{2,1,0:T(8,128)(2,1)S(1)} %get-tuple-element.32), channel_id=1, source_target_pairs={{0,192},{1,25},{8,200},{9,1},{16,208},{17,9},{24,216},{25,17},{64,... | collective-permute-start | bytes 1572872 | tf_op jit(solution)/shard_map/ppermute | solution.py:36
  63.1 2.4 %shard_map.96 = (bf16[256,4096]{1,0:T(8,128)(2,1)S(1)}, f32[256,256]{1,0:T(8,128)S(1)}) custom-call(s32[2,16]{1,0:T(2,128)S(1)} %copy-done.9, bf16[256,4096]{1,0:T(8,128)(2,1)S(1)} %pad_maximum_fusion.weight, f32[1,4096]{1,0:T(1,128)S(1)} %bitcast.64, f32[1,256]{1,0:T(1,128)S(1)} %bitcast.68, bf16[4,64,1024]{2,1,0:T(8,128)(2,1)S(1)} %pad_maximum_fusion.2.refs_0_, ...), custom_call_target="tpu_custom_call" | custom-call | flops 536870912 | bytes 4194304 | tf_op jit(solution)/shard_map/pallas_call | solution.py:76
  68.5 1.6 shard_map.97
  70.1 2.3 %collective-permute-start.18 = (bf16[4,64,1024]{2,1,0:T(8,128)(2,1)S(1)}, bf16[4,64,1024]{2,1,0:T(8,128)(2,1)S(1)}, u32[]{:S(2)}, u32[]{:S(2)}) collective-permute-start(bf16[4,64,1024]{2,1,0:T(8,128)(2,1)S(1)} %get-tuple-element.35), channel_id=1, source_target_pairs={{0,128},{1,17},{8,136},{9,25},{16,144},{17,1},{24,152},{25,9},{64,... | collective-permute-start | bytes 1572872 | tf_op jit(solution)/shard_map/ppermute | solution.py:36
  73.6 6.2 %collective-permute-done.10 = bf16[4,64,1024]{2,1,0:T(8,128)(2,1)S(1)} collective-permute-done((bf16[4,64,1024]{2,1,0:T(8,128)(2,1)S(1)}, bf16[4,64,1024]{2,1,0:T(8,128)(2,1)S(1)}, u32[]{:S(2)}, u32[]{:S(2)}) %collective-permute-start.10) | collective-permute-done | bytes 524320 | tf_op jit(solution)/shard_map/ppermute | solution.py:36
  79.8 3.4 %collective-permute-start.20 = (bf16[4,64,1024]{2,1,0:T(8,128)(2,1)S(1)}, bf16[4,64,1024]{2,1,0:T(8,128)(2,1)S(1)}, u32[]{:S(2)}, u32[]{:S(2)}) collective-permute-start(bf16[4,64,1024]{2,1,0:T(8,128)(2,1)S(1)} %get-tuple-element.37), channel_id=1, source_target_pairs={{0,192},{1,25},{8,200},{9,1},{16,208},{17,9},{24,216},{25,17},{64,... | collective-permute-start | bytes 1572872 | tf_op jit(solution)/shard_map/ppermute | solution.py:36
  83.8 3.4 %collective-permute-start.13 = (bf16[64,1024]{1,0:T(8,128)(2,1)S(1)}, bf16[64,1024]{1,0:T(8,128)(2,1)S(1)}, u32[]{:S(2)}, u32[]{:S(2)}) collective-permute-start(bf16[64,1024]{1,0:T(8,128)(2,1)S(1)} %get-tuple-element.56), channel_id=1, source_target_pairs={{0,24},{1,193},{8,0},{9,201},{16,8},{17,209},{24,16},{25,217},{64,... | collective-permute-start | bytes 393224 | tf_op jit(solution)/shard_map/ppermute | solution.py:36
  87.2 4.5 %collective-permute-done.19 = bf16[4,64,1024]{2,1,0:T(8,128)(2,1)S(1)} collective-permute-done((bf16[4,64,1024]{2,1,0:T(8,128)(2,1)S(1)}, bf16[4,64,1024]{2,1,0:T(8,128)(2,1)S(1)}, u32[]{:S(2)}, u32[]{:S(2)}) %collective-permute-start.19) | collective-permute-done | bytes 524320 | tf_op jit(solution)/shard_map/ppermute | solution.py:36
  94.9 1.5 collective-permute-start.23
  96.4 1.7 collective-permute-done.21
  98.2 1.3 collective-permute-done.22
  100.3 3.4 %all-to-all-start.1 = ((bf16[8,16,1024]{2,1,0:T(8,128)(2,1)}), bf16[8,16,1024]{2,1,0:T(8,128)(2,1)S(1)}, u32[]{:S(2)}, u32[]{:S(2)}) async-start(bf16[8,16,1024]{2,1,0:T(8,128)(2,1)} %pad_maximum_fusion.5), calls=%async_computation.1 | async-start | bytes 524288 | tf_op jit(solution)/shard_map/all_to_all | solution.py:252
  105.3 7.8 %all-to-all-done.1 = bf16[8,16,1024]{2,1,0:T(8,128)(2,1)S(1)} async-done(((bf16[8,16,1024]{2,1,0:T(8,128)(2,1)}), bf16[8,16,1024]{2,1,0:T(8,128)(2,1)S(1)}, u32[]{:S(2)}, u32[]{:S(2)}) %all-to-all-start.1) | async-done | bytes 262176 | tf_op jit(solution)/shard_map/all_to_all | solution.py:252
  113.1 11.8 %all_to_all.15 = bf16[8,16,1024]{2,1,0:T(8,128)(2,1)S(1)} all-to-all(bf16[8,16,1024]{2,1,0:T(8,128)(2,1)S(1)} %broadcast_in_dim.28), channel_id=1, replica_groups=mesh['x'=4,'zl'=2,'y'=4,'zh'=4,'c'=2] {'zh','zl'}, dimensions={0} | all-to-all | bytes 524288 | tf_op jit(solution)/shard_map/all_to_all | solution.py:255
  124.9 1.6 collective-permute-start.30
  126.5 2.4 %collective-permute-start.31 = (bf16[64,1024]{1,0:T(8,128)(2,1)S(1)}, bf16[64,1024]{1,0:T(8,128)(2,1)S(1)}, u32[]{:S(2)}, u32[]{:S(2)}) collective-permute-start(bf16[64,1024]{1,0:T(8,128)(2,1)S(1)} %get-tuple-element.63), channel_id=1, source_target_pairs={{0,8},{1,65},{8,16},{9,73},{16,24},{17,81},{24,0},{25,89},{64,72},... | collective-permute-start | bytes 393224 | tf_op jit(solution)/shard_map/ppermute | solution.py:36
  130.4 1.4 collective-permute-done.31
  133.1 2.9 %collective-permute-start.34 = (bf16[4,64,1024]{2,1,0:T(8,128)(2,1)S(1)}, bf16[4,64,1024]{2,1,0:T(8,128)(2,1)S(1)}, u32[]{:S(2)}, u32[]{:S(2)}) collective-permute-start(bf16[4,64,1024]{2,1,0:T(8,128)(2,1)S(1)} %pad_maximum_fusion.4.refs_0_), channel_id=1, source_target_pairs={{0,64},{1,9},{8,72},{9,17},{16,80},{17,25},{24,88},{25,1},{64,128}... | collective-permute-start | bytes 1572872 | tf_op jit(solution)/shard_map/ppermute | solution.py:36
  136.0 1.5 collective-permute-start.24
  137.5 1.4 collective-permute-start.25
  138.9 2.4 %collective-permute-done.24 = bf16[64,1024]{1,0:T(8,128)(2,1)S(1)} collective-permute-done((bf16[64,1024]{1,0:T(8,128)(2,1)S(1)}, bf16[64,1024]{1,0:T(8,128)(2,1)S(1)}, u32[]{:S(2)}, u32[]{:S(2)}) %collective-permute-start.24) | collective-permute-done | bytes 131104 | tf_op jit(solution)/shard_map/ppermute | solution.py:36
  141.3 2.3 %collective-permute-start.26 = (bf16[64,1024]{1,0:T(8,128)(2,1)S(1)}, bf16[64,1024]{1,0:T(8,128)(2,1)S(1)}, u32[]{:S(2)}, u32[]{:S(2)}) collective-permute-start(bf16[64,1024]{1,0:T(8,128)(2,1)S(1)} %get-tuple-element.62), channel_id=1, source_target_pairs={{0,24},{1,193},{8,0},{9,201},{16,8},{17,209},{24,16},{25,217},{64,... | collective-permute-start | bytes 393224 | tf_op jit(solution)/shard_map/ppermute | solution.py:36
  143.6 6.3 %collective-permute-done.26 = bf16[64,1024]{1,0:T(8,128)(2,1)S(1)} collective-permute-done((bf16[64,1024]{1,0:T(8,128)(2,1)S(1)}, bf16[64,1024]{1,0:T(8,128)(2,1)S(1)}, u32[]{:S(2)}, u32[]{:S(2)}) %collective-permute-start.26) | collective-permute-done | bytes 131104 | tf_op jit(solution)/shard_map/ppermute | solution.py:36
  150.1 1.9 collective-permute-start.28
  153.3 1.6 shard_map.98
  154.8 15.6 %collective-permute-start.36 = (f32[256,256]{1,0:T(8,128)S(1)}, f32[256,256]{1,0:T(8,128)S(1)}, u32[]{:S(2)}, u32[]{:S(2)}) collective-permute-start(f32[256,256]{1,0:T(8,128)S(1)} %get-tuple-element.38.own), channel_id=1, source_target_pairs={{0,1},{1,0},{2,3},{3,2},{4,5},{5,4},{6,7},{7,6},{8,9},{9,8},{10,11... | collective-permute-start | bytes 786440 | tf_op jit(solution)/shard_map/ppermute | solution.py:40
  171.6 1.9 shard_map.99.refs_4_.refs_0_
  173.5 1.6 shard_map.100
  175.1 6.9 %collective-permute-start.37 = (f32[256,256]{1,0:T(8,128)S(1)}, f32[256,256]{1,0:T(8,128)S(1)}, u32[]{:S(2)}, u32[]{:S(2)}) collective-permute-start(f32[256,256]{1,0:T(8,128)S(1)} %get-tuple-element.43.own), channel_id=1, source_target_pairs={{0,1},{1,0},{2,3},{3,2},{4,5},{5,4},{6,7},{7,6},{8,9},{9,8},{10,11... | collective-permute-start | bytes 786440 | tf_op jit(solution)/shard_map/ppermute | solution.py:40
  183.2 1.9 shard_map.101
  185.5 3.4 %shard_map.102 = (bf16[128,8192]{1,0:T(8,128)(2,1)}, bf16[128,8192]{1,0:T(8,128)(2,1)}, bf16[128,8192]{1,0:T(8,128)(2,1)}) custom-call(s32[1]{0:T(128)} %bitcast.at, f32[128,4096]{1,0:T(8,128)S(1)} %get-tuple-element.49.gradient_ref, bf16[128,8192]{1,0:T(8,128)(2,1)S(1)} %copy-done, bf16[128,8192]{1,0:T(8,128)(2,1)S(1)} %copy-done.1), custom_call_target="tpu_custom_call" | custom-call | flops 10485760 | bytes 7340032 | tf_op jit(solution)/shard_map/pallas_call | solution.py:189
  189.0 3.4 %shard_map.103 = (bf16[128,8192]{1,0:T(8,128)(2,1)}, bf16[128,8192]{1,0:T(8,128)(2,1)}, bf16[128,8192]{1,0:T(8,128)(2,1)}) custom-call(s32[1]{0:T(128)S(6)} %sub.21.at, bf16[128,4096]{1,0:T(8,128)(2,1)S(1)} %collective-permute-done.38.gradient_ref, bf16[128,8192]{1,0:T(8,128)(2,1)S(1)} %copy-done, ...), custom_call_target="tpu_custom_call", output_to_operand_aliasing={{0}: (4, {}), {1}: (5, {}), {2}: (6, {})} | custom-call | flops 10485760 | bytes 7340032 | tf_op jit(solution)/shard_map/pallas_call | solution.py:189
  (121 shorter events, 25.5 us)
Async XLA Ops:
  2.2 20.1 %all-to-all-start = ((bf16[8,16,1024]{2,1,0:T(8,128)(2,1)}), bf16[8,16,1024]{2,1,0:T(8,128)(2,1)S(1)}, u32[]{:S(2)}, u32[]{:S(2)}) async-start(bf16[8,16,1024]{2,1,0:T(8,128)(2,1)} %bitcast.5), calls=%async_computation | async-start | bytes 524288 | tf_op jit(solution)/shard_map/all_to_all | solution.py:223
  14.9 23.2 %collective-permute-start = (bf16[128,4096]{1,0:T(8,128)(2,1)S(1)}, bf16[128,4096]{1,0:T(8,128)(2,1)}, u32[]{:S(2)}, u32[]{:S(2)}) collective-permute-start(bf16[128,4096]{1,0:T(8,128)(2,1)S(1)} %get-tuple-element.54), channel_id=1, source_target_pairs={{0,1},{1,0},{2,3},{3,2},{4,5},{5,4},{6,7},{7,6},{8,9},{9,8},{10,11... | collective-permute-start | bytes 3145736 | tf_op jit(solution)/shard_map/ppermute | solution.py:40
  22.2 15.8 %copy-start.15 = (bf16[8,16,1024]{2,1,0:T(8,128)(2,1)}, bf16[8,16,1024]{2,1,0:T(8,128)(2,1)S(1)}, u32[]{:S(2)}) copy-start(bf16[8,16,1024]{2,1,0:T(8,128)(2,1)S(1)} %all-to-all-done) | copy-start | bytes 786436
  22.2 6.7 %collective-permute-start.1 = (bf16[128,1024]{1,0:T(8,128)(2,1)S(1)}, bf16[128,1024]{1,0:T(8,128)(2,1)S(1)}, u32[]{:S(2)}, u32[]{:S(2)}) collective-permute-start(bf16[128,1024]{1,0:T(8,128)(2,1)S(1)} %bitcast.71), channel_id=1, source_target_pairs={{0,16},{1,129},{8,24},{9,137},{16,0},{17,145},{24,8},{25,153},{64,... | collective-permute-start | bytes 786440 | tf_op jit(solution)/shard_map/ppermute | solution.py:36
  25.0 23.2 %copy-start.8 = (s32[2,16]{1,0:T(2,128)}, s32[2,16]{1,0:T(2,128)S(1)}, u32[]{:S(2)}) copy-start(s32[2,16]{1,0:T(2,128)S(1)} %pad_add_fusion.place) | copy-start | bytes 388
  25.0 23.1 %copy-start.11 = (f32[256]{0:T(256)}, f32[256]{0:T(256)S(1)}, u32[]{:S(2)}) copy-start(f32[256]{0:T(256)S(1)} %concatenate.13) | copy-start | bytes 3076
  25.1 13.6 %copy-start.14 = (bf16[128,4096]{1,0:T(8,128)(2,1)S(1)}, bf16[128,4096]{1,0:T(8,128)(2,1)}, u32[]{:S(2)}) copy-start(bf16[128,4096]{1,0:T(8,128)(2,1)} %get-tuple-element.53) | copy-start | bytes 3145732
  25.1 7.0 %collective-permute-start.2 = (bf16[128,1024]{1,0:T(8,128)(2,1)S(1)}, bf16[128,1024]{1,0:T(8,128)(2,1)S(1)}, u32[]{:S(2)}, u32[]{:S(2)}) collective-permute-start(bf16[128,1024]{1,0:T(8,128)(2,1)S(1)} %bitcast.72), channel_id=1, source_target_pairs={{0,8},{1,65},{8,16},{9,73},{16,24},{17,81},{24,0},{25,89},{64,72},... | collective-permute-start | bytes 786440 | tf_op jit(solution)/shard_map/ppermute | solution.py:36
  25.5 6.6 %collective-permute-start.3 = (bf16[128,1024]{1,0:T(8,128)(2,1)S(1)}, bf16[128,1024]{1,0:T(8,128)(2,1)S(1)}, u32[]{:S(2)}, u32[]{:S(2)}) collective-permute-start(bf16[128,1024]{1,0:T(8,128)(2,1)S(1)} %bitcast.73), channel_id=1, source_target_pairs={{0,24},{1,193},{8,0},{9,201},{16,8},{17,209},{24,16},{25,217},{64,... | collective-permute-start | bytes 786440 | tf_op jit(solution)/shard_map/ppermute | solution.py:36
  32.2 10.0 %collective-permute-start.4 = (bf16[4,64,1024]{2,1,0:T(8,128)(2,1)S(1)}, bf16[4,64,1024]{2,1,0:T(8,128)(2,1)S(1)}, u32[]{:S(2)}, u32[]{:S(2)}) collective-permute-start(bf16[4,64,1024]{2,1,0:T(8,128)(2,1)S(1)} %pad_maximum_fusion.1.refs_0_), channel_id=1, source_target_pairs={{0,128},{1,17},{8,136},{9,25},{16,144},{17,1},{24,152},{25,9},{64,... | collective-permute-start | bytes 1572872 | tf_op jit(solution)/shard_map/ppermute | solution.py:36
  35.3 12.5 %collective-permute-start.5 = (bf16[4,64,1024]{2,1,0:T(8,128)(2,1)S(1)}, bf16[4,64,1024]{2,1,0:T(8,128)(2,1)S(1)}, u32[]{:S(2)}, u32[]{:S(2)}) collective-permute-start(bf16[4,64,1024]{2,1,0:T(8,128)(2,1)S(1)} %pad_maximum_fusion.1.refs_0_), channel_id=1, source_target_pairs={{0,64},{1,9},{8,72},{9,17},{16,80},{17,25},{24,88},{25,1},{64,128}... | collective-permute-start | bytes 1572872 | tf_op jit(solution)/shard_map/ppermute | solution.py:36
  35.6 12.5 %collective-permute-start.6 = (bf16[4,64,1024]{2,1,0:T(8,128)(2,1)S(1)}, bf16[4,64,1024]{2,1,0:T(8,128)(2,1)S(1)}, u32[]{:S(2)}, u32[]{:S(2)}) collective-permute-start(bf16[4,64,1024]{2,1,0:T(8,128)(2,1)S(1)} %pad_maximum_fusion.1.refs_0_), channel_id=1, source_target_pairs={{0,192},{1,25},{8,200},{9,1},{16,208},{17,9},{24,216},{25,17},{64,... | collective-permute-start | bytes 1572872 | tf_op jit(solution)/shard_map/ppermute | solution.py:36
  38.0 24.5 %collective-permute-start.14 = (bf16[4,64,1024]{2,1,0:T(8,128)(2,1)S(1)}, bf16[4,64,1024]{2,1,0:T(8,128)(2,1)S(1)}, u32[]{:S(2)}, u32[]{:S(2)}) collective-permute-start(bf16[4,64,1024]{2,1,0:T(8,128)(2,1)S(1)} %pad_maximum_fusion.2.refs_0_), channel_id=1, source_target_pairs={{0,128},{1,17},{8,136},{9,25},{16,144},{17,1},{24,152},{25,9},{64,... | collective-permute-start | bytes 1572872 | tf_op jit(solution)/shard_map/ppermute | solution.py:36
  38.1 25.0 %collective-permute-start.15 = (bf16[4,64,1024]{2,1,0:T(8,128)(2,1)S(1)}, bf16[4,64,1024]{2,1,0:T(8,128)(2,1)}, u32[]{:S(2)}, u32[]{:S(2)}) collective-permute-start(bf16[4,64,1024]{2,1,0:T(8,128)(2,1)S(1)} %pad_maximum_fusion.2.refs_0_), channel_id=1, source_target_pairs={{0,64},{1,9},{8,72},{9,17},{16,80},{17,25},{24,88},{25,1},{64,128}... | collective-permute-start | bytes 1572872 | tf_op jit(solution)/shard_map/ppermute | solution.py:36
  42.2 21.0 %collective-permute-start.16 = (bf16[4,64,1024]{2,1,0:T(8,128)(2,1)S(1)}, bf16[4,64,1024]{2,1,0:T(8,128)(2,1)}, u32[]{:S(2)}, u32[]{:S(2)}) collective-permute-start(bf16[4,64,1024]{2,1,0:T(8,128)(2,1)S(1)} %pad_maximum_fusion.2.refs_0_), channel_id=1, source_target_pairs={{0,192},{1,25},{8,200},{9,1},{16,208},{17,9},{24,216},{25,17},{64,... | collective-permute-start | bytes 1572872 | tf_op jit(solution)/shard_map/ppermute | solution.py:36
  51.2 5.4 %collective-permute-start.7 = (f32[256,256]{1,0:T(8,128)S(1)}, f32[256,256]{1,0:T(8,128)}, u32[]{:S(2)}, u32[]{:S(2)}) collective-permute-start(f32[256,256]{1,0:T(8,128)S(1)} %get-tuple-element.28.own), channel_id=1, source_target_pairs={{0,1},{1,0},{2,3},{3,2},{4,5},{5,4},{6,7},{7,6},{8,9},{9,8},{10,11... | collective-permute-start | bytes 786440 | tf_op jit(solution)/shard_map/ppermute | solution.py:40
  59.5 20.3 %collective-permute-start.10 = (bf16[4,64,1024]{2,1,0:T(8,128)(2,1)S(1)}, bf16[4,64,1024]{2,1,0:T(8,128)(2,1)S(1)}, u32[]{:S(2)}, u32[]{:S(2)}) collective-permute-start(bf16[4,64,1024]{2,1,0:T(8,128)(2,1)S(1)} %get-tuple-element.32), channel_id=1, source_target_pairs={{0,192},{1,25},{8,200},{9,1},{16,208},{17,9},{24,216},{25,17},{64,... | collective-permute-start | bytes 1572872 | tf_op jit(solution)/shard_map/ppermute | solution.py:36
  62.4 20.8 %collective-permute-start.8 = (bf16[4,64,1024]{2,1,0:T(8,128)(2,1)S(1)}, bf16[4,64,1024]{2,1,0:T(8,128)(2,1)S(1)}, u32[]{:S(2)}, u32[]{:S(2)}) collective-permute-start(bf16[4,64,1024]{2,1,0:T(8,128)(2,1)S(1)} %get-tuple-element.30), channel_id=1, source_target_pairs={{0,128},{1,17},{8,136},{9,25},{16,144},{17,1},{24,152},{25,9},{64,... | collective-permute-start | bytes 1572872 | tf_op jit(solution)/shard_map/ppermute | solution.py:36
  62.5 20.7 %collective-permute-start.9 = (bf16[4,64,1024]{2,1,0:T(8,128)(2,1)S(1)}, bf16[4,64,1024]{2,1,0:T(8,128)(2,1)S(1)}, u32[]{:S(2)}, u32[]{:S(2)}) collective-permute-start(bf16[4,64,1024]{2,1,0:T(8,128)(2,1)S(1)} %get-tuple-element.31), channel_id=1, source_target_pairs={{0,64},{1,9},{8,72},{9,17},{16,80},{17,25},{24,88},{25,1},{64,128}... | collective-permute-start | bytes 1572872 | tf_op jit(solution)/shard_map/ppermute | solution.py:36
  66.9 1.6 collective-permute-start.17
  70.1 13.7 %collective-permute-start.18 = (bf16[4,64,1024]{2,1,0:T(8,128)(2,1)S(1)}, bf16[4,64,1024]{2,1,0:T(8,128)(2,1)S(1)}, u32[]{:S(2)}, u32[]{:S(2)}) collective-permute-start(bf16[4,64,1024]{2,1,0:T(8,128)(2,1)S(1)} %get-tuple-element.35), channel_id=1, source_target_pairs={{0,128},{1,17},{8,136},{9,25},{16,144},{17,1},{24,152},{25,9},{64,... | collective-permute-start | bytes 1572872 | tf_op jit(solution)/shard_map/ppermute | solution.py:36
  72.4 19.3 %collective-permute-start.19 = (bf16[4,64,1024]{2,1,0:T(8,128)(2,1)S(1)}, bf16[4,64,1024]{2,1,0:T(8,128)(2,1)S(1)}, u32[]{:S(2)}, u32[]{:S(2)}) collective-permute-start(bf16[4,64,1024]{2,1,0:T(8,128)(2,1)S(1)} %get-tuple-element.36), channel_id=1, source_target_pairs={{0,64},{1,9},{8,72},{9,17},{16,80},{17,25},{24,88},{25,1},{64,128}... | collective-permute-start | bytes 1572872 | tf_op jit(solution)/shard_map/ppermute | solution.py:36
  79.8 12.3 %collective-permute-start.20 = (bf16[4,64,1024]{2,1,0:T(8,128)(2,1)S(1)}, bf16[4,64,1024]{2,1,0:T(8,128)(2,1)S(1)}, u32[]{:S(2)}, u32[]{:S(2)}) collective-permute-start(bf16[4,64,1024]{2,1,0:T(8,128)(2,1)S(1)} %get-tuple-element.37), channel_id=1, source_target_pairs={{0,192},{1,25},{8,200},{9,1},{16,208},{17,9},{24,216},{25,17},{64,... | collective-permute-start | bytes 1572872 | tf_op jit(solution)/shard_map/ppermute | solution.py:36
  83.6 11.2 %collective-permute-start.11 = (bf16[64,1024]{1,0:T(8,128)(2,1)S(1)}, bf16[64,1024]{1,0:T(8,128)(2,1)S(1)}, u32[]{:S(2)}, u32[]{:S(2)}) collective-permute-start(bf16[64,1024]{1,0:T(8,128)(2,1)S(1)} %get-tuple-element.55), channel_id=1, source_target_pairs={{0,16},{1,129},{8,24},{9,137},{16,0},{17,145},{24,8},{25,153},{64,... | collective-permute-start | bytes 393224 | tf_op jit(solution)/shard_map/ppermute | solution.py:36
  83.7 12.6 %collective-permute-start.12 = (bf16[64,1024]{1,0:T(8,128)(2,1)S(1)}, bf16[64,1024]{1,0:T(8,128)(2,1)S(1)}, u32[]{:S(2)}, u32[]{:S(2)}) collective-permute-start(bf16[64,1024]{1,0:T(8,128)(2,1)S(1)} %get-tuple-element.57), channel_id=1, source_target_pairs={{0,8},{1,65},{8,16},{9,73},{16,24},{17,81},{24,0},{25,89},{64,72},... | collective-permute-start | bytes 393224 | tf_op jit(solution)/shard_map/ppermute | solution.py:36
  83.8 12.5 %collective-permute-start.13 = (bf16[64,1024]{1,0:T(8,128)(2,1)S(1)}, bf16[64,1024]{1,0:T(8,128)(2,1)S(1)}, u32[]{:S(2)}, u32[]{:S(2)}) collective-permute-start(bf16[64,1024]{1,0:T(8,128)(2,1)S(1)} %get-tuple-element.56), channel_id=1, source_target_pairs={{0,24},{1,193},{8,0},{9,201},{16,8},{17,209},{24,16},{25,217},{64,... | collective-permute-start | bytes 393224 | tf_op jit(solution)/shard_map/ppermute | solution.py:36
  92.5 5.7 %collective-permute-start.21 = (bf16[64,1024]{1,0:T(8,128)(2,1)S(1)}, bf16[64,1024]{1,0:T(8,128)(2,1)S(1)}, u32[]{:S(2)}, u32[]{:S(2)}) collective-permute-start(bf16[64,1024]{1,0:T(8,128)(2,1)S(1)} %get-tuple-element.58), channel_id=1, source_target_pairs={{0,16},{1,129},{8,24},{9,137},{16,0},{17,145},{24,8},{25,153},{64,... | collective-permute-start | bytes 393224 | tf_op jit(solution)/shard_map/ppermute | solution.py:36
  93.7 5.8 %collective-permute-start.22 = (bf16[64,1024]{1,0:T(8,128)(2,1)S(1)}, bf16[64,1024]{1,0:T(8,128)(2,1)S(1)}, u32[]{:S(2)}, u32[]{:S(2)}) collective-permute-start(bf16[64,1024]{1,0:T(8,128)(2,1)S(1)} %get-tuple-element.60), channel_id=1, source_target_pairs={{0,8},{1,65},{8,16},{9,73},{16,24},{17,81},{24,0},{25,89},{64,72},... | collective-permute-start | bytes 393224 | tf_op jit(solution)/shard_map/ppermute | solution.py:36
  94.9 4.7 %collective-permute-start.23 = (bf16[64,1024]{1,0:T(8,128)(2,1)S(1)}, bf16[64,1024]{1,0:T(8,128)(2,1)S(1)}, u32[]{:S(2)}, u32[]{:S(2)}) collective-permute-start(bf16[64,1024]{1,0:T(8,128)(2,1)S(1)} %get-tuple-element.59), channel_id=1, source_target_pairs={{0,24},{1,193},{8,0},{9,201},{16,8},{17,209},{24,16},{25,217},{64,... | collective-permute-start | bytes 393224 | tf_op jit(solution)/shard_map/ppermute | solution.py:36
  100.3 12.7 %all-to-all-start.1 = ((bf16[8,16,1024]{2,1,0:T(8,128)(2,1)}), bf16[8,16,1024]{2,1,0:T(8,128)(2,1)S(1)}, u32[]{:S(2)}, u32[]{:S(2)}) async-start(bf16[8,16,1024]{2,1,0:T(8,128)(2,1)} %pad_maximum_fusion.5), calls=%async_computation.1 | async-start | bytes 524288 | tf_op jit(solution)/shard_map/all_to_all | solution.py:252
  105.3 48.0 %copy-start.10 = (s32[2,16]{1,0:T(2,128)S(1)}, s32[2,16]{1,0:T(2,128)}, u32[]{:S(2)}) copy-start(s32[2,16]{1,0:T(2,128)} %copy-done.8) | copy-start | bytes 388
  105.3 48.0 %copy-start.13 = (f32[256]{0:T(256)S(1)}, f32[256]{0:T(256)}, u32[]{:S(2)}) copy-start(f32[256]{0:T(256)} %copy-done.11) | copy-start | bytes 3076
  124.9 5.4 %collective-permute-start.30 = (bf16[64,1024]{1,0:T(8,128)(2,1)S(1)}, bf16[64,1024]{1,0:T(8,128)(2,1)S(1)}, u32[]{:S(2)}, u32[]{:S(2)}) collective-permute-start(bf16[64,1024]{1,0:T(8,128)(2,1)S(1)} %get-tuple-element.63), channel_id=1, source_target_pairs={{0,16},{1,129},{8,24},{9,137},{16,0},{17,145},{24,8},{25,153},{64,... | collective-permute-start | bytes 393224 | tf_op jit(solution)/shard_map/ppermute | solution.py:36
  126.5 5.3 %collective-permute-start.31 = (bf16[64,1024]{1,0:T(8,128)(2,1)S(1)}, bf16[64,1024]{1,0:T(8,128)(2,1)S(1)}, u32[]{:S(2)}, u32[]{:S(2)}) collective-permute-start(bf16[64,1024]{1,0:T(8,128)(2,1)S(1)} %get-tuple-element.63), channel_id=1, source_target_pairs={{0,8},{1,65},{8,16},{9,73},{16,24},{17,81},{24,0},{25,89},{64,72},... | collective-permute-start | bytes 393224 | tf_op jit(solution)/shard_map/ppermute | solution.py:36
  128.9 3.8 %collective-permute-start.32 = (bf16[64,1024]{1,0:T(8,128)(2,1)S(1)}, bf16[64,1024]{1,0:T(8,128)(2,1)S(1)}, u32[]{:S(2)}, u32[]{:S(2)}) collective-permute-start(bf16[64,1024]{1,0:T(8,128)(2,1)S(1)} %get-tuple-element.63), channel_id=1, source_target_pairs={{0,24},{1,193},{8,0},{9,201},{16,8},{17,209},{24,16},{25,217},{64,... | collective-permute-start | bytes 393224 | tf_op jit(solution)/shard_map/ppermute | solution.py:36
  132.8 19.2 %collective-permute-start.33 = (bf16[4,64,1024]{2,1,0:T(8,128)(2,1)S(1)}, bf16[4,64,1024]{2,1,0:T(8,128)(2,1)S(1)}, u32[]{:S(2)}, u32[]{:S(2)}) collective-permute-start(bf16[4,64,1024]{2,1,0:T(8,128)(2,1)S(1)} %pad_maximum_fusion.4.refs_0_), channel_id=1, source_target_pairs={{0,128},{1,17},{8,136},{9,25},{16,144},{17,1},{24,152},{25,9},{64,... | collective-permute-start | bytes 1572872 | tf_op jit(solution)/shard_map/ppermute | solution.py:36
  133.1 20.2 %collective-permute-start.34 = (bf16[4,64,1024]{2,1,0:T(8,128)(2,1)S(1)}, bf16[4,64,1024]{2,1,0:T(8,128)(2,1)S(1)}, u32[]{:S(2)}, u32[]{:S(2)}) collective-permute-start(bf16[4,64,1024]{2,1,0:T(8,128)(2,1)S(1)} %pad_maximum_fusion.4.refs_0_), channel_id=1, source_target_pairs={{0,64},{1,9},{8,72},{9,17},{16,80},{17,25},{24,88},{25,1},{64,128}... | collective-permute-start | bytes 1572872 | tf_op jit(solution)/shard_map/ppermute | solution.py:36
  136.0 17.3 %collective-permute-start.35 = (bf16[4,64,1024]{2,1,0:T(8,128)(2,1)S(1)}, bf16[4,64,1024]{2,1,0:T(8,128)(2,1)S(1)}, u32[]{:S(2)}, u32[]{:S(2)}) collective-permute-start(bf16[4,64,1024]{2,1,0:T(8,128)(2,1)S(1)} %pad_maximum_fusion.4.refs_0_), channel_id=1, source_target_pairs={{0,192},{1,25},{8,200},{9,1},{16,208},{17,9},{24,216},{25,17},{64,... | collective-permute-start | bytes 1572872 | tf_op jit(solution)/shard_map/ppermute | solution.py:36
  136.0 5.3 %collective-permute-start.24 = (bf16[64,1024]{1,0:T(8,128)(2,1)S(1)}, bf16[64,1024]{1,0:T(8,128)(2,1)S(1)}, u32[]{:S(2)}, u32[]{:S(2)}) collective-permute-start(bf16[64,1024]{1,0:T(8,128)(2,1)S(1)} %get-tuple-element.62), channel_id=1, source_target_pairs={{0,16},{1,129},{8,24},{9,137},{16,0},{17,145},{24,8},{25,153},{64,... | collective-permute-start | bytes 393224 | tf_op jit(solution)/shard_map/ppermute | solution.py:36
  137.5 6.1 %collective-permute-start.25 = (bf16[64,1024]{1,0:T(8,128)(2,1)S(1)}, bf16[64,1024]{1,0:T(8,128)(2,1)S(1)}, u32[]{:S(2)}, u32[]{:S(2)}) collective-permute-start(bf16[64,1024]{1,0:T(8,128)(2,1)S(1)} %get-tuple-element.62), channel_id=1, source_target_pairs={{0,8},{1,65},{8,16},{9,73},{16,24},{17,81},{24,0},{25,89},{64,72},... | collective-permute-start | bytes 393224 | tf_op jit(solution)/shard_map/ppermute | solution.py:36
  141.3 8.6 %collective-permute-start.26 = (bf16[64,1024]{1,0:T(8,128)(2,1)S(1)}, bf16[64,1024]{1,0:T(8,128)(2,1)S(1)}, u32[]{:S(2)}, u32[]{:S(2)}) collective-permute-start(bf16[64,1024]{1,0:T(8,128)(2,1)S(1)} %get-tuple-element.62), channel_id=1, source_target_pairs={{0,24},{1,193},{8,0},{9,201},{16,8},{17,209},{24,16},{25,217},{64,... | collective-permute-start | bytes 393224 | tf_op jit(solution)/shard_map/ppermute | solution.py:36
  150.0 21.6 %copy-start.3 = (bf16[256,4096]{1,0:T(8,128)(2,1)S(1)}, bf16[256,4096]{1,0:T(8,128)(2,1)}, u32[]{:S(2)}) copy-start(bf16[256,4096]{1,0:T(8,128)(2,1)} %copy-done.2) | copy-start | bytes 6291460
  150.0 23.5 %collective-permute-start.27 = (bf16[4,64,1024]{2,1,0:T(8,128)(2,1)S(1)}, bf16[4,64,1024]{2,1,0:T(8,128)(2,1)S(1)}, u32[]{:S(2)}, u32[]{:S(2)}) collective-permute-start(bf16[4,64,1024]{2,1,0:T(8,128)(2,1)S(1)} %pad_maximum_fusion.3.refs_0_), channel_id=1, source_target_pairs={{0,128},{1,17},{8,136},{9,25},{16,144},{17,1},{24,152},{25,9},{64,... | collective-permute-start | bytes 1572872 | tf_op jit(solution)/shard_map/ppermute | solution.py:36
  150.1 23.4 %collective-permute-start.28 = (bf16[4,64,1024]{2,1,0:T(8,128)(2,1)S(1)}, bf16[4,64,1024]{2,1,0:T(8,128)(2,1)S(1)}, u32[]{:S(2)}, u32[]{:S(2)}) collective-permute-start(bf16[4,64,1024]{2,1,0:T(8,128)(2,1)S(1)} %pad_maximum_fusion.3.refs_0_), channel_id=1, source_target_pairs={{0,64},{1,9},{8,72},{9,17},{16,80},{17,25},{24,88},{25,1},{64,128}... | collective-permute-start | bytes 1572872 | tf_op jit(solution)/shard_map/ppermute | solution.py:36
  152.0 21.6 %collective-permute-start.29 = (bf16[4,64,1024]{2,1,0:T(8,128)(2,1)S(1)}, bf16[4,64,1024]{2,1,0:T(8,128)(2,1)S(1)}, u32[]{:S(2)}, u32[]{:S(2)}) collective-permute-start(bf16[4,64,1024]{2,1,0:T(8,128)(2,1)S(1)} %pad_maximum_fusion.3.refs_0_), channel_id=1, source_target_pairs={{0,192},{1,25},{8,200},{9,1},{16,208},{17,9},{24,216},{25,17},{64,... | collective-permute-start | bytes 1572872 | tf_op jit(solution)/shard_map/ppermute | solution.py:36
  154.8 16.8 %collective-permute-start.36 = (f32[256,256]{1,0:T(8,128)S(1)}, f32[256,256]{1,0:T(8,128)S(1)}, u32[]{:S(2)}, u32[]{:S(2)}) collective-permute-start(f32[256,256]{1,0:T(8,128)S(1)} %get-tuple-element.38.own), channel_id=1, source_target_pairs={{0,1},{1,0},{2,3},{3,2},{4,5},{5,4},{6,7},{7,6},{8,9},{9,8},{10,11... | collective-permute-start | bytes 786440 | tf_op jit(solution)/shard_map/ppermute | solution.py:40
  175.1 8.1 %collective-permute-start.37 = (f32[256,256]{1,0:T(8,128)S(1)}, f32[256,256]{1,0:T(8,128)S(1)}, u32[]{:S(2)}, u32[]{:S(2)}) collective-permute-start(f32[256,256]{1,0:T(8,128)S(1)} %get-tuple-element.43.own), channel_id=1, source_target_pairs={{0,1},{1,0},{2,3},{3,2},{4,5},{5,4},{6,7},{7,6},{8,9},{9,8},{10,11... | collective-permute-start | bytes 786440 | tf_op jit(solution)/shard_map/ppermute | solution.py:40
  185.1 3.9 %collective-permute-start.38 = (bf16[128,4096]{1,0:T(8,128)(2,1)S(1)}, bf16[128,4096]{1,0:T(8,128)(2,1)S(1)}, u32[]{:S(2)}, u32[]{:S(2)}) collective-permute-start(bf16[128,4096]{1,0:T(8,128)(2,1)S(1)} %get-tuple-element.48), channel_id=1, source_target_pairs={{0,1},{1,0},{2,3},{3,2},{4,5},{5,4},{6,7},{7,6},{8,9},{9,8},{10,11... | collective-permute-start | bytes 3145736 | tf_op jit(solution)/shard_map/ppermute | solution.py:40
  (13 other events, 64.0 us)

commit v4 on v3

--- a/solution.py
+++ b/solution.py
@@ -17,7 +17,7 @@
 Z = ("zh", "zl")
 VMEM = pl.BlockSpec(memory_space=pltpu.VMEM)
 SMEM = pl.BlockSpec(memory_space=pltpu.SMEM)
-PARAMS = pltpu.CompilerParams(vmem_limit_bytes=16 * 1024 * 1024)
+PARAMS = pltpu.CompilerParams(vmem_limit_bytes=8 * 1024 * 1024)
 
 
 def plane_pairs(by, last):
@@ -196,7 +196,7 @@
             out_specs=(there,) * 3,
         ),
         input_output_aliases={4 + i: i for i in range(len(outs))},
-        compiler_params=pltpu.CompilerParams(vmem_limit_bytes=32 * 1024 * 1024),
+        compiler_params=PARAMS,
         cost_estimate=pl.CostEstimate(flops=20 * gradient.size, bytes_accessed=14 * gradient.size, transcendentals=0),
     )(at, gradient, first_moment, second_moment, *outs)
 
@@ -238,23 +238,25 @@
         total = blocks[0].astype(F32)
         for slot in (1, 2, 3):
             total = total + shift(blocks[slot], ORDER[slot], True).astype(F32)
-        total = total.astype(BF16)
-        strip = total[0].astype(F32)
-        for by in ORDER[1:]:
-            strip = strip + shift(total[ORDER.index(SIDE - by)], by, False).astype(F32)
-        return strip.astype(BF16).reshape(8, thin, part)
+        return total.astype(BF16)
+
+    def fan(gathered):
+        return [spread(jnp.stack([g[k * split : (k + 1) * split] for g in gathered]), True) for k in chunks]
 
     chunks = range(CHUNKS)
-    pieces = [spread(jnp.stack([g[k * split : (k + 1) * split] for g in gathered]), True) for k in chunks]
+    pieces = fan(gathered)
     ahead = [project(gather_place, pair, decoder, lift, pieces[k], True) for k in chunks]
     made = [recon(send_place, ahead[k][1], swap(ahead[k][1]), pair) for k in chunks]
-    parts = jnp.concatenate([reduce(made[k][2:]) for k in chunks], 1)
-    recon_sum = jnp.sum(lax.all_to_all(parts, Z, 0, 0, tiled=True).astype(F32), 0)
-    here = [lax.dynamic_slice_in_dim(source, k * split + z * thin, thin, 0) for k in chunks]
-    error = (recon_sum + share - jnp.concatenate(here, 0).astype(F32)).astype(BF16)
+    blocks = jnp.concatenate([reduce(made[k][2:]) for k in chunks], 1)
+    strip = blocks[0].astype(F32)
+    for by in ORDER[1:]:
+        strip = strip + shift(blocks[ORDER.index(SIDE - by)], by, False).astype(F32)
+    parts = lax.all_to_all(strip.astype(BF16).reshape(8, CHUNKS * thin, part), Z, 0, 0, tiled=True)
+    recon_sum = jnp.sum(parts.astype(F32), 0)
+    here = lax.dynamic_slice_in_dim(source, z * CHUNKS * thin, CHUNKS * thin, 0).astype(F32)
+    error = (recon_sum + share - here).astype(BF16)
     error = lax.all_to_all(jnp.broadcast_to(error, (8,) + error.shape), Z, 0, 0, tiled=True)
-    error = [error[:, k * thin : (k + 1) * thin].reshape(split, part) for k in chunks]
-    pieces = [spread(jnp.stack(spread(error[k], False)), True) for k in chunks]
+    pieces = fan(spread(error.reshape(-1, part), False))
     total = None
     for k in chunks:
         after = () if total is None else (total,)

time: 193 us -> 184 us (0.953); the launches traced: 192 us -> 181 us
  starting transfers between devices: 89.5 us -> 74.8 us
  waiting for transfers between devices: 54.6 us -> 58 us
    ppermute x6, starting transfers between devices: 27.5 us -> 15.1 us  [swap(): return lax.ppermute(value, 'c', [(0, 1), (1, 0)])]
    ppermute x33 -> x27, waiting for transfers between devices: 35.9 us -> 39.7 us  [shift(): return lax.ppermute(value, PLANE, plane_pairs(by, last))]
    ppermute x33 -> x27, starting transfers between devices: 48.6 us -> 46.3 us  [shift(): return lax.ppermute(value, PLANE, plane_pairs(by, last))]
  transfers between devices with their start and end apart: 41 -> 35, of which waited for: 21 -> 21; matrix products, arithmetic and copies ran while one was open for 4% -> 3% of each run, Pallas kernels for 8% -> 8%
where the time goes in v4:
time: 184 us; the launch traced here: 181 us
  starting transfers between devices  74.8 us (41%)
  waiting for transfers between devices  58 us (32%)
  Pallas kernels  21.3 us (12%)
  blocking collectives  11.9 us (6%)
  local copies, waits for them, and re-layouts  9.88 us (5%)
  other arithmetic  4.24 us (2%)
    ppermute x27, starting transfers between devices, shift(): return lax.ppermute(value, PLANE, plane_pairs(by, last))  46.3 us
    ppermute x27, waiting for transfers between devices, shift(): return lax.ppermute(value, PLANE, plane_pairs(by, last))  39.7 us
    ppermute x6, starting transfers between devices, swap(): return lax.ppermute(value, 'c', [(0, 1), (1, 0)])  15.1 us
    all_to_all x1, blocking collectives, body(): lax.all_to_all(jnp.broadcast_to(error, (8,) + error.shape), Z, 0, 0, tile...  11.9 us
    all_to_all x1, starting transfers between devices, body(): lax.all_to_all(block.reshape((8,) + own_columns[0].shape), ('zh', 'c'), 0...  9.97 us
    all_to_all x1, waiting for transfers between devices, body(): lax.all_to_all(strip.astype(BF16).reshape(8, CHUNKS * thin, part), Z, 0,...  8.51 us
    pallas_call x4, Pallas kernels, project(): pl.pallas_call(functools.partial(project_kernel, centre=centre), out_shap...  7.22 us
    all_to_all x1, waiting for transfers between devices, body(): lax.all_to_all(block.reshape((8,) + own_columns[0].shape), ('zh', 'c'), 0...  7.07 us
  transfers between devices with their start and end apart: 35, of which 21 were waited for; matrix products, arithmetic and copies ran while one was open for 3% of the time, Pallas kernels for 8%

profile of v4, /device:TPU:1, one launch (start us, length us, event | category | flops | bytes accessed | tf_op | source)
XLA Modules:
  0.0 181.2 jit_solution(2143970988453785834)
XLA Ops:
  2.2 10.0 %all-to-all-start = ((bf16[8,16,1024]{2,1,0:T(8,128)(2,1)}), bf16[8,16,1024]{2,1,0:T(8,128)(2,1)S(1)}, u32[]{:S(2)}, u32[]{:S(2)}) async-start(bf16[8,16,1024]{2,1,0:T(8,128)(2,1)} %bitcast.5), calls=%async_computation | async-start | bytes 524288 | tf_op jit(solution)/shard_map/all_to_all | solution.py:223
  12.2 2.7 %constant_dynamic-slice_fusion.1 = (bf16[128,4096]{1,0:T(8,128)(2,1)}, bf16[128,4096]{1,0:T(8,128)(2,1)S(1)}) fusion(bf16[128,8192]{1,0:T(8,128)(2,1)} %param.9, s32[]{:T(128)S(6)} %select_n.113, s32[]{:T(128)S(6)} %select_n.114), kind=kLoop, calls=%fused_computation.52 | loop fusion | bytes 4194312 | tf_op jit(solution)/shard_map/dynamic_slice | solution.py:230
  15.2 7.1 %all-to-all-done = bf16[8,16,1024]{2,1,0:T(8,128)(2,1)S(1)} async-done(((bf16[8,16,1024]{2,1,0:T(8,128)(2,1)}), bf16[8,16,1024]{2,1,0:T(8,128)(2,1)S(1)}, u32[]{:S(2)}, u32[]{:S(2)}) %all-to-all-start) | async-done | bytes 262176 | tf_op jit(solution)/shard_map/all_to_all | solution.py:223
  22.2 2.7 %collective-permute-start.1 = (bf16[128,1024]{1,0:T(8,128)(2,1)S(1)}, bf16[128,1024]{1,0:T(8,128)(2,1)S(1)}, u32[]{:S(2)}, u32[]{:S(2)}) collective-permute-start(bf16[128,1024]{1,0:T(8,128)(2,1)S(1)} %bitcast.58), channel_id=1, source_target_pairs={{0,16},{1,129},{8,24},{9,137},{16,0},{17,145},{24,8},{25,153},{64,... | collective-permute-start | bytes 786440 | tf_op jit(solution)/shard_map/ppermute | solution.py:36
  25.5 2.4 %collective-permute-start.3 = (bf16[128,1024]{1,0:T(8,128)(2,1)S(1)}, bf16[128,1024]{1,0:T(8,128)(2,1)S(1)}, u32[]{:S(2)}, u32[]{:S(2)}) collective-permute-start(bf16[128,1024]{1,0:T(8,128)(2,1)S(1)} %bitcast.60), channel_id=1, source_target_pairs={{0,24},{1,193},{8,0},{9,201},{16,8},{17,209},{24,16},{25,217},{64,... | collective-permute-start | bytes 786440 | tf_op jit(solution)/shard_map/ppermute | solution.py:36
  29.0 3.1 %collective-permute-done.2 = bf16[128,1024]{1,0:T(8,128)(2,1)S(1)} collective-permute-done((bf16[128,1024]{1,0:T(8,128)(2,1)S(1)}, bf16[128,1024]{1,0:T(8,128)(2,1)S(1)}, u32[]{:S(2)}, u32[]{:S(2)}) %collective-permute-start.2) | collective-permute-done | bytes 262176 | tf_op jit(solution)/shard_map/ppermute | solution.py:36
  32.2 3.0 %collective-permute-start.11 = (bf16[4,64,1024]{2,1,0:T(8,128)(2,1)S(1)}, bf16[4,64,1024]{2,1,0:T(8,128)(2,1)S(1)}, u32[]{:S(2)}, u32[]{:S(2)}) collective-permute-start(bf16[4,64,1024]{2,1,0:T(8,128)(2,1)S(1)} %pad_maximum_fusion.2.refs_0_), channel_id=1, source_target_pairs={{0,128},{1,17},{8,136},{9,25},{16,144},{17,1},{24,152},{25,9},{64,... | collective-permute-start | bytes 1572872 | tf_op jit(solution)/shard_map/ppermute | solution.py:36
  35.6 2.3 %collective-permute-start.13 = (bf16[4,64,1024]{2,1,0:T(8,128)(2,1)S(1)}, bf16[4,64,1024]{2,1,0:T(8,128)(2,1)S(1)}, u32[]{:S(2)}, u32[]{:S(2)}) collective-permute-start(bf16[4,64,1024]{2,1,0:T(8,128)(2,1)S(1)} %pad_maximum_fusion.2.refs_0_), channel_id=1, source_target_pairs={{0,192},{1,25},{8,200},{9,1},{16,208},{17,9},{24,216},{25,17},{64,... | collective-permute-start | bytes 1572872 | tf_op jit(solution)/shard_map/ppermute | solution.py:36
  38.7 1.4 pad_maximum_fusion.weight
  40.1 2.1 %collective-permute-done.11.refs_1_ = bf16[4,64,1024]{2,1,0:T(8,128)(2,1)S(1)} collective-permute-done((bf16[4,64,1024]{2,1,0:T(8,128)(2,1)S(1)}, bf16[4,64,1024]{2,1,0:T(8,128)(2,1)S(1)}, u32[]{:S(2)}, u32[]{:S(2)}) %collective-permute-start.11) | collective-permute-done | bytes 524320 | tf_op jit(solution)/shard_map/ppermute | solution.py:36
  42.2 2.8 %collective-permute-start.6 = (bf16[4,64,1024]{2,1,0:T(8,128)(2,1)S(1)}, bf16[4,64,1024]{2,1,0:T(8,128)(2,1)}, u32[]{:S(2)}, u32[]{:S(2)}) collective-permute-start(bf16[4,64,1024]{2,1,0:T(8,128)(2,1)S(1)} %pad_maximum_fusion.1.refs_0_), channel_id=1, source_target_pairs={{0,192},{1,25},{8,200},{9,1},{16,208},{17,9},{24,216},{25,17},{64,... | collective-permute-start | bytes 1572872 | tf_op jit(solution)/shard_map/ppermute | solution.py:36
  44.9 2.8 %collective-permute-done.12.refs_2_ = bf16[4,64,1024]{2,1,0:T(8,128)(2,1)S(1)} collective-permute-done((bf16[4,64,1024]{2,1,0:T(8,128)(2,1)S(1)}, bf16[4,64,1024]{2,1,0:T(8,128)(2,1)S(1)}, u32[]{:S(2)}, u32[]{:S(2)}) %collective-permute-start.12) | collective-permute-done | bytes 524320 | tf_op jit(solution)/shard_map/ppermute | solution.py:36
  48.2 1.7 shard_map.96
  49.9 1.3 copy-done.2
  51.2 4.1 %collective-permute-start.14 = (f32[256,256]{1,0:T(8,128)S(1)}, f32[256,256]{1,0:T(8,128)}, u32[]{:S(2)}, u32[]{:S(2)}) collective-permute-start(f32[256,256]{1,0:T(8,128)S(1)} %get-tuple-element.33.own), channel_id=1, source_target_pairs={{0,1},{1,0},{2,3},{3,2},{4,5},{5,4},{6,7},{7,6},{8,9},{9,8},{10,11... | collective-permute-start | bytes 786440 | tf_op jit(solution)/shard_map/ppermute | solution.py:40
  57.5 2.0 %shard_map.97 = (f32[256,256]{1,0:T(8,128)S(1)}, bf16[256,256]{1,0:T(8,128)(2,1)S(1)}, bf16[4,64,1024]{2,1,0:T(8,128)(2,1)S(1)}, bf16[4,64,1024]{2,1,0:T(8,128)(...) custom-call(s32[2,16]{1,0:T(2,128)S(1)} %pad_add_fusion.1.place, f32[256,256]{1,0:T(8,128)S(1)} %copy-done.7, ...), custom_call_target="tpu_custom_call" | custom-call | flops 536870912 | bytes 4194304 | tf_op jit(solution)/shard_map/pallas_call | solution.py:120
  59.5 2.1 %collective-permute-start.15 = (bf16[4,64,1024]{2,1,0:T(8,128)(2,1)S(1)}, bf16[4,64,1024]{2,1,0:T(8,128)(2,1)S(1)}, u32[]{:S(2)}, u32[]{:S(2)}) collective-permute-start(bf16[4,64,1024]{2,1,0:T(8,128)(2,1)S(1)} %get-tuple-element.35), channel_id=1, source_target_pairs={{0,128},{1,17},{8,136},{9,25},{16,144},{17,1},{24,152},{25,9},{64,... | collective-permute-start | bytes 1572872 | tf_op jit(solution)/shard_map/ppermute | solution.py:36
  61.6 2.4 %shard_map.94 = (bf16[256,4096]{1,0:T(8,128)(2,1)S(1)}, f32[256,256]{1,0:T(8,128)S(1)}) custom-call(s32[2,16]{1,0:T(2,128)S(1)} %copy-done.9, bf16[256,4096]{1,0:T(8,128)(2,1)S(1)} %pad_maximum_fusion.weight, f32[1,4096]{1,0:T(1,128)S(1)} %bitcast.51, f32[1,256]{1,0:T(1,128)S(1)} %bitcast.55, bf16[4,64,1024]{2,1,0:T(8,128)(2,1)S(1)} %pad_maximum_fusion.1.refs_0_, ...), custom_call_target="tpu_custom_call" | custom-call | flops 536870912 | bytes 4194304 | tf_op jit(solution)/shard_map/pallas_call | solution.py:76
  65.3 2.0 %collective-permute-start.7 = (f32[256,256]{1,0:T(8,128)S(1)}, f32[256,256]{1,0:T(8,128)S(1)}, u32[]{:S(2)}, u32[]{:S(2)}) collective-permute-start(f32[256,256]{1,0:T(8,128)S(1)} %get-tuple-element.28.own), channel_id=1, source_target_pairs={{0,1},{1,0},{2,3},{3,2},{4,5},{5,4},{6,7},{7,6},{8,9},{9,8},{10,11... | collective-permute-start | bytes 786440 | tf_op jit(solution)/shard_map/ppermute | solution.py:40
  68.5 1.7 collective-permute-start.17
  70.2 1.6 shard_map.95
  71.8 1.5 collective-permute-start.10
  74.0 3.1 %collective-permute-done.16 = bf16[4,64,1024]{2,1,0:T(8,128)(2,1)S(1)} collective-permute-done((bf16[4,64,1024]{2,1,0:T(8,128)(2,1)S(1)}, bf16[4,64,1024]{2,1,0:T(8,128)(2,1)S(1)}, u32[]{:S(2)}, u32[]{:S(2)}) %collective-permute-start.16) | collective-permute-done | bytes 524320 | tf_op jit(solution)/shard_map/ppermute | solution.py:36
  77.5 10.1 %collective-permute-done.10 = bf16[4,64,1024]{2,1,0:T(8,128)(2,1)S(1)} collective-permute-done((bf16[4,64,1024]{2,1,0:T(8,128)(2,1)S(1)}, bf16[4,64,1024]{2,1,0:T(8,128)(2,1)S(1)}, u32[]{:S(2)}, u32[]{:S(2)}) %collective-permute-start.10) | collective-permute-done | bytes 524320 | tf_op jit(solution)/shard_map/ppermute | solution.py:36
  89.0 1.5 collective-permute-start.18
  90.5 1.5 collective-permute-start.19
  93.2 2.9 %collective-permute-done.18 = bf16[128,1024]{1,0:T(8,128)(2,1)S(1)} collective-permute-done((bf16[128,1024]{1,0:T(8,128)(2,1)S(1)}, bf16[128,1024]{1,0:T(8,128)(2,1)S(1)}, u32[]{:S(2)}, u32[]{:S(2)}) %collective-permute-start.18) | collective-permute-done | bytes 262176 | tf_op jit(solution)/shard_map/ppermute | solution.py:36
  96.1 2.8 %collective-permute-done.19 = bf16[128,1024]{1,0:T(8,128)(2,1)S(1)} collective-permute-done((bf16[128,1024]{1,0:T(8,128)(2,1)S(1)}, bf16[128,1024]{1,0:T(8,128)(2,1)S(1)}, u32[]{:S(2)}, u32[]{:S(2)}) %collective-permute-start.19) | collective-permute-done | bytes 262176 | tf_op jit(solution)/shard_map/ppermute | solution.py:36
  99.8 3.4 %all-to-all-start.1 = ((bf16[8,16,1024]{2,1,0:T(8,128)(2,1)}), bf16[8,16,1024]{2,1,0:T(8,128)(2,1)S(1)}, u32[]{:S(2)}, u32[]{:S(2)}) async-start(bf16[8,16,1024]{2,1,0:T(8,128)(2,1)} %bitcast.19), calls=%async_computation.1 | async-start | bytes 524288 | tf_op jit(solution)/shard_map/all_to_all | solution.py:254
  104.0 8.5 %all-to-all-done.1 = bf16[8,16,1024]{2,1,0:T(8,128)(2,1)S(1)} async-done(((bf16[8,16,1024]{2,1,0:T(8,128)(2,1)}), bf16[8,16,1024]{2,1,0:T(8,128)(2,1)S(1)}, u32[]{:S(2)}, u32[]{:S(2)}) %all-to-all-start.1) | async-done | bytes 262176 | tf_op jit(solution)/shard_map/all_to_all | solution.py:254
  113.3 11.9 %all_to_all.15 = bf16[8,16,1024]{2,1,0:T(8,128)(2,1)S(1)} all-to-all(bf16[8,16,1024]{2,1,0:T(8,128)(2,1)S(1)} %broadcast_in_dim.28), channel_id=1, replica_groups=mesh['x'=4,'zl'=2,'y'=4,'zh'=4,'c'=2] {'zh','zl'}, dimensions={0} | all-to-all | bytes 524288 | tf_op jit(solution)/shard_map/all_to_all | solution.py:258
  125.2 2.4 %collective-permute-start.21 = (bf16[128,1024]{1,0:T(8,128)(2,1)S(1)}, bf16[128,1024]{1,0:T(8,128)(2,1)S(1)}, u32[]{:S(2)}, u32[]{:S(2)}) collective-permute-start(bf16[128,1024]{1,0:T(8,128)(2,1)S(1)} %bitcast.62), channel_id=1, source_target_pairs={{0,16},{1,129},{8,24},{9,137},{16,0},{17,145},{24,8},{25,153},{64,... | collective-permute-start | bytes 786440 | tf_op jit(solution)/shard_map/ppermute | solution.py:36
  128.1 2.2 %collective-permute-start.23 = (bf16[128,1024]{1,0:T(8,128)(2,1)S(1)}, bf16[128,1024]{1,0:T(8,128)(2,1)S(1)}, u32[]{:S(2)}, u32[]{:S(2)}) collective-permute-start(bf16[128,1024]{1,0:T(8,128)(2,1)S(1)} %bitcast.64), channel_id=1, source_target_pairs={{0,24},{1,193},{8,0},{9,201},{16,8},{17,209},{24,16},{25,217},{64,... | collective-permute-start | bytes 786440 | tf_op jit(solution)/shard_map/ppermute | solution.py:36
  130.3 1.7 collective-permute-done.21
  132.1 3.0 %collective-permute-done.22 = bf16[128,1024]{1,0:T(8,128)(2,1)S(1)} collective-permute-done((bf16[128,1024]{1,0:T(8,128)(2,1)S(1)}, bf16[128,1024]{1,0:T(8,128)(2,1)S(1)}, u32[]{:S(2)}, u32[]{:S(2)}) %collective-permute-start.22) | collective-permute-done | bytes 262176 | tf_op jit(solution)/shard_map/ppermute | solution.py:36
  135.8 5.5 %collective-permute-start.28 = (bf16[4,64,1024]{2,1,0:T(8,128)(2,1)S(1)}, bf16[4,64,1024]{2,1,0:T(8,128)(2,1)S(1)}, u32[]{:S(2)}, u32[]{:S(2)}) collective-permute-start(bf16[4,64,1024]{2,1,0:T(8,128)(2,1)S(1)} %pad_maximum_fusion.4.refs_0_), channel_id=1, source_target_pairs={{0,64},{1,9},{8,72},{9,17},{16,80},{17,25},{24,88},{25,1},{64,128}... | collective-permute-start | bytes 1572872 | tf_op jit(solution)/shard_map/ppermute | solution.py:36
  141.3 2.3 %collective-permute-start.29 = (bf16[4,64,1024]{2,1,0:T(8,128)(2,1)S(1)}, bf16[4,64,1024]{2,1,0:T(8,128)(2,1)S(1)}, u32[]{:S(2)}, u32[]{:S(2)}) collective-permute-start(bf16[4,64,1024]{2,1,0:T(8,128)(2,1)S(1)} %pad_maximum_fusion.4.refs_0_), channel_id=1, source_target_pairs={{0,192},{1,25},{8,200},{9,1},{16,208},{17,9},{24,216},{25,17},{64,... | collective-permute-start | bytes 1572872 | tf_op jit(solution)/shard_map/ppermute | solution.py:36
  145.8 4.7 %collective-permute-start.26 = (bf16[4,64,1024]{2,1,0:T(8,128)(2,1)S(1)}, bf16[4,64,1024]{2,1,0:T(8,128)(2,1)S(1)}, u32[]{:S(2)}, u32[]{:S(2)}) collective-permute-start(bf16[4,64,1024]{2,1,0:T(8,128)(2,1)S(1)} %pad_maximum_fusion.3.refs_0_), channel_id=1, source_target_pairs={{0,192},{1,25},{8,200},{9,1},{16,208},{17,9},{24,216},{25,17},{64,... | collective-permute-start | bytes 1572872 | tf_op jit(solution)/shard_map/ppermute | solution.py:36
  151.5 2.2 %collective-permute-done.29.refs_3_ = bf16[4,64,1024]{2,1,0:T(8,128)(2,1)S(1)} collective-permute-done((bf16[4,64,1024]{2,1,0:T(8,128)(2,1)S(1)}, bf16[4,64,1024]{2,1,0:T(8,128)(2,1)S(1)}, u32[]{:S(2)}, u32[]{:S(2)}) %collective-permute-start.29) | collective-permute-done | bytes 524320 | tf_op jit(solution)/shard_map/ppermute | solution.py:36
  153.7 1.6 shard_map.98
  155.3 4.3 %collective-permute-start.30 = (f32[256,256]{1,0:T(8,128)S(1)}, f32[256,256]{1,0:T(8,128)S(1)}, u32[]{:S(2)}, u32[]{:S(2)}) collective-permute-start(f32[256,256]{1,0:T(8,128)S(1)} %get-tuple-element.38.own), channel_id=1, source_target_pairs={{0,1},{1,0},{2,3},{3,2},{4,5},{5,4},{6,7},{7,6},{8,9},{9,8},{10,11... | collective-permute-start | bytes 786440 | tf_op jit(solution)/shard_map/ppermute | solution.py:40
  160.8 1.9 %shard_map.99.refs_4_.refs_0_ = f32[256,4096]{1,0:T(8,128)S(1)} custom-call(f32[256,256]{1,0:T(8,128)S(1)} %get-tuple-element.38.own, f32[256,256]{1,0:T(8,128)S(1)} %collective-permute-done.30.other, f32[256,256]{1,0:T(8,128)S(1)} %get-tuple-element.39.preact, bf16[256,256]{1,0:T(8,128)(2,1)S(1)} %get-tuple-element.40.flat, ...), custom_call_target="tpu_custom_call" | custom-call | flops 1073741824 | bytes 12582912 | tf_op jit(solution)/shard_map/pallas_call | solution.py:161
  162.8 2.2 %collective-permute-done.26.refs_3_ = bf16[4,64,1024]{2,1,0:T(8,128)(2,1)S(1)} collective-permute-done((bf16[4,64,1024]{2,1,0:T(8,128)(2,1)S(1)}, bf16[4,64,1024]{2,1,0:T(8,128)(2,1)S(1)}, u32[]{:S(2)}, u32[]{:S(2)}) %collective-permute-start.26) | collective-permute-done | bytes 524320 | tf_op jit(solution)/shard_map/ppermute | solution.py:36
  165.0 1.5 shard_map.100
  166.6 4.3 %collective-permute-start.31 = (f32[256,256]{1,0:T(8,128)S(1)}, f32[256,256]{1,0:T(8,128)S(1)}, u32[]{:S(2)}, u32[]{:S(2)}) collective-permute-start(f32[256,256]{1,0:T(8,128)S(1)} %get-tuple-element.43.own), channel_id=1, source_target_pairs={{0,1},{1,0},{2,3},{3,2},{4,5},{5,4},{6,7},{7,6},{8,9},{9,8},{10,11... | collective-permute-start | bytes 786440 | tf_op jit(solution)/shard_map/ppermute | solution.py:40
  172.0 1.9 %shard_map.101 = (f32[128,4096]{1,0:T(8,128)S(1)}, bf16[128,4096]{1,0:T(8,128)(2,1)S(1)}) custom-call(f32[256,256]{1,0:T(8,128)S(1)} %get-tuple-element.43.own, f32[256,256]{1,0:T(8,128)S(1)} %collective-permute-done.31.other, f32[256,256]{1,0:T(8,128)S(1)} %get-tuple-element.44.preact, bf16[256,256]{1,0:T(8,128)(2,1)S(1)} %get-tuple-element.45.flat, ...), custom_call_target="tpu_custom_call" | custom-call | flops 1073741824 | bytes 12582912 | tf_op jit(solution)/shard_map/pallas_call | solution.py:161
  174.4 3.4 %shard_map.102 = (bf16[128,8192]{1,0:T(8,128)(2,1)}, bf16[128,8192]{1,0:T(8,128)(2,1)}, bf16[128,8192]{1,0:T(8,128)(2,1)}) custom-call(s32[1]{0:T(128)} %bitcast.at, f32[128,4096]{1,0:T(8,128)S(1)} %get-tuple-element.49.gradient_ref, bf16[128,8192]{1,0:T(8,128)(2,1)S(1)} %copy-done, bf16[128,8192]{1,0:T(8,128)(2,1)S(1)} %copy-done.1), custom_call_target="tpu_custom_call" | custom-call | flops 10485760 | bytes 7340032 | tf_op jit(solution)/shard_map/pallas_call | solution.py:189
  177.8 3.4 %shard_map.103 = (bf16[128,8192]{1,0:T(8,128)(2,1)}, bf16[128,8192]{1,0:T(8,128)(2,1)}, bf16[128,8192]{1,0:T(8,128)(2,1)}) custom-call(s32[1]{0:T(128)S(6)} %sub.21.at, bf16[128,4096]{1,0:T(8,128)(2,1)S(1)} %collective-permute-done.32.gradient_ref, bf16[128,8192]{1,0:T(8,128)(2,1)S(1)} %copy-done, ...), custom_call_target="tpu_custom_call", output_to_operand_aliasing={{0}: (4, {}), {1}: (5, {}), {2}: (6, {})} | custom-call | flops 10485760 | bytes 7340032 | tf_op jit(solution)/shard_map/pallas_call | solution.py:189
  (108 shorter events, 23.3 us)
Async XLA Ops:
  2.2 20.1 %all-to-all-start = ((bf16[8,16,1024]{2,1,0:T(8,128)(2,1)}), bf16[8,16,1024]{2,1,0:T(8,128)(2,1)S(1)}, u32[]{:S(2)}, u32[]{:S(2)}) async-start(bf16[8,16,1024]{2,1,0:T(8,128)(2,1)} %bitcast.5), calls=%async_computation | async-start | bytes 524288 | tf_op jit(solution)/shard_map/all_to_all | solution.py:223
  12.1 2.8 %copy-start.18 = (s32[4]{0:T(128)S(1)}, s32[4]{0:T(128)}, u32[]{:S(2)}) copy-start(s32[4]{0:T(128)} %constant.82) | copy-start | bytes 52
  12.1 12.9 %copy-start.16 = (f32[8192]{0:T(1024)S(1)}, f32[8192]{0:T(1024)}, u32[]{:S(2)}) copy-start(f32[8192]{0:T(1024)} %param.8) | copy-start | bytes 98308
  12.1 12.9 %copy-start.19 = (f32[128]{0:T(128)S(1)}, f32[128]{0:T(128)}, u32[]{:S(2)}) copy-start(f32[128]{0:T(128)} %param.10) | copy-start | bytes 1540
  14.9 23.2 %collective-permute-start = (bf16[128,4096]{1,0:T(8,128)(2,1)S(1)}, bf16[128,4096]{1,0:T(8,128)(2,1)}, u32[]{:S(2)}, u32[]{:S(2)}) collective-permute-start(bf16[128,4096]{1,0:T(8,128)(2,1)S(1)} %get-tuple-element.54), channel_id=1, source_target_pairs={{0,1},{1,0},{2,3},{3,2},{4,5},{5,4},{6,7},{7,6},{8,9},{9,8},{10,11... | collective-permute-start | bytes 3145736 | tf_op jit(solution)/shard_map/ppermute | solution.py:40
  22.2 15.8 %copy-start.15 = (bf16[8,16,1024]{2,1,0:T(8,128)(2,1)}, bf16[8,16,1024]{2,1,0:T(8,128)(2,1)S(1)}, u32[]{:S(2)}) copy-start(bf16[8,16,1024]{2,1,0:T(8,128)(2,1)S(1)} %all-to-all-done) | copy-start | bytes 786436
  22.2 6.7 %collective-permute-start.1 = (bf16[128,1024]{1,0:T(8,128)(2,1)S(1)}, bf16[128,1024]{1,0:T(8,128)(2,1)S(1)}, u32[]{:S(2)}, u32[]{:S(2)}) collective-permute-start(bf16[128,1024]{1,0:T(8,128)(2,1)S(1)} %bitcast.58), channel_id=1, source_target_pairs={{0,16},{1,129},{8,24},{9,137},{16,0},{17,145},{24,8},{25,153},{64,... | collective-permute-start | bytes 786440 | tf_op jit(solution)/shard_map/ppermute | solution.py:36
  25.0 23.2 %copy-start.8 = (s32[2,16]{1,0:T(2,128)}, s32[2,16]{1,0:T(2,128)S(1)}, u32[]{:S(2)}) copy-start(s32[2,16]{1,0:T(2,128)S(1)} %pad_add_fusion.place) | copy-start | bytes 388
  25.0 23.1 %copy-start.11 = (f32[256]{0:T(256)}, f32[256]{0:T(256)S(1)}, u32[]{:S(2)}) copy-start(f32[256]{0:T(256)S(1)} %concatenate.10) | copy-start | bytes 3076
  25.1 13.6 %copy-start.14 = (bf16[128,4096]{1,0:T(8,128)(2,1)S(1)}, bf16[128,4096]{1,0:T(8,128)(2,1)}, u32[]{:S(2)}) copy-start(bf16[128,4096]{1,0:T(8,128)(2,1)} %get-tuple-element.53) | copy-start | bytes 3145732
  25.1 7.0 %collective-permute-start.2 = (bf16[128,1024]{1,0:T(8,128)(2,1)S(1)}, bf16[128,1024]{1,0:T(8,128)(2,1)S(1)}, u32[]{:S(2)}, u32[]{:S(2)}) collective-permute-start(bf16[128,1024]{1,0:T(8,128)(2,1)S(1)} %bitcast.59), channel_id=1, source_target_pairs={{0,8},{1,65},{8,16},{9,73},{16,24},{17,81},{24,0},{25,89},{64,72},... | collective-permute-start | bytes 786440 | tf_op jit(solution)/shard_map/ppermute | solution.py:36
  25.5 6.6 %collective-permute-start.3 = (bf16[128,1024]{1,0:T(8,128)(2,1)S(1)}, bf16[128,1024]{1,0:T(8,128)(2,1)S(1)}, u32[]{:S(2)}, u32[]{:S(2)}) collective-permute-start(bf16[128,1024]{1,0:T(8,128)(2,1)S(1)} %bitcast.60), channel_id=1, source_target_pairs={{0,24},{1,193},{8,0},{9,201},{16,8},{17,209},{24,16},{25,217},{64,... | collective-permute-start | bytes 786440 | tf_op jit(solution)/shard_map/ppermute | solution.py:36
  32.2 10.0 %collective-permute-start.11 = (bf16[4,64,1024]{2,1,0:T(8,128)(2,1)S(1)}, bf16[4,64,1024]{2,1,0:T(8,128)(2,1)S(1)}, u32[]{:S(2)}, u32[]{:S(2)}) collective-permute-start(bf16[4,64,1024]{2,1,0:T(8,128)(2,1)S(1)} %pad_maximum_fusion.2.refs_0_), channel_id=1, source_target_pairs={{0,128},{1,17},{8,136},{9,25},{16,144},{17,1},{24,152},{25,9},{64,... | collective-permute-start | bytes 1572872 | tf_op jit(solution)/shard_map/ppermute | solution.py:36
  35.3 12.5 %collective-permute-start.12 = (bf16[4,64,1024]{2,1,0:T(8,128)(2,1)S(1)}, bf16[4,64,1024]{2,1,0:T(8,128)(2,1)S(1)}, u32[]{:S(2)}, u32[]{:S(2)}) collective-permute-start(bf16[4,64,1024]{2,1,0:T(8,128)(2,1)S(1)} %pad_maximum_fusion.2.refs_0_), channel_id=1, source_target_pairs={{0,64},{1,9},{8,72},{9,17},{16,80},{17,25},{24,88},{25,1},{64,128}... | collective-permute-start | bytes 1572872 | tf_op jit(solution)/shard_map/ppermute | solution.py:36
  35.6 12.5 %collective-permute-start.13 = (bf16[4,64,1024]{2,1,0:T(8,128)(2,1)S(1)}, bf16[4,64,1024]{2,1,0:T(8,128)(2,1)S(1)}, u32[]{:S(2)}, u32[]{:S(2)}) collective-permute-start(bf16[4,64,1024]{2,1,0:T(8,128)(2,1)S(1)} %pad_maximum_fusion.2.refs_0_), channel_id=1, source_target_pairs={{0,192},{1,25},{8,200},{9,1},{16,208},{17,9},{24,216},{25,17},{64,... | collective-permute-start | bytes 1572872 | tf_op jit(solution)/shard_map/ppermute | solution.py:36
  38.0 23.6 %collective-permute-start.4 = (bf16[4,64,1024]{2,1,0:T(8,128)(2,1)S(1)}, bf16[4,64,1024]{2,1,0:T(8,128)(2,1)S(1)}, u32[]{:S(2)}, u32[]{:S(2)}) collective-permute-start(bf16[4,64,1024]{2,1,0:T(8,128)(2,1)S(1)} %pad_maximum_fusion.1.refs_0_), channel_id=1, source_target_pairs={{0,128},{1,17},{8,136},{9,25},{16,144},{17,1},{24,152},{25,9},{64,... | collective-permute-start | bytes 1572872 | tf_op jit(solution)/shard_map/ppermute | solution.py:36
  38.1 23.5 %collective-permute-start.5 = (bf16[4,64,1024]{2,1,0:T(8,128)(2,1)S(1)}, bf16[4,64,1024]{2,1,0:T(8,128)(2,1)}, u32[]{:S(2)}, u32[]{:S(2)}) collective-permute-start(bf16[4,64,1024]{2,1,0:T(8,128)(2,1)S(1)} %pad_maximum_fusion.1.refs_0_), channel_id=1, source_target_pairs={{0,64},{1,9},{8,72},{9,17},{16,80},{17,25},{24,88},{25,1},{64,128}... | collective-permute-start | bytes 1572872 | tf_op jit(solution)/shard_map/ppermute | solution.py:36
  42.2 19.4 %collective-permute-start.6 = (bf16[4,64,1024]{2,1,0:T(8,128)(2,1)S(1)}, bf16[4,64,1024]{2,1,0:T(8,128)(2,1)}, u32[]{:S(2)}, u32[]{:S(2)}) collective-permute-start(bf16[4,64,1024]{2,1,0:T(8,128)(2,1)S(1)} %pad_maximum_fusion.1.refs_0_), channel_id=1, source_target_pairs={{0,192},{1,25},{8,200},{9,1},{16,208},{17,9},{24,216},{25,17},{64,... | collective-permute-start | bytes 1572872 | tf_op jit(solution)/shard_map/ppermute | solution.py:36
  51.2 5.4 %collective-permute-start.14 = (f32[256,256]{1,0:T(8,128)S(1)}, f32[256,256]{1,0:T(8,128)}, u32[]{:S(2)}, u32[]{:S(2)}) collective-permute-start(f32[256,256]{1,0:T(8,128)S(1)} %get-tuple-element.33.own), channel_id=1, source_target_pairs={{0,1},{1,0},{2,3},{3,2},{4,5},{5,4},{6,7},{7,6},{8,9},{9,8},{10,11... | collective-permute-start | bytes 786440 | tf_op jit(solution)/shard_map/ppermute | solution.py:40
  56.2 5.4 %copy-start.9 = (s32[2,16]{1,0:T(2,128)S(1)}, s32[2,16]{1,0:T(2,128)}, u32[]{:S(2)}) copy-start(s32[2,16]{1,0:T(2,128)} %copy-done.8) | copy-start | bytes 388
  56.2 5.5 %copy-start.12 = (f32[256]{0:T(256)S(1)}, f32[256]{0:T(256)}, u32[]{:S(2)}) copy-start(f32[256]{0:T(256)} %copy-done.11) | copy-start | bytes 3076
  59.5 13.9 %collective-permute-start.15 = (bf16[4,64,1024]{2,1,0:T(8,128)(2,1)S(1)}, bf16[4,64,1024]{2,1,0:T(8,128)(2,1)S(1)}, u32[]{:S(2)}, u32[]{:S(2)}) collective-permute-start(bf16[4,64,1024]{2,1,0:T(8,128)(2,1)S(1)} %get-tuple-element.35), channel_id=1, source_target_pairs={{0,128},{1,17},{8,136},{9,25},{16,144},{17,1},{24,152},{25,9},{64,... | collective-permute-start | bytes 1572872 | tf_op jit(solution)/shard_map/ppermute | solution.py:36
  65.3 4.9 %collective-permute-start.7 = (f32[256,256]{1,0:T(8,128)S(1)}, f32[256,256]{1,0:T(8,128)S(1)}, u32[]{:S(2)}, u32[]{:S(2)}) collective-permute-start(f32[256,256]{1,0:T(8,128)S(1)} %get-tuple-element.28.own), channel_id=1, source_target_pairs={{0,1},{1,0},{2,3},{3,2},{4,5},{5,4},{6,7},{7,6},{8,9},{9,8},{10,11... | collective-permute-start | bytes 786440 | tf_op jit(solution)/shard_map/ppermute | solution.py:40
  67.3 9.7 %collective-permute-start.16 = (bf16[4,64,1024]{2,1,0:T(8,128)(2,1)S(1)}, bf16[4,64,1024]{2,1,0:T(8,128)(2,1)S(1)}, u32[]{:S(2)}, u32[]{:S(2)}) collective-permute-start(bf16[4,64,1024]{2,1,0:T(8,128)(2,1)S(1)} %get-tuple-element.36), channel_id=1, source_target_pairs={{0,64},{1,9},{8,72},{9,17},{16,80},{17,25},{24,88},{25,1},{64,128}... | collective-permute-start | bytes 1572872 | tf_op jit(solution)/shard_map/ppermute | solution.py:36
  68.5 8.6 %collective-permute-start.17 = (bf16[4,64,1024]{2,1,0:T(8,128)(2,1)S(1)}, bf16[4,64,1024]{2,1,0:T(8,128)(2,1)S(1)}, u32[]{:S(2)}, u32[]{:S(2)}) collective-permute-start(bf16[4,64,1024]{2,1,0:T(8,128)(2,1)S(1)} %get-tuple-element.37), channel_id=1, source_target_pairs={{0,192},{1,25},{8,200},{9,1},{16,208},{17,9},{24,216},{25,17},{64,... | collective-permute-start | bytes 1572872 | tf_op jit(solution)/shard_map/ppermute | solution.py:36
  71.8 15.8 %collective-permute-start.10 = (bf16[4,64,1024]{2,1,0:T(8,128)(2,1)S(1)}, bf16[4,64,1024]{2,1,0:T(8,128)(2,1)S(1)}, u32[]{:S(2)}, u32[]{:S(2)}) collective-permute-start(bf16[4,64,1024]{2,1,0:T(8,128)(2,1)S(1)} %get-tuple-element.32), channel_id=1, source_target_pairs={{0,192},{1,25},{8,200},{9,1},{16,208},{17,9},{24,216},{25,17},{64,... | collective-permute-start | bytes 1572872 | tf_op jit(solution)/shard_map/ppermute | solution.py:36
  73.3 14.3 %collective-permute-start.8 = (bf16[4,64,1024]{2,1,0:T(8,128)(2,1)S(1)}, bf16[4,64,1024]{2,1,0:T(8,128)(2,1)S(1)}, u32[]{:S(2)}, u32[]{:S(2)}) collective-permute-start(bf16[4,64,1024]{2,1,0:T(8,128)(2,1)S(1)} %get-tuple-element.30), channel_id=1, source_target_pairs={{0,128},{1,17},{8,136},{9,25},{16,144},{17,1},{24,152},{25,9},{64,... | collective-permute-start | bytes 1572872 | tf_op jit(solution)/shard_map/ppermute | solution.py:36
  73.4 15.2 %collective-permute-start.9 = (bf16[4,64,1024]{2,1,0:T(8,128)(2,1)S(1)}, bf16[4,64,1024]{2,1,0:T(8,128)(2,1)S(1)}, u32[]{:S(2)}, u32[]{:S(2)}) collective-permute-start(bf16[4,64,1024]{2,1,0:T(8,128)(2,1)S(1)} %get-tuple-element.31), channel_id=1, source_target_pairs={{0,64},{1,9},{8,72},{9,17},{16,80},{17,25},{24,88},{25,1},{64,128}... | collective-permute-start | bytes 1572872 | tf_op jit(solution)/shard_map/ppermute | solution.py:36
  89.0 7.1 %collective-permute-start.18 = (bf16[128,1024]{1,0:T(8,128)(2,1)S(1)}, bf16[128,1024]{1,0:T(8,128)(2,1)S(1)}, u32[]{:S(2)}, u32[]{:S(2)}) collective-permute-start(bf16[128,1024]{1,0:T(8,128)(2,1)S(1)} %get-tuple-element.55), channel_id=1, source_target_pairs={{0,16},{1,129},{8,24},{9,137},{16,0},{17,145},{24,8},{25,153},{64,... | collective-permute-start | bytes 786440 | tf_op jit(solution)/shard_map/ppermute | solution.py:36
  90.5 8.4 %collective-permute-start.19 = (bf16[128,1024]{1,0:T(8,128)(2,1)S(1)}, bf16[128,1024]{1,0:T(8,128)(2,1)S(1)}, u32[]{:S(2)}, u32[]{:S(2)}) collective-permute-start(bf16[128,1024]{1,0:T(8,128)(2,1)S(1)} %get-tuple-element.57), channel_id=1, source_target_pairs={{0,8},{1,65},{8,16},{9,73},{16,24},{17,81},{24,0},{25,89},{64,72},... | collective-permute-start | bytes 786440 | tf_op jit(solution)/shard_map/ppermute | solution.py:36
  92.0 6.9 %collective-permute-start.20 = (bf16[128,1024]{1,0:T(8,128)(2,1)S(1)}, bf16[128,1024]{1,0:T(8,128)(2,1)S(1)}, u32[]{:S(2)}, u32[]{:S(2)}) collective-permute-start(bf16[128,1024]{1,0:T(8,128)(2,1)S(1)} %get-tuple-element.56), channel_id=1, source_target_pairs={{0,24},{1,193},{8,0},{9,201},{16,8},{17,209},{24,16},{25,217},{64,... | collective-permute-start | bytes 786440 | tf_op jit(solution)/shard_map/ppermute | solution.py:36
  99.8 12.7 %all-to-all-start.1 = ((bf16[8,16,1024]{2,1,0:T(8,128)(2,1)}), bf16[8,16,1024]{2,1,0:T(8,128)(2,1)S(1)}, u32[]{:S(2)}, u32[]{:S(2)}) async-start(bf16[8,16,1024]{2,1,0:T(8,128)(2,1)} %bitcast.19), calls=%async_computation.1 | async-start | bytes 524288 | tf_op jit(solution)/shard_map/all_to_all | solution.py:254
  125.2 28.5 %copy-start.10 = (s32[2,16]{1,0:T(2,128)S(1)}, s32[2,16]{1,0:T(2,128)}, u32[]{:S(2)}) copy-start(s32[2,16]{1,0:T(2,128)} %copy-done.8) | copy-start | bytes 388
  125.2 28.5 %copy-start.13 = (f32[256]{0:T(256)S(1)}, f32[256]{0:T(256)}, u32[]{:S(2)}) copy-start(f32[256]{0:T(256)} %copy-done.11) | copy-start | bytes 3076
  125.2 6.8 %collective-permute-start.21 = (bf16[128,1024]{1,0:T(8,128)(2,1)S(1)}, bf16[128,1024]{1,0:T(8,128)(2,1)S(1)}, u32[]{:S(2)}, u32[]{:S(2)}) collective-permute-start(bf16[128,1024]{1,0:T(8,128)(2,1)S(1)} %bitcast.62), channel_id=1, source_target_pairs={{0,16},{1,129},{8,24},{9,137},{16,0},{17,145},{24,8},{25,153},{64,... | collective-permute-start | bytes 786440 | tf_op jit(solution)/shard_map/ppermute | solution.py:36
  127.6 7.5 %collective-permute-start.22 = (bf16[128,1024]{1,0:T(8,128)(2,1)S(1)}, bf16[128,1024]{1,0:T(8,128)(2,1)S(1)}, u32[]{:S(2)}, u32[]{:S(2)}) collective-permute-start(bf16[128,1024]{1,0:T(8,128)(2,1)S(1)} %bitcast.63), channel_id=1, source_target_pairs={{0,8},{1,65},{8,16},{9,73},{16,24},{17,81},{24,0},{25,89},{64,72},... | collective-permute-start | bytes 786440 | tf_op jit(solution)/shard_map/ppermute | solution.py:36
  128.1 7.0 %collective-permute-start.23 = (bf16[128,1024]{1,0:T(8,128)(2,1)S(1)}, bf16[128,1024]{1,0:T(8,128)(2,1)S(1)}, u32[]{:S(2)}, u32[]{:S(2)}) collective-permute-start(bf16[128,1024]{1,0:T(8,128)(2,1)S(1)} %bitcast.64), channel_id=1, source_target_pairs={{0,24},{1,193},{8,0},{9,201},{16,8},{17,209},{24,16},{25,217},{64,... | collective-permute-start | bytes 786440 | tf_op jit(solution)/shard_map/ppermute | solution.py:36
  135.2 10.6 %collective-permute-start.27 = (bf16[4,64,1024]{2,1,0:T(8,128)(2,1)S(1)}, bf16[4,64,1024]{2,1,0:T(8,128)(2,1)S(1)}, u32[]{:S(2)}, u32[]{:S(2)}) collective-permute-start(bf16[4,64,1024]{2,1,0:T(8,128)(2,1)S(1)} %pad_maximum_fusion.4.refs_0_), channel_id=1, source_target_pairs={{0,128},{1,17},{8,136},{9,25},{16,144},{17,1},{24,152},{25,9},{64,... | collective-permute-start | bytes 1572872 | tf_op jit(solution)/shard_map/ppermute | solution.py:36
  135.8 15.7 %collective-permute-start.28 = (bf16[4,64,1024]{2,1,0:T(8,128)(2,1)S(1)}, bf16[4,64,1024]{2,1,0:T(8,128)(2,1)S(1)}, u32[]{:S(2)}, u32[]{:S(2)}) collective-permute-start(bf16[4,64,1024]{2,1,0:T(8,128)(2,1)S(1)} %pad_maximum_fusion.4.refs_0_), channel_id=1, source_target_pairs={{0,64},{1,9},{8,72},{9,17},{16,80},{17,25},{24,88},{25,1},{64,128}... | collective-permute-start | bytes 1572872 | tf_op jit(solution)/shard_map/ppermute | solution.py:36
  141.3 12.4 %collective-permute-start.29 = (bf16[4,64,1024]{2,1,0:T(8,128)(2,1)S(1)}, bf16[4,64,1024]{2,1,0:T(8,128)(2,1)S(1)}, u32[]{:S(2)}, u32[]{:S(2)}) collective-permute-start(bf16[4,64,1024]{2,1,0:T(8,128)(2,1)S(1)} %pad_maximum_fusion.4.refs_0_), channel_id=1, source_target_pairs={{0,192},{1,25},{8,200},{9,1},{16,208},{17,9},{24,216},{25,17},{64,... | collective-permute-start | bytes 1572872 | tf_op jit(solution)/shard_map/ppermute | solution.py:36
  143.7 17.1 %copy-start.5 = (bf16[256,4096]{1,0:T(8,128)(2,1)S(1)}, bf16[256,4096]{1,0:T(8,128)(2,1)}, u32[]{:S(2)}) copy-start(bf16[256,4096]{1,0:T(8,128)(2,1)} %copy-done.4) | copy-start | bytes 6291460
  143.7 19.0 %collective-permute-start.24 = (bf16[4,64,1024]{2,1,0:T(8,128)(2,1)S(1)}, bf16[4,64,1024]{2,1,0:T(8,128)(2,1)S(1)}, u32[]{:S(2)}, u32[]{:S(2)}) collective-permute-start(bf16[4,64,1024]{2,1,0:T(8,128)(2,1)S(1)} %pad_maximum_fusion.3.refs_0_), channel_id=1, source_target_pairs={{0,128},{1,17},{8,136},{9,25},{16,144},{17,1},{24,152},{25,9},{64,... | collective-permute-start | bytes 1572872 | tf_op jit(solution)/shard_map/ppermute | solution.py:36
  145.0 17.8 %collective-permute-start.25 = (bf16[4,64,1024]{2,1,0:T(8,128)(2,1)S(1)}, bf16[4,64,1024]{2,1,0:T(8,128)(2,1)S(1)}, u32[]{:S(2)}, u32[]{:S(2)}) collective-permute-start(bf16[4,64,1024]{2,1,0:T(8,128)(2,1)S(1)} %pad_maximum_fusion.3.refs_0_), channel_id=1, source_target_pairs={{0,64},{1,9},{8,72},{9,17},{16,80},{17,25},{24,88},{25,1},{64,128}... | collective-permute-start | bytes 1572872 | tf_op jit(solution)/shard_map/ppermute | solution.py:36
  145.8 19.2 %collective-permute-start.26 = (bf16[4,64,1024]{2,1,0:T(8,128)(2,1)S(1)}, bf16[4,64,1024]{2,1,0:T(8,128)(2,1)S(1)}, u32[]{:S(2)}, u32[]{:S(2)}) collective-permute-start(bf16[4,64,1024]{2,1,0:T(8,128)(2,1)S(1)} %pad_maximum_fusion.3.refs_0_), channel_id=1, source_target_pairs={{0,192},{1,25},{8,200},{9,1},{16,208},{17,9},{24,216},{25,17},{64,... | collective-permute-start | bytes 1572872 | tf_op jit(solution)/shard_map/ppermute | solution.py:36
  155.3 5.5 %collective-permute-start.30 = (f32[256,256]{1,0:T(8,128)S(1)}, f32[256,256]{1,0:T(8,128)S(1)}, u32[]{:S(2)}, u32[]{:S(2)}) collective-permute-start(f32[256,256]{1,0:T(8,128)S(1)} %get-tuple-element.38.own), channel_id=1, source_target_pairs={{0,1},{1,0},{2,3},{3,2},{4,5},{5,4},{6,7},{7,6},{8,9},{9,8},{10,11... | collective-permute-start | bytes 786440 | tf_op jit(solution)/shard_map/ppermute | solution.py:40
  162.7 9.3 %copy-start.3 = (bf16[256,4096]{1,0:T(8,128)(2,1)S(1)}, bf16[256,4096]{1,0:T(8,128)(2,1)}, u32[]{:S(2)}) copy-start(bf16[256,4096]{1,0:T(8,128)(2,1)} %copy-done.2) | copy-start | bytes 6291460
  166.6 5.4 %collective-permute-start.31 = (f32[256,256]{1,0:T(8,128)S(1)}, f32[256,256]{1,0:T(8,128)S(1)}, u32[]{:S(2)}, u32[]{:S(2)}) collective-permute-start(f32[256,256]{1,0:T(8,128)S(1)} %get-tuple-element.43.own), channel_id=1, source_target_pairs={{0,1},{1,0},{2,3},{3,2},{4,5},{5,4},{6,7},{7,6},{8,9},{9,8},{10,11... | collective-permute-start | bytes 786440 | tf_op jit(solution)/shard_map/ppermute | solution.py:40
  173.9 3.9 %collective-permute-start.32 = (bf16[128,4096]{1,0:T(8,128)(2,1)S(1)}, bf16[128,4096]{1,0:T(8,128)(2,1)S(1)}, u32[]{:S(2)}, u32[]{:S(2)}) collective-permute-start(bf16[128,4096]{1,0:T(8,128)(2,1)S(1)} %get-tuple-element.48), channel_id=1, source_target_pairs={{0,1},{1,0},{2,3},{3,2},{4,5},{5,4},{6,7},{7,6},{8,9},{9,8},{10,11... | collective-permute-start | bytes 3145736 | tf_op jit(solution)/shard_map/ppermute | solution.py:40
  (7 other events, 11.8 us)

commit v5 on v4

--- a/solution.py
+++ b/solution.py
@@ -17,6 +17,8 @@
 Z = ("zh", "zl")
 VMEM = pl.BlockSpec(memory_space=pltpu.VMEM)
 SMEM = pl.BlockSpec(memory_space=pltpu.SMEM)
+LAYOUT = ((0, (0, 1, 2, 3)), (-1, (0, 1, 2, 3)), (1, (0, 1, 2, 3)), (2, (0, 1)), (2, (2, 3)))
+PIECES = len(LAYOUT)
 PARAMS = pltpu.CompilerParams(vmem_limit_bytes=8 * 1024 * 1024)
 
 
@@ -40,25 +42,40 @@
     return lax.ppermute(value, "c", [(0, 1), (1, 0)])
 
 
-def spread(piece, last):
-    return [piece] + [shift(piece, by, last) for by in ORDER[1:]]
-
-
-def project_kernel(place, weight, extra, lift, *refs, centre):
-    pieces, (laid, product) = refs[:SIDE], refs[-2:]
+def spread(piece):
+    return [piece] + [shift(piece, by, False) for by in ORDER[1:]]
+
+
+def relay(piece):
+    behind, ahead = shift(piece, 1, True), shift(piece, SIDE - 1, True)
+    return [piece, behind, ahead, shift(behind[:2], 1, True), shift(ahead[2:], SIDE - 1, True)]
+
+
+def fold(own, up, down, far_up, far_down):
+    from_behind, from_ahead = shift(far_up, 1, True), shift(far_down, SIDE - 1, True)
+    up = jnp.concatenate([up[:2] + from_behind, up[2:]], 0)
+    down = jnp.concatenate([down[:2], down[2:] + from_ahead], 0)
+    from_behind, from_ahead = shift(up, 1, True), shift(down, SIDE - 1, True)
+    return (own.astype(F32) + from_behind.astype(F32) + from_ahead.astype(F32)).astype(BF16)
+
+
+def corner(me, away, j, thick, part):
+    last = (me[1] + (away + SIDE)) % SIDE
+    first = (me[2] + (SIDE - ORDER[j])) % SIDE
+    row, column = jnp.where(me[0] == 0, first, last), jnp.where(me[0] == 0, last, first)
+    return pl.multiple_of(row * thick, thick), pl.multiple_of(column * part, part)
+
+
+def project_kernel(me, weight, extra, lift, *refs, centre):
+    pieces, (laid, product) = refs[:PIECES], refs[-2:]
     thick, part = pieces[0].shape[1:]
-    for i, piece in enumerate(pieces):
-
-        def step(j, carry, i=i, piece=piece):
-            row = pl.multiple_of(place[0, i * SIDE + j] * thick, thick)
-            column = pl.multiple_of(place[1, i * SIDE + j] * part, part)
-            block = piece[j]
+    for piece, (away, blocks) in zip(pieces, LAYOUT):
+        for i, j in enumerate(blocks):
+            row, column = corner(me, away, j, thick, part)
+            block = piece[i]
             if centre:
                 block = (block.astype(F32) - extra[:, pl.ds(column, part)]).astype(BF16)
             laid[pl.ds(row, thick), pl.ds(column, part)] = block
-            return carry
-
-        lax.fori_loop(0, SIDE, step, 0)
     total = lift[...] if centre else None
     for q in range(SIDE):
         columns = pl.ds(q * part, part)
@@ -69,14 +86,14 @@
     product[...] = total
 
 
-def project(place, weight, extra, lift, pieces, centre, after=()):
+def project(me, weight, extra, lift, pieces, centre, after=()):
     thick, part = pieces[0].shape[1:]
     rows, width = thick * SIDE, part * SIDE
-    args = (place, weight, extra, lift, *pieces, *after)
+    args = (me, weight, extra, lift, *pieces, *after)
     return pl.pallas_call(
         functools.partial(project_kernel, centre=centre),
         out_shape=(jax.ShapeDtypeStruct((rows, width), BF16), jax.ShapeDtypeStruct((rows, weight.shape[0]), F32)),
-        in_specs=[SMEM] + [VMEM] * (3 + SIDE) + [pl.BlockSpec(memory_space=pl.ANY)] * len(after),
+        in_specs=[SMEM] + [VMEM] * (3 + PIECES) + [pl.BlockSpec(memory_space=pl.ANY)] * len(after),
         out_specs=(VMEM, VMEM),
         compiler_params=PARAMS,
         cost_estimate=pl.CostEstimate(
@@ -89,8 +106,8 @@
     return jnp.concatenate([own[:, :latents] + other[:, latents:], own[:, latents:] + other[:, :latents]], 1)
 
 
-def recon_kernel(place, own, other, weight, preact, flat, *refs):
-    blocks, (activity, laid) = refs[:SIDE], refs[SIDE:]
+def recon_kernel(me, own, other, weight, preact, flat, *refs):
+    blocks, (activity, laid) = refs[:PIECES], refs[PIECES:]
     _, thick, part = blocks[0].shape
     value = join(own[...], other[...], own.shape[1] // 2)
     preact[...] = value
@@ -100,32 +117,49 @@
     for q in range(SIDE):
         columns = pl.ds(q * part, part)
         laid[:, columns] = jnp.dot(activity[...], weight[:, columns], preferred_element_type=F32).astype(BF16)
-    for i, block in enumerate(blocks):
-
-        def step(j, carry, i=i, block=block):
-            row = pl.multiple_of(place[0, i * SIDE + j] * thick, thick)
-            column = pl.multiple_of(place[1, i * SIDE + j] * part, part)
-            block[j] = laid[pl.ds(row, thick), pl.ds(column, part)]
-            return carry
-
-        lax.fori_loop(0, SIDE, step, 0)
-
-
-def recon(place, own, other, weight):
+    for piece, (away, wanted) in zip(blocks, LAYOUT):
+        for i, j in enumerate(wanted):
+            row, column = corner(me, -away, j, thick, part)
+            piece[i] = laid[pl.ds(row, thick), pl.ds(column, part)]
+
+
+def recon(me, own, other, weight):
     rows, wide = own.shape
     width = weight.shape[1]
-    blocks = jax.ShapeDtypeStruct((SIDE, rows // SIDE, width // SIDE), BF16)
-    args = (place, own, other, weight)
-    shapes = (jax.ShapeDtypeStruct((rows, wide), F32), jax.ShapeDtypeStruct((wide, rows), BF16)) + (blocks,) * SIDE
+    args = (me, own, other, weight)
+    shapes = [jax.ShapeDtypeStruct((rows, wide), F32), jax.ShapeDtypeStruct((wide, rows), BF16)]
+    for _, wanted in LAYOUT:
+        shapes.append(jax.ShapeDtypeStruct((len(wanted), rows // SIDE, width // SIDE), BF16))
     return pl.pallas_call(
         recon_kernel,
-        out_shape=shapes,
+        out_shape=tuple(shapes),
         in_specs=[SMEM] + [VMEM] * 3,
         out_specs=(VMEM,) * len(shapes),
         scratch_shapes=[pltpu.VMEM((rows, wide), BF16), pltpu.VMEM((rows, width), BF16)],
         compiler_params=PARAMS,
         cost_estimate=pl.CostEstimate(flops=2 * rows * wide * width, bytes_accessed=4 * rows * width, transcendentals=0),
     )(*args)
+
+
+def error_kernel(me, parts, source, decoder, out):
+    thin, part = out.shape[1:]
+    x = jnp.where(me[0] == 0, me[1], me[2])
+    rows = pl.ds(pl.multiple_of(me[3] * thin, thin), thin)
+    value = jnp.sum(parts[...].astype(F32), 0) + decoder[:, pl.ds(pl.multiple_of(x * part, part), part)]
+    value = (value - source[rows, :].astype(F32)).astype(BF16)
+    for k in range(out.shape[0]):
+        out[k] = value
+
+
+def find_error(me, parts, source, decoder):
+    return pl.pallas_call(
+        error_kernel,
+        out_shape=jax.ShapeDtypeStruct(parts.shape, BF16),
+        in_specs=[SMEM] + [VMEM] * 3,
+        out_specs=VMEM,
+        compiler_params=PARAMS,
+        cost_estimate=pl.CostEstimate(flops=10 * parts.size, bytes_accessed=4 * parts.size, transcendentals=0),
+    )(me, parts, source, decoder)
 
 
 def gradient_kernel(own, other, preact, flat, error, centered, *refs, chunk, final):
@@ -208,15 +242,7 @@
     x, y, c = lax.axis_index("x"), lax.axis_index("y"), lax.axis_index("c")
     z = lax.axis_index(Z)
     last_me, first_me = jnp.where(c == 0, x, y), jnp.where(c == 0, y, x)
-    order = jnp.array(ORDER, jnp.int32)
-    behind_last = jnp.repeat((last_me - order) % SIDE, SIDE)
-    behind_first = jnp.tile((first_me - order) % SIDE, SIDE)
-    ahead_last = jnp.repeat((last_me + order) % SIDE, SIDE)
-
-    def places(last):
-        return jnp.stack([jnp.where(c == 0, behind_first, last), jnp.where(c == 0, last, behind_first)])
-
-    gather_place, send_place = places(behind_last), places(ahead_last)
+    me = jnp.stack([c, last_me, first_me, z]).astype(jnp.int32)
 
     own_columns = [lax.dynamic_slice_in_dim(inputs, core * half + x * part, part, 1) for core in range(2)]
     block = jnp.broadcast_to(jnp.stack(own_columns), (SIDE, 2) + own_columns[0].shape)
@@ -224,43 +250,34 @@
     block = block.reshape(-1, part)
     source = block
     split = source.shape[0] // CHUNKS
-    gathered = spread(source, False)
+    gathered = spread(source)
 
     taken = swap(lax.dynamic_slice_in_dim(weight, (1 - c) * half, half, 1))
     pair = jnp.concatenate([lax.dynamic_slice_in_dim(weight, c * half, half, 1), taken], 0)
     decoder = lax.dynamic_slice_in_dim(dec_bias, c * half, half, 0)[None, :]
     lift = jnp.concatenate([enc_bias, jnp.zeros_like(enc_bias)])[None, :]
     rows = source.shape[0] * SIDE
-    thin = split // 8
-    share = lax.dynamic_slice_in_dim(decoder, x * part, part, 1)
-
-    def reduce(blocks):
-        total = blocks[0].astype(F32)
-        for slot in (1, 2, 3):
-            total = total + shift(blocks[slot], ORDER[slot], True).astype(F32)
-        return total.astype(BF16)
+    thin = source.shape[0] // 8
 
     def fan(gathered):
-        return [spread(jnp.stack([g[k * split : (k + 1) * split] for g in gathered]), True) for k in chunks]
+        return [relay(jnp.stack([g[k * split : (k + 1) * split] for g in gathered])) for k in chunks]
 
     chunks = range(CHUNKS)
     pieces = fan(gathered)
-    ahead = [project(gather_place, pair, decoder, lift, pieces[k], True) for k in chunks]
-    made = [recon(send_place, ahead[k][1], swap(ahead[k][1]), pair) for k in chunks]
-    blocks = jnp.concatenate([reduce(made[k][2:]) for k in chunks], 1)
+    ahead = [project(me, pair, decoder, lift, pieces[k], True) for k in chunks]
+    made = [recon(me, ahead[k][1], swap(ahead[k][1]), pair) for k in chunks]
+    blocks = jnp.concatenate([fold(*made[k][2:]) for k in chunks], 1)
     strip = blocks[0].astype(F32)
     for by in ORDER[1:]:
         strip = strip + shift(blocks[ORDER.index(SIDE - by)], by, False).astype(F32)
-    parts = lax.all_to_all(strip.astype(BF16).reshape(8, CHUNKS * thin, part), Z, 0, 0, tiled=True)
-    recon_sum = jnp.sum(parts.astype(F32), 0)
-    here = lax.dynamic_slice_in_dim(source, z * CHUNKS * thin, CHUNKS * thin, 0).astype(F32)
-    error = (recon_sum + share - here).astype(BF16)
-    error = lax.all_to_all(jnp.broadcast_to(error, (8,) + error.shape), Z, 0, 0, tiled=True)
-    pieces = fan(spread(error.reshape(-1, part), False))
+    parts = lax.all_to_all(strip.astype(BF16).reshape(8, thin, part), Z, 0, 0, tiled=True)
+    error = find_error(me, parts, source, decoder)
+    error = lax.all_to_all(error, Z, 0, 0, tiled=True)
+    pieces = fan(spread(error.reshape(-1, part)))
     total = None
     for k in chunks:
         after = () if total is None else (total,)
-        laid, own = project(gather_place, pair, decoder, lift, pieces[k], False, after)
+        laid, own = project(me, pair, decoder, lift, pieces[k], False, after)
         total = gradient((own, swap(own), made[k][0], made[k][1], laid, ahead[k][0]), total)
     mine, theirs = total
     arrived = swap(theirs)

time: 184 us -> 195 us (1.060)
  blocking collectives: 11.9 us -> 23.6 us
  starting transfers between devices: 74.8 us -> 85.3 us
  local copies, waits for them, and re-layouts: 9.88 us -> 4.52 us
  waiting for transfers between devices: 58 us -> 54.1 us
    all_to_all x1 -> x2, blocking collectives: 11.9 us -> 23.6 us  [the longest x1 11.8 us: body(): lax.all_to_all(strip.astype(BF16).reshape(8, thin, part), Z, 0, 0, tiled=...]
    ppermute x27 -> x33, starting transfers between devices: 46.3 us -> 56.5 us  [shift(): return lax.ppermute(value, PLANE, plane_pairs(by, last))]
    all_to_all x1 -> x0, waiting for transfers between devices: 8.51 us -> none  [body(): lax.all_to_all(strip.astype(BF16).reshape(8, CHUNKS * thin, part), Z, 0,...]
    unnamed x40 -> x8, local copies, waits for them, and re-layouts: 4.35 us -> 0.01 us
    ppermute x6, starting transfers between devices: 15.1 us -> 18.8 us  [swap(): return lax.ppermute(value, 'c', [(0, 1), (1, 0)])]
    all_to_all x1 -> x0, starting transfers between devices: 3.41 us -> none  [body(): lax.all_to_all(strip.astype(BF16).reshape(8, CHUNKS * thin, part), Z, 0,...]
    ppermute x27 -> x33, waiting for transfers between devices: 39.7 us -> 42.8 us  [shift(): return lax.ppermute(value, PLANE, plane_pairs(by, last))]
    all_to_all x1, waiting for transfers between devices: 7.07 us -> 10.1 us  [body(): lax.all_to_all(block.reshape((8,) + own_columns[0].shape), ('zh', 'c'), 0...]
  transfers between devices with their start and end apart: 35 -> 40, of which waited for: 21 -> 14; matrix products, arithmetic and copies ran while one was open for 3% -> 3% of each run, Pallas kernels for 8% -> 7%
where the time goes in v5:
time: 195 us; the launch traced here: 192 us
  starting transfers between devices  85.3 us (44%)
  waiting for transfers between devices  54.1 us (28%)
  blocking collectives  23.6 us (12%)
  Pallas kernels  20.2 us (10%)
  local copies, waits for them, and re-layouts  4.52 us (2%)
  other arithmetic  2.91 us (1%)
    ppermute x33, starting transfers between devices, shift(): return lax.ppermute(value, PLANE, plane_pairs(by, last))  56.5 us
    ppermute x33, waiting for transfers between devices, shift(): return lax.ppermute(value, PLANE, plane_pairs(by, last))  42.8 us
    ppermute x6, starting transfers between devices, swap(): return lax.ppermute(value, 'c', [(0, 1), (1, 0)])  18.8 us
    all_to_all x1, blocking collectives, body(): lax.all_to_all(strip.astype(BF16).reshape(8, thin, part), Z, 0, 0, tiled=...  11.8 us
    all_to_all x1, blocking collectives, body(): error = lax.all_to_all(error, Z, 0, 0, tiled=True)  11.7 us
    all_to_all x1, waiting for transfers between devices, body(): lax.all_to_all(block.reshape((8,) + own_columns[0].shape), ('zh', 'c'), 0...  10.1 us
    all_to_all x1, starting transfers between devices, body(): lax.all_to_all(block.reshape((8,) + own_columns[0].shape), ('zh', 'c'), 0...  9.97 us
    pallas_call x2, Pallas kernels, adam(): pl.pallas_call(functools.partial(adam_kernel, rows=rows), out_shape=(jax....  6.85 us
  transfers between devices with their start and end apart: 40, of which 14 were waited for; matrix products, arithmetic and copies ran while one was open for 3% of the time, Pallas kernels for 7%

profile of v5, /device:TPU:1, one launch (start us, length us, event | category | flops | bytes accessed | tf_op | source)
XLA Modules:
  0.0 191.8 jit_solution(12697572102885317606)
XLA Ops:
  2.2 10.0 %all-to-all-start = ((bf16[8,16,1024]{2,1,0:T(8,128)(2,1)}), bf16[8,16,1024]{2,1,0:T(8,128)(2,1)S(1)}, u32[]{:S(2)}, u32[]{:S(2)}) async-start(bf16[8,16,1024]{2,1,0:T(8,128)(2,1)} %bitcast.8), calls=%async_computation | async-start | bytes 524288 | tf_op jit(solution)/shard_map/all_to_all | solution.py:249
  12.1 10.1 %all-to-all-done = bf16[8,16,1024]{2,1,0:T(8,128)(2,1)S(1)} async-done(((bf16[8,16,1024]{2,1,0:T(8,128)(2,1)}), bf16[8,16,1024]{2,1,0:T(8,128)(2,1)S(1)}, u32[]{:S(2)}, u32[]{:S(2)}) %all-to-all-start) | async-done | bytes 262176 | tf_op jit(solution)/shard_map/all_to_all | solution.py:249
  22.2 2.7 %collective-permute-start.1 = (bf16[128,1024]{1,0:T(8,128)(2,1)S(1)}, bf16[128,1024]{1,0:T(8,128)(2,1)S(1)}, u32[]{:S(2)}, u32[]{:S(2)}) collective-permute-start(bf16[128,1024]{1,0:T(8,128)(2,1)S(1)} %bitcast.53), channel_id=1, source_target_pairs={{0,16},{1,129},{8,24},{9,137},{16,0},{17,145},{24,8},{25,153},{64,... | collective-permute-start | bytes 786440 | tf_op jit(solution)/shard_map/ppermute | solution.py:38
  25.0 2.7 %constant_dynamic-slice_fusion.1 = (bf16[128,4096]{1,0:T(8,128)(2,1)S(1)}, bf16[128,4096]{1,0:T(8,128)(2,1)}) fusion(bf16[128,8192]{1,0:T(8,128)(2,1)} %param.8, s32[]{:T(128)S(6)} %select_n.22, s32[]{:T(128)S(6)} %select_n.23), kind=kLoop, calls=%fused_computation.49 | loop fusion | bytes 4194312 | tf_op jit(solution)/shard_map/dynamic_slice | solution.py:256
  27.7 2.8 %collective-permute-start = (bf16[128,4096]{1,0:T(8,128)(2,1)}, bf16[128,4096]{1,0:T(8,128)(2,1)}, u32[]{:S(2)}, u32[]{:S(2)}) collective-permute-start(bf16[128,4096]{1,0:T(8,128)(2,1)} %get-tuple-element.58), channel_id=1, source_target_pairs={{0,1},{1,0},{2,3},{3,2},{4,5},{5,4},{6,7},{7,6},{8,9},{9,8},{10,11... | collective-permute-start | bytes 3145736 | tf_op jit(solution)/shard_map/ppermute | solution.py:42
  31.7 1.5 collective-permute-start.3
  33.2 4.0 %collective-permute-done.2 = bf16[128,1024]{1,0:T(8,128)(2,1)S(1)} collective-permute-done((bf16[128,1024]{1,0:T(8,128)(2,1)S(1)}, bf16[128,1024]{1,0:T(8,128)(2,1)S(1)}, u32[]{:S(2)}, u32[]{:S(2)}) %collective-permute-start.2) | collective-permute-done | bytes 262176 | tf_op jit(solution)/shard_map/ppermute | solution.py:38
  37.5 2.6 %collective-permute-start.14 = (bf16[4,64,1024]{2,1,0:T(8,128)(2,1)S(1)}, bf16[4,64,1024]{2,1,0:T(8,128)(2,1)S(1)}, u32[]{:S(2)}, u32[]{:S(2)}) collective-permute-start(bf16[4,64,1024]{2,1,0:T(8,128)(2,1)S(1)} %pad_maximum_fusion.4.refs_0_), channel_id=1, source_target_pairs={{0,192},{1,25},{8,200},{9,1},{16,208},{17,9},{24,216},{25,17},{64,... | collective-permute-start | bytes 1572872 | tf_op jit(solution)/shard_map/ppermute | solution.py:38
  40.3 2.7 %collective-permute-start.5 = (bf16[4,64,1024]{2,1,0:T(8,128)(2,1)S(1)}, bf16[4,64,1024]{2,1,0:T(8,128)(2,1)S(1)}, u32[]{:S(2)}, u32[]{:S(2)}) collective-permute-start(bf16[4,64,1024]{2,1,0:T(8,128)(2,1)S(1)} %pad_maximum_fusion.1.refs_0_), channel_id=1, source_target_pairs={{0,192},{1,25},{8,200},{9,1},{16,208},{17,9},{24,216},{25,17},{64,... | collective-permute-start | bytes 1572872 | tf_op jit(solution)/shard_map/ppermute | solution.py:38
  43.0 3.9 %collective-permute-done.13.refs_1_ = bf16[4,64,1024]{2,1,0:T(8,128)(2,1)S(1)} collective-permute-done((bf16[4,64,1024]{2,1,0:T(8,128)(2,1)S(1)}, bf16[4,64,1024]{2,1,0:T(8,128)(2,1)S(1)}, u32[]{:S(2)}, u32[]{:S(2)}) %collective-permute-start.13) | collective-permute-done | bytes 524320 | tf_op jit(solution)/shard_map/ppermute | solution.py:38
  47.1 2.7 %collective-permute-start.16 = (bf16[2,64,1024]{2,1,0:T(8,128)(2,1)S(1)}, bf16[2,64,1024]{2,1,0:T(8,128)(2,1)S(1)}, u32[]{:S(2)}, u32[]{:S(2)}) collective-permute-start(bf16[2,64,1024]{2,1,0:T(8,128)(2,1)S(1)} %slice.159), channel_id=1, source_target_pairs={{0,192},{1,25},{8,200},{9,1},{16,208},{17,9},{24,216},{25,17},{64,... | collective-permute-start | bytes 786440 | tf_op jit(solution)/shard_map/ppermute | solution.py:38
  49.8 1.4 pad_maximum_fusion.weight
  52.7 2.7 %collective-permute-start.7 = (bf16[2,64,1024]{2,1,0:T(8,128)(2,1)S(1)}, bf16[2,64,1024]{2,1,0:T(8,128)(2,1)S(1)}, u32[]{:S(2)}, u32[]{:S(2)}) collective-permute-start(bf16[2,64,1024]{2,1,0:T(8,128)(2,1)S(1)} %slice.153), channel_id=1, source_target_pairs={{0,192},{1,25},{8,200},{9,1},{16,208},{17,9},{24,216},{25,17},{64,... | collective-permute-start | bytes 786440 | tf_op jit(solution)/shard_map/ppermute | solution.py:38
  55.5 1.7 shard_map.87
  57.2 2.7 %collective-permute-start.17 = (f32[256,256]{1,0:T(8,128)S(1)}, f32[256,256]{1,0:T(8,128)S(1)}, u32[]{:S(2)}, u32[]{:S(2)}) collective-permute-start(f32[256,256]{1,0:T(8,128)S(1)} %get-tuple-element.36.own), channel_id=1, source_target_pairs={{0,1},{1,0},{2,3},{3,2},{4,5},{5,4},{6,7},{7,6},{8,9},{9,8},{10,11... | collective-permute-start | bytes 786440 | tf_op jit(solution)/shard_map/ppermute | solution.py:42
  59.9 1.7 shard_map.85
  61.6 2.3 %collective-permute-start.8 = (f32[256,256]{1,0:T(8,128)S(1)}, f32[256,256]{1,0:T(8,128)S(1)}, u32[]{:S(2)}, u32[]{:S(2)}) collective-permute-start(f32[256,256]{1,0:T(8,128)S(1)} %get-tuple-element.30.own), channel_id=1, source_target_pairs={{0,1},{1,0},{2,3},{3,2},{4,5},{5,4},{6,7},{7,6},{8,9},{9,8},{10,11... | collective-permute-start | bytes 786440 | tf_op jit(solution)/shard_map/ppermute | solution.py:42
  63.8 1.4 shard_map.88
  65.4 3.0 %collective-permute-start.20 = (bf16[2,64,1024]{2,1,0:T(8,128)(2,1)S(1)}, bf16[2,64,1024]{2,1,0:T(8,128)(2,1)S(1)}, u32[]{:S(2)}, u32[]{:S(2)}) collective-permute-start(bf16[2,64,1024]{2,1,0:T(8,128)(2,1)S(1)} %get-tuple-element.41), channel_id=1, source_target_pairs={{0,192},{1,25},{8,200},{9,1},{16,208},{17,9},{24,216},{25,17},{64,... | collective-permute-start | bytes 786440 | tf_op jit(solution)/shard_map/ppermute | solution.py:38
  68.4 1.4 shard_map.86
  69.9 2.7 %collective-permute-start.11 = (bf16[2,64,1024]{2,1,0:T(8,128)(2,1)S(1)}, bf16[2,64,1024]{2,1,0:T(8,128)(2,1)S(1)}, u32[]{:S(2)}, u32[]{:S(2)}) collective-permute-start(bf16[2,64,1024]{2,1,0:T(8,128)(2,1)S(1)} %get-tuple-element.35), channel_id=1, source_target_pairs={{0,192},{1,25},{8,200},{9,1},{16,208},{17,9},{24,216},{25,17},{64,... | collective-permute-start | bytes 786440 | tf_op jit(solution)/shard_map/ppermute | solution.py:38
  72.8 2.7 %collective-permute-start.21 = (bf16[4,64,1024]{2,1,0:T(8,128)(2,1)S(1)}, bf16[4,64,1024]{2,1,0:T(8,128)(2,1)S(1)}, u32[]{:S(2)}, u32[]{:S(2)}) collective-permute-start(bf16[4,64,1024]{2,1,0:T(8,128)(2,1)S(1)} %pad_maximum_fusion.6), channel_id=1, source_target_pairs={{0,192},{1,25},{8,200},{9,1},{16,208},{17,9},{24,216},{25,17},{64,... | collective-permute-start | bytes 1572872 | tf_op jit(solution)/shard_map/ppermute | solution.py:38
  76.9 2.7 %collective-permute-start.12 = (bf16[4,64,1024]{2,1,0:T(8,128)(2,1)S(1)}, bf16[4,64,1024]{2,1,0:T(8,128)(2,1)S(1)}, u32[]{:S(2)}, u32[]{:S(2)}) collective-permute-start(bf16[4,64,1024]{2,1,0:T(8,128)(2,1)S(1)} %pad_maximum_fusion.3), channel_id=1, source_target_pairs={{0,192},{1,25},{8,200},{9,1},{16,208},{17,9},{24,216},{25,17},{64,... | collective-permute-start | bytes 1572872 | tf_op jit(solution)/shard_map/ppermute | solution.py:38
  79.6 2.6 %collective-permute-done.19 = bf16[4,64,1024]{2,1,0:T(8,128)(2,1)S(1)} collective-permute-done((bf16[4,64,1024]{2,1,0:T(8,128)(2,1)S(1)}, bf16[4,64,1024]{2,1,0:T(8,128)(2,1)S(1)}, u32[]{:S(2)}, u32[]{:S(2)}) %collective-permute-start.19) | collective-permute-done | bytes 524320 | tf_op jit(solution)/shard_map/ppermute | solution.py:38
  82.5 5.3 %collective-permute-done.10 = bf16[4,64,1024]{2,1,0:T(8,128)(2,1)S(1)} collective-permute-done((bf16[4,64,1024]{2,1,0:T(8,128)(2,1)S(1)}, bf16[4,64,1024]{2,1,0:T(8,128)(2,1)S(1)}, u32[]{:S(2)}, u32[]{:S(2)}) %collective-permute-start.10) | collective-permute-done | bytes 524320 | tf_op jit(solution)/shard_map/ppermute | solution.py:38
  88.2 1.4 collective-permute-start.22
  89.6 2.3 %collective-permute-start.23 = (bf16[128,1024]{1,0:T(8,128)(2,1)S(1)}, bf16[128,1024]{1,0:T(8,128)(2,1)S(1)}, u32[]{:S(2)}, u32[]{:S(2)}) collective-permute-start(bf16[128,1024]{1,0:T(8,128)(2,1)S(1)} %get-tuple-element.61), channel_id=1, source_target_pairs={{0,8},{1,65},{8,16},{9,73},{16,24},{17,81},{24,0},{25,89},{64,72},... | collective-permute-start | bytes 786440 | tf_op jit(solution)/shard_map/ppermute | solution.py:38
  91.9 10.0 %collective-permute-start.24 = (bf16[128,1024]{1,0:T(8,128)(2,1)S(1)}, bf16[128,1024]{1,0:T(8,128)(2,1)S(1)}, u32[]{:S(2)}, u32[]{:S(2)}) collective-permute-start(bf16[128,1024]{1,0:T(8,128)(2,1)S(1)} %get-tuple-element.60), channel_id=1, source_target_pairs={{0,24},{1,193},{8,0},{9,201},{16,8},{17,209},{24,16},{25,217},{64,... | collective-permute-start | bytes 786440 | tf_op jit(solution)/shard_map/ppermute | solution.py:38
  101.9 5.1 %collective-permute-done.24 = bf16[128,1024]{1,0:T(8,128)(2,1)S(1)} collective-permute-done((bf16[128,1024]{1,0:T(8,128)(2,1)S(1)}, bf16[128,1024]{1,0:T(8,128)(2,1)S(1)}, u32[]{:S(2)}, u32[]{:S(2)}) %collective-permute-start.24) | collective-permute-done | bytes 262176 | tf_op jit(solution)/shard_map/ppermute | solution.py:38
  107.2 11.8 %all_to_all.15.parts = bf16[8,16,1024]{2,1,0:T(8,128)(2,1)S(1)} all-to-all(bf16[8,16,1024]{2,1,0:T(8,128)(2,1)S(1)} %bitcast.69), channel_id=1, replica_groups=mesh['x'=4,'zl'=2,'y'=4,'zh'=4,'c'=2] {'zh','zl'}, dimensions={0} | all-to-all | bytes 524288 | tf_op jit(solution)/shard_map/all_to_all | solution.py:273
  119.7 11.7 %all_to_all.16 = bf16[8,16,1024]{2,1,0:T(8,128)(2,1)S(1)} all-to-all(bf16[8,16,1024]{2,1,0:T(8,128)(2,1)S(1)} %shard_map.89), channel_id=1, replica_groups=mesh['x'=4,'zl'=2,'y'=4,'zh'=4,'c'=2] {'zh','zl'}, dimensions={0} | all-to-all | bytes 524288 | tf_op jit(solution)/shard_map/all_to_all | solution.py:275
  131.8 1.4 collective-permute-start.26
  134.5 3.7 %collective-permute-done.25 = bf16[128,1024]{1,0:T(8,128)(2,1)S(1)} collective-permute-done((bf16[128,1024]{1,0:T(8,128)(2,1)S(1)}, bf16[128,1024]{1,0:T(8,128)(2,1)S(1)}, u32[]{:S(2)}, u32[]{:S(2)}) %collective-permute-start.25) | collective-permute-done | bytes 262176 | tf_op jit(solution)/shard_map/ppermute | solution.py:38
  138.3 2.7 %collective-permute-done.26 = bf16[128,1024]{1,0:T(8,128)(2,1)S(1)} collective-permute-done((bf16[128,1024]{1,0:T(8,128)(2,1)S(1)}, bf16[128,1024]{1,0:T(8,128)(2,1)S(1)}, u32[]{:S(2)}, u32[]{:S(2)}) %collective-permute-start.26) | collective-permute-done | bytes 262176 | tf_op jit(solution)/shard_map/ppermute | solution.py:38
  141.2 3.3 %collective-permute-start.33 = (bf16[4,64,1024]{2,1,0:T(8,128)(2,1)S(1)}, bf16[4,64,1024]{2,1,0:T(8,128)(2,1)S(1)}, u32[]{:S(2)}, u32[]{:S(2)}) collective-permute-start(bf16[4,64,1024]{2,1,0:T(8,128)(2,1)S(1)} %pad_maximum_fusion.8.refs_0_), channel_id=1, source_target_pairs={{0,192},{1,25},{8,200},{9,1},{16,208},{17,9},{24,216},{25,17},{64,... | collective-permute-start | bytes 1572872 | tf_op jit(solution)/shard_map/ppermute | solution.py:38
  144.6 2.7 %collective-permute-start.29 = (bf16[4,64,1024]{2,1,0:T(8,128)(2,1)S(1)}, bf16[4,64,1024]{2,1,0:T(8,128)(2,1)S(1)}, u32[]{:S(2)}, u32[]{:S(2)}) collective-permute-start(bf16[4,64,1024]{2,1,0:T(8,128)(2,1)S(1)} %pad_maximum_fusion.7.refs_0_), channel_id=1, source_target_pairs={{0,192},{1,25},{8,200},{9,1},{16,208},{17,9},{24,216},{25,17},{64,... | collective-permute-start | bytes 1572872 | tf_op jit(solution)/shard_map/ppermute | solution.py:38
  147.3 5.0 %collective-permute-done.32.refs_1_ = bf16[4,64,1024]{2,1,0:T(8,128)(2,1)S(1)} collective-permute-done((bf16[4,64,1024]{2,1,0:T(8,128)(2,1)S(1)}, bf16[4,64,1024]{2,1,0:T(8,128)(2,1)S(1)}, u32[]{:S(2)}, u32[]{:S(2)}) %collective-permute-start.32) | collective-permute-done | bytes 524320 | tf_op jit(solution)/shard_map/ppermute | solution.py:38
  152.5 2.7 %collective-permute-start.35 = (bf16[2,64,1024]{2,1,0:T(8,128)(2,1)S(1)}, bf16[2,64,1024]{2,1,0:T(8,128)(2,1)S(1)}, u32[]{:S(2)}, u32[]{:S(2)}) collective-permute-start(bf16[2,64,1024]{2,1,0:T(8,128)(2,1)S(1)} %slice.177), channel_id=1, source_target_pairs={{0,192},{1,25},{8,200},{9,1},{16,208},{17,9},{24,216},{25,17},{64,... | collective-permute-start | bytes 786440 | tf_op jit(solution)/shard_map/ppermute | solution.py:38
  155.2 5.8 %collective-permute-done.34.refs_3_ = bf16[2,64,1024]{2,1,0:T(8,128)(2,1)S(1)} collective-permute-done((bf16[2,64,1024]{2,1,0:T(8,128)(2,1)S(1)}, bf16[2,64,1024]{2,1,0:T(8,128)(2,1)S(1)}, u32[]{:S(2)}, u32[]{:S(2)}) %collective-permute-start.34) | collective-permute-done | bytes 262176 | tf_op jit(solution)/shard_map/ppermute | solution.py:38
  161.1 1.4 shard_map.90
  162.5 9.3 %collective-permute-start.36 = (f32[256,256]{1,0:T(8,128)S(1)}, f32[256,256]{1,0:T(8,128)S(1)}, u32[]{:S(2)}, u32[]{:S(2)}) collective-permute-start(f32[256,256]{1,0:T(8,128)S(1)} %get-tuple-element.42.own), channel_id=1, source_target_pairs={{0,1},{1,0},{2,3},{3,2},{4,5},{5,4},{6,7},{7,6},{8,9},{9,8},{10,11... | collective-permute-start | bytes 786440 | tf_op jit(solution)/shard_map/ppermute | solution.py:42
  171.9 2.7 %collective-permute-start.31 = (bf16[2,64,1024]{2,1,0:T(8,128)(2,1)S(1)}, bf16[2,64,1024]{2,1,0:T(8,128)(2,1)S(1)}, u32[]{:S(2)}, u32[]{:S(2)}) collective-permute-start(bf16[2,64,1024]{2,1,0:T(8,128)(2,1)S(1)} %slice.171), channel_id=1, source_target_pairs={{0,192},{1,25},{8,200},{9,1},{16,208},{17,9},{24,216},{25,17},{64,... | collective-permute-start | bytes 786440 | tf_op jit(solution)/shard_map/ppermute | solution.py:38
  174.6 1.9 shard_map.91.refs_5_.refs_0_
  176.5 2.1 %collective-permute-done.30.refs_3_ = bf16[2,64,1024]{2,1,0:T(8,128)(2,1)S(1)} collective-permute-done((bf16[2,64,1024]{2,1,0:T(8,128)(2,1)S(1)}, bf16[2,64,1024]{2,1,0:T(8,128)(2,1)S(1)}, u32[]{:S(2)}, u32[]{:S(2)}) %collective-permute-start.30) | collective-permute-done | bytes 262176 | tf_op jit(solution)/shard_map/ppermute | solution.py:38
  178.6 1.4 shard_map.92
  182.4 1.9 shard_map.93
  184.8 3.4 %shard_map.94 = (bf16[128,8192]{1,0:T(8,128)(2,1)}, bf16[128,8192]{1,0:T(8,128)(2,1)}, bf16[128,8192]{1,0:T(8,128)(2,1)}) custom-call(s32[1]{0:T(128)} %bitcast.at, f32[128,4096]{1,0:T(8,128)S(1)} %get-tuple-element.53.gradient_ref, bf16[128,8192]{1,0:T(8,128)(2,1)S(1)} %copy-done, bf16[128,8192]{1,0:T(8,128)(2,1)S(1)} %copy-done.1), custom_call_target="tpu_custom_call" | custom-call | flops 10485760 | bytes 7340032 | tf_op jit(solution)/shard_map/pallas_call | solution.py:223
  188.2 3.4 %shard_map.95 = (bf16[128,8192]{1,0:T(8,128)(2,1)}, bf16[128,8192]{1,0:T(8,128)(2,1)}, bf16[128,8192]{1,0:T(8,128)(2,1)}) custom-call(s32[1]{0:T(128)S(6)} %sub.6.at, bf16[128,4096]{1,0:T(8,128)(2,1)S(1)} %collective-permute-done.38.gradient_ref, bf16[128,8192]{1,0:T(8,128)(2,1)S(1)} %copy-done, ...), custom_call_target="tpu_custom_call", output_to_operand_aliasing={{0}: (4, {}), {1}: (5, {}), {2}: (6, {})} | custom-call | flops 10485760 | bytes 7340032 | tf_op jit(solution)/shard_map/pallas_call | solution.py:223
  (93 shorter events, 13.2 us)
Async XLA Ops:
  2.2 20.1 %all-to-all-start = ((bf16[8,16,1024]{2,1,0:T(8,128)(2,1)}), bf16[8,16,1024]{2,1,0:T(8,128)(2,1)S(1)}, u32[]{:S(2)}, u32[]{:S(2)}) async-start(bf16[8,16,1024]{2,1,0:T(8,128)(2,1)} %bitcast.8), calls=%async_computation | async-start | bytes 524288 | tf_op jit(solution)/shard_map/all_to_all | solution.py:249
  22.2 10.9 %collective-permute-start.1 = (bf16[128,1024]{1,0:T(8,128)(2,1)S(1)}, bf16[128,1024]{1,0:T(8,128)(2,1)S(1)}, u32[]{:S(2)}, u32[]{:S(2)}) collective-permute-start(bf16[128,1024]{1,0:T(8,128)(2,1)S(1)} %bitcast.53), channel_id=1, source_target_pairs={{0,16},{1,129},{8,24},{9,137},{16,0},{17,145},{24,8},{25,153},{64,... | collective-permute-start | bytes 786440 | tf_op jit(solution)/shard_map/ppermute | solution.py:38
  27.7 15.3 %copy-start.2 = (f32[8192]{0:T(1024)S(1)}, f32[8192]{0:T(1024)}, u32[]{:S(2)}) copy-start(f32[8192]{0:T(1024)} %param.7) | copy-start | bytes 98308
  27.7 15.3 %copy-start.3 = (f32[128]{0:T(128)S(1)}, f32[128]{0:T(128)}, u32[]{:S(2)}) copy-start(f32[128]{0:T(128)} %param.9) | copy-start | bytes 1540
  27.7 22.2 %collective-permute-start = (bf16[128,4096]{1,0:T(8,128)(2,1)}, bf16[128,4096]{1,0:T(8,128)(2,1)}, u32[]{:S(2)}, u32[]{:S(2)}) collective-permute-start(bf16[128,4096]{1,0:T(8,128)(2,1)} %get-tuple-element.58), channel_id=1, source_target_pairs={{0,1},{1,0},{2,3},{3,2},{4,5},{5,4},{6,7},{7,6},{8,9},{9,8},{10,11... | collective-permute-start | bytes 3145736 | tf_op jit(solution)/shard_map/ppermute | solution.py:42
  30.5 6.7 %collective-permute-start.2 = (bf16[128,1024]{1,0:T(8,128)(2,1)S(1)}, bf16[128,1024]{1,0:T(8,128)(2,1)S(1)}, u32[]{:S(2)}, u32[]{:S(2)}) collective-permute-start(bf16[128,1024]{1,0:T(8,128)(2,1)S(1)} %bitcast.54), channel_id=1, source_target_pairs={{0,8},{1,65},{8,16},{9,73},{16,24},{17,81},{24,0},{25,89},{64,72},... | collective-permute-start | bytes 786440 | tf_op jit(solution)/shard_map/ppermute | solution.py:38
  31.7 5.5 %collective-permute-start.3 = (bf16[128,1024]{1,0:T(8,128)(2,1)S(1)}, bf16[128,1024]{1,0:T(8,128)(2,1)S(1)}, u32[]{:S(2)}, u32[]{:S(2)}) collective-permute-start(bf16[128,1024]{1,0:T(8,128)(2,1)S(1)} %bitcast.55), channel_id=1, source_target_pairs={{0,24},{1,193},{8,0},{9,201},{16,8},{17,209},{24,16},{25,217},{64,... | collective-permute-start | bytes 786440 | tf_op jit(solution)/shard_map/ppermute | solution.py:38
  37.3 9.6 %collective-permute-start.13 = (bf16[4,64,1024]{2,1,0:T(8,128)(2,1)S(1)}, bf16[4,64,1024]{2,1,0:T(8,128)(2,1)S(1)}, u32[]{:S(2)}, u32[]{:S(2)}) collective-permute-start(bf16[4,64,1024]{2,1,0:T(8,128)(2,1)S(1)} %pad_maximum_fusion.4.refs_0_), channel_id=1, source_target_pairs={{0,64},{1,9},{8,72},{9,17},{16,80},{17,25},{24,88},{25,1},{64,128}... | collective-permute-start | bytes 1572872 | tf_op jit(solution)/shard_map/ppermute | solution.py:38
  37.5 9.5 %collective-permute-start.14 = (bf16[4,64,1024]{2,1,0:T(8,128)(2,1)S(1)}, bf16[4,64,1024]{2,1,0:T(8,128)(2,1)S(1)}, u32[]{:S(2)}, u32[]{:S(2)}) collective-permute-start(bf16[4,64,1024]{2,1,0:T(8,128)(2,1)S(1)} %pad_maximum_fusion.4.refs_0_), channel_id=1, source_target_pairs={{0,192},{1,25},{8,200},{9,1},{16,208},{17,9},{24,216},{25,17},{64,... | collective-permute-start | bytes 1572872 | tf_op jit(solution)/shard_map/ppermute | solution.py:38
  40.2 12.4 %collective-permute-start.4 = (bf16[4,64,1024]{2,1,0:T(8,128)(2,1)S(1)}, bf16[4,64,1024]{2,1,0:T(8,128)(2,1)S(1)}, u32[]{:S(2)}, u32[]{:S(2)}) collective-permute-start(bf16[4,64,1024]{2,1,0:T(8,128)(2,1)S(1)} %pad_maximum_fusion.1.refs_0_), channel_id=1, source_target_pairs={{0,64},{1,9},{8,72},{9,17},{16,80},{17,25},{24,88},{25,1},{64,128}... | collective-permute-start | bytes 1572872 | tf_op jit(solution)/shard_map/ppermute | solution.py:38
  40.3 12.4 %collective-permute-start.5 = (bf16[4,64,1024]{2,1,0:T(8,128)(2,1)S(1)}, bf16[4,64,1024]{2,1,0:T(8,128)(2,1)S(1)}, u32[]{:S(2)}, u32[]{:S(2)}) collective-permute-start(bf16[4,64,1024]{2,1,0:T(8,128)(2,1)S(1)} %pad_maximum_fusion.1.refs_0_), channel_id=1, source_target_pairs={{0,192},{1,25},{8,200},{9,1},{16,208},{17,9},{24,216},{25,17},{64,... | collective-permute-start | bytes 1572872 | tf_op jit(solution)/shard_map/ppermute | solution.py:38
  47.0 8.5 %collective-permute-start.15 = (bf16[2,64,1024]{2,1,0:T(8,128)(2,1)S(1)}, bf16[2,64,1024]{2,1,0:T(8,128)(2,1)S(1)}, u32[]{:S(2)}, u32[]{:S(2)}) collective-permute-start(bf16[2,64,1024]{2,1,0:T(8,128)(2,1)S(1)} %slice.158), channel_id=1, source_target_pairs={{0,64},{1,9},{8,72},{9,17},{16,80},{17,25},{24,88},{25,1},{64,128}... | collective-permute-start | bytes 786440 | tf_op jit(solution)/shard_map/ppermute | solution.py:38
  47.1 8.4 %collective-permute-start.16 = (bf16[2,64,1024]{2,1,0:T(8,128)(2,1)S(1)}, bf16[2,64,1024]{2,1,0:T(8,128)(2,1)S(1)}, u32[]{:S(2)}, u32[]{:S(2)}) collective-permute-start(bf16[2,64,1024]{2,1,0:T(8,128)(2,1)S(1)} %slice.159), channel_id=1, source_target_pairs={{0,192},{1,25},{8,200},{9,1},{16,208},{17,9},{24,216},{25,17},{64,... | collective-permute-start | bytes 786440 | tf_op jit(solution)/shard_map/ppermute | solution.py:38
  52.6 7.3 %collective-permute-start.6 = (bf16[2,64,1024]{2,1,0:T(8,128)(2,1)S(1)}, bf16[2,64,1024]{2,1,0:T(8,128)(2,1)S(1)}, u32[]{:S(2)}, u32[]{:S(2)}) collective-permute-start(bf16[2,64,1024]{2,1,0:T(8,128)(2,1)S(1)} %slice.152), channel_id=1, source_target_pairs={{0,64},{1,9},{8,72},{9,17},{16,80},{17,25},{24,88},{25,1},{64,128}... | collective-permute-start | bytes 786440 | tf_op jit(solution)/shard_map/ppermute | solution.py:38
  52.7 7.1 %collective-permute-start.7 = (bf16[2,64,1024]{2,1,0:T(8,128)(2,1)S(1)}, bf16[2,64,1024]{2,1,0:T(8,128)(2,1)S(1)}, u32[]{:S(2)}, u32[]{:S(2)}) collective-permute-start(bf16[2,64,1024]{2,1,0:T(8,128)(2,1)S(1)} %slice.153), channel_id=1, source_target_pairs={{0,192},{1,25},{8,200},{9,1},{16,208},{17,9},{24,216},{25,17},{64,... | collective-permute-start | bytes 786440 | tf_op jit(solution)/shard_map/ppermute | solution.py:38
  57.2 6.7 %collective-permute-start.17 = (f32[256,256]{1,0:T(8,128)S(1)}, f32[256,256]{1,0:T(8,128)S(1)}, u32[]{:S(2)}, u32[]{:S(2)}) collective-permute-start(f32[256,256]{1,0:T(8,128)S(1)} %get-tuple-element.36.own), channel_id=1, source_target_pairs={{0,1},{1,0},{2,3},{3,2},{4,5},{5,4},{6,7},{7,6},{8,9},{9,8},{10,11... | collective-permute-start | bytes 786440 | tf_op jit(solution)/shard_map/ppermute | solution.py:42
  61.6 6.8 %collective-permute-start.8 = (f32[256,256]{1,0:T(8,128)S(1)}, f32[256,256]{1,0:T(8,128)S(1)}, u32[]{:S(2)}, u32[]{:S(2)}) collective-permute-start(f32[256,256]{1,0:T(8,128)S(1)} %get-tuple-element.30.own), channel_id=1, source_target_pairs={{0,1},{1,0},{2,3},{3,2},{4,5},{5,4},{6,7},{7,6},{8,9},{9,8},{10,11... | collective-permute-start | bytes 786440 | tf_op jit(solution)/shard_map/ppermute | solution.py:42
  65.3 7.3 %collective-permute-start.18 = (bf16[2,64,1024]{2,1,0:T(8,128)(2,1)S(1)}, bf16[2,64,1024]{2,1,0:T(8,128)(2,1)S(1)}, u32[]{:S(2)}, u32[]{:S(2)}) collective-permute-start(bf16[2,64,1024]{2,1,0:T(8,128)(2,1)S(1)} %get-tuple-element.39), channel_id=1, source_target_pairs={{0,64},{1,9},{8,72},{9,17},{16,80},{17,25},{24,88},{25,1},{64,128}... | collective-permute-start | bytes 786440 | tf_op jit(solution)/shard_map/ppermute | solution.py:38
  65.4 7.4 %collective-permute-start.20 = (bf16[2,64,1024]{2,1,0:T(8,128)(2,1)S(1)}, bf16[2,64,1024]{2,1,0:T(8,128)(2,1)S(1)}, u32[]{:S(2)}, u32[]{:S(2)}) collective-permute-start(bf16[2,64,1024]{2,1,0:T(8,128)(2,1)S(1)} %get-tuple-element.41), channel_id=1, source_target_pairs={{0,192},{1,25},{8,200},{9,1},{16,208},{17,9},{24,216},{25,17},{64,... | collective-permute-start | bytes 786440 | tf_op jit(solution)/shard_map/ppermute | solution.py:38
  69.8 6.8 %collective-permute-start.9 = (bf16[2,64,1024]{2,1,0:T(8,128)(2,1)S(1)}, bf16[2,64,1024]{2,1,0:T(8,128)(2,1)S(1)}, u32[]{:S(2)}, u32[]{:S(2)}) collective-permute-start(bf16[2,64,1024]{2,1,0:T(8,128)(2,1)S(1)} %get-tuple-element.33), channel_id=1, source_target_pairs={{0,64},{1,9},{8,72},{9,17},{16,80},{17,25},{24,88},{25,1},{64,128}... | collective-permute-start | bytes 786440 | tf_op jit(solution)/shard_map/ppermute | solution.py:38
  69.9 6.9 %collective-permute-start.11 = (bf16[2,64,1024]{2,1,0:T(8,128)(2,1)S(1)}, bf16[2,64,1024]{2,1,0:T(8,128)(2,1)S(1)}, u32[]{:S(2)}, u32[]{:S(2)}) collective-permute-start(bf16[2,64,1024]{2,1,0:T(8,128)(2,1)S(1)} %get-tuple-element.35), channel_id=1, source_target_pairs={{0,192},{1,25},{8,200},{9,1},{16,208},{17,9},{24,216},{25,17},{64,... | collective-permute-start | bytes 786440 | tf_op jit(solution)/shard_map/ppermute | solution.py:38
  72.6 9.6 %collective-permute-start.19 = (bf16[4,64,1024]{2,1,0:T(8,128)(2,1)S(1)}, bf16[4,64,1024]{2,1,0:T(8,128)(2,1)S(1)}, u32[]{:S(2)}, u32[]{:S(2)}) collective-permute-start(bf16[4,64,1024]{2,1,0:T(8,128)(2,1)S(1)} %pad_maximum_fusion.5), channel_id=1, source_target_pairs={{0,64},{1,9},{8,72},{9,17},{16,80},{17,25},{24,88},{25,1},{64,128}... | collective-permute-start | bytes 1572872 | tf_op jit(solution)/shard_map/ppermute | solution.py:38
  72.8 9.4 %collective-permute-start.21 = (bf16[4,64,1024]{2,1,0:T(8,128)(2,1)S(1)}, bf16[4,64,1024]{2,1,0:T(8,128)(2,1)S(1)}, u32[]{:S(2)}, u32[]{:S(2)}) collective-permute-start(bf16[4,64,1024]{2,1,0:T(8,128)(2,1)S(1)} %pad_maximum_fusion.6), channel_id=1, source_target_pairs={{0,192},{1,25},{8,200},{9,1},{16,208},{17,9},{24,216},{25,17},{64,... | collective-permute-start | bytes 1572872 | tf_op jit(solution)/shard_map/ppermute | solution.py:38
  76.7 11.2 %collective-permute-start.10 = (bf16[4,64,1024]{2,1,0:T(8,128)(2,1)S(1)}, bf16[4,64,1024]{2,1,0:T(8,128)(2,1)S(1)}, u32[]{:S(2)}, u32[]{:S(2)}) collective-permute-start(bf16[4,64,1024]{2,1,0:T(8,128)(2,1)S(1)} %pad_maximum_fusion.2), channel_id=1, source_target_pairs={{0,64},{1,9},{8,72},{9,17},{16,80},{17,25},{24,88},{25,1},{64,128}... | collective-permute-start | bytes 1572872 | tf_op jit(solution)/shard_map/ppermute | solution.py:38
  76.9 11.0 %collective-permute-start.12 = (bf16[4,64,1024]{2,1,0:T(8,128)(2,1)S(1)}, bf16[4,64,1024]{2,1,0:T(8,128)(2,1)S(1)}, u32[]{:S(2)}, u32[]{:S(2)}) collective-permute-start(bf16[4,64,1024]{2,1,0:T(8,128)(2,1)S(1)} %pad_maximum_fusion.3), channel_id=1, source_target_pairs={{0,192},{1,25},{8,200},{9,1},{16,208},{17,9},{24,216},{25,17},{64,... | collective-permute-start | bytes 1572872 | tf_op jit(solution)/shard_map/ppermute | solution.py:38
  88.2 13.7 %collective-permute-start.22 = (bf16[128,1024]{1,0:T(8,128)(2,1)S(1)}, bf16[128,1024]{1,0:T(8,128)(2,1)S(1)}, u32[]{:S(2)}, u32[]{:S(2)}) collective-permute-start(bf16[128,1024]{1,0:T(8,128)(2,1)S(1)} %get-tuple-element.59), channel_id=1, source_target_pairs={{0,16},{1,129},{8,24},{9,137},{16,0},{17,145},{24,8},{25,153},{64,... | collective-permute-start | bytes 786440 | tf_op jit(solution)/shard_map/ppermute | solution.py:38
  89.6 12.3 %collective-permute-start.23 = (bf16[128,1024]{1,0:T(8,128)(2,1)S(1)}, bf16[128,1024]{1,0:T(8,128)(2,1)S(1)}, u32[]{:S(2)}, u32[]{:S(2)}) collective-permute-start(bf16[128,1024]{1,0:T(8,128)(2,1)S(1)} %get-tuple-element.61), channel_id=1, source_target_pairs={{0,8},{1,65},{8,16},{9,73},{16,24},{17,81},{24,0},{25,89},{64,72},... | collective-permute-start | bytes 786440 | tf_op jit(solution)/shard_map/ppermute | solution.py:38
  91.9 15.1 %collective-permute-start.24 = (bf16[128,1024]{1,0:T(8,128)(2,1)S(1)}, bf16[128,1024]{1,0:T(8,128)(2,1)S(1)}, u32[]{:S(2)}, u32[]{:S(2)}) collective-permute-start(bf16[128,1024]{1,0:T(8,128)(2,1)S(1)} %get-tuple-element.60), channel_id=1, source_target_pairs={{0,24},{1,193},{8,0},{9,201},{16,8},{17,209},{24,16},{25,217},{64,... | collective-permute-start | bytes 786440 | tf_op jit(solution)/shard_map/ppermute | solution.py:38
  131.4 6.8 %collective-permute-start.25 = (bf16[128,1024]{1,0:T(8,128)(2,1)S(1)}, bf16[128,1024]{1,0:T(8,128)(2,1)S(1)}, u32[]{:S(2)}, u32[]{:S(2)}) collective-permute-start(bf16[128,1024]{1,0:T(8,128)(2,1)S(1)} %bitcast.66), channel_id=1, source_target_pairs={{0,16},{1,129},{8,24},{9,137},{16,0},{17,145},{24,8},{25,153},{64,... | collective-permute-start | bytes 786440 | tf_op jit(solution)/shard_map/ppermute | solution.py:38
  131.8 9.1 %collective-permute-start.26 = (bf16[128,1024]{1,0:T(8,128)(2,1)S(1)}, bf16[128,1024]{1,0:T(8,128)(2,1)S(1)}, u32[]{:S(2)}, u32[]{:S(2)}) collective-permute-start(bf16[128,1024]{1,0:T(8,128)(2,1)S(1)} %bitcast.67), channel_id=1, source_target_pairs={{0,8},{1,65},{8,16},{9,73},{16,24},{17,81},{24,0},{25,89},{64,72},... | collective-permute-start | bytes 786440 | tf_op jit(solution)/shard_map/ppermute | solution.py:38
  133.2 7.8 %collective-permute-start.27 = (bf16[128,1024]{1,0:T(8,128)(2,1)S(1)}, bf16[128,1024]{1,0:T(8,128)(2,1)S(1)}, u32[]{:S(2)}, u32[]{:S(2)}) collective-permute-start(bf16[128,1024]{1,0:T(8,128)(2,1)S(1)} %bitcast.68), channel_id=1, source_target_pairs={{0,24},{1,193},{8,0},{9,201},{16,8},{17,209},{24,16},{25,217},{64,... | collective-permute-start | bytes 786440 | tf_op jit(solution)/shard_map/ppermute | solution.py:38
  141.1 11.3 %collective-permute-start.32 = (bf16[4,64,1024]{2,1,0:T(8,128)(2,1)S(1)}, bf16[4,64,1024]{2,1,0:T(8,128)(2,1)S(1)}, u32[]{:S(2)}, u32[]{:S(2)}) collective-permute-start(bf16[4,64,1024]{2,1,0:T(8,128)(2,1)S(1)} %pad_maximum_fusion.8.refs_0_), channel_id=1, source_target_pairs={{0,64},{1,9},{8,72},{9,17},{16,80},{17,25},{24,88},{25,1},{64,128}... | collective-permute-start | bytes 1572872 | tf_op jit(solution)/shard_map/ppermute | solution.py:38
  141.2 11.3 %collective-permute-start.33 = (bf16[4,64,1024]{2,1,0:T(8,128)(2,1)S(1)}, bf16[4,64,1024]{2,1,0:T(8,128)(2,1)S(1)}, u32[]{:S(2)}, u32[]{:S(2)}) collective-permute-start(bf16[4,64,1024]{2,1,0:T(8,128)(2,1)S(1)} %pad_maximum_fusion.8.refs_0_), channel_id=1, source_target_pairs={{0,192},{1,25},{8,200},{9,1},{16,208},{17,9},{24,216},{25,17},{64,... | collective-permute-start | bytes 1572872 | tf_op jit(solution)/shard_map/ppermute | solution.py:38
  144.5 27.2 %collective-permute-start.28 = (bf16[4,64,1024]{2,1,0:T(8,128)(2,1)S(1)}, bf16[4,64,1024]{2,1,0:T(8,128)(2,1)S(1)}, u32[]{:S(2)}, u32[]{:S(2)}) collective-permute-start(bf16[4,64,1024]{2,1,0:T(8,128)(2,1)S(1)} %pad_maximum_fusion.7.refs_0_), channel_id=1, source_target_pairs={{0,64},{1,9},{8,72},{9,17},{16,80},{17,25},{24,88},{25,1},{64,128}... | collective-permute-start | bytes 1572872 | tf_op jit(solution)/shard_map/ppermute | solution.py:38
  144.6 27.2 %collective-permute-start.29 = (bf16[4,64,1024]{2,1,0:T(8,128)(2,1)S(1)}, bf16[4,64,1024]{2,1,0:T(8,128)(2,1)S(1)}, u32[]{:S(2)}, u32[]{:S(2)}) collective-permute-start(bf16[4,64,1024]{2,1,0:T(8,128)(2,1)S(1)} %pad_maximum_fusion.7.refs_0_), channel_id=1, source_target_pairs={{0,192},{1,25},{8,200},{9,1},{16,208},{17,9},{24,216},{25,17},{64,... | collective-permute-start | bytes 1572872 | tf_op jit(solution)/shard_map/ppermute | solution.py:38
  152.4 8.7 %collective-permute-start.34 = (bf16[2,64,1024]{2,1,0:T(8,128)(2,1)S(1)}, bf16[2,64,1024]{2,1,0:T(8,128)(2,1)S(1)}, u32[]{:S(2)}, u32[]{:S(2)}) collective-permute-start(bf16[2,64,1024]{2,1,0:T(8,128)(2,1)S(1)} %slice.176), channel_id=1, source_target_pairs={{0,64},{1,9},{8,72},{9,17},{16,80},{17,25},{24,88},{25,1},{64,128}... | collective-permute-start | bytes 786440 | tf_op jit(solution)/shard_map/ppermute | solution.py:38
  152.5 8.6 %collective-permute-start.35 = (bf16[2,64,1024]{2,1,0:T(8,128)(2,1)S(1)}, bf16[2,64,1024]{2,1,0:T(8,128)(2,1)S(1)}, u32[]{:S(2)}, u32[]{:S(2)}) collective-permute-start(bf16[2,64,1024]{2,1,0:T(8,128)(2,1)S(1)} %slice.177), channel_id=1, source_target_pairs={{0,192},{1,25},{8,200},{9,1},{16,208},{17,9},{24,216},{25,17},{64,... | collective-permute-start | bytes 786440 | tf_op jit(solution)/shard_map/ppermute | solution.py:38
  162.5 12.1 %collective-permute-start.36 = (f32[256,256]{1,0:T(8,128)S(1)}, f32[256,256]{1,0:T(8,128)S(1)}, u32[]{:S(2)}, u32[]{:S(2)}) collective-permute-start(f32[256,256]{1,0:T(8,128)S(1)} %get-tuple-element.42.own), channel_id=1, source_target_pairs={{0,1},{1,0},{2,3},{3,2},{4,5},{5,4},{6,7},{7,6},{8,9},{9,8},{10,11... | collective-permute-start | bytes 786440 | tf_op jit(solution)/shard_map/ppermute | solution.py:42
  171.8 6.8 %collective-permute-start.30 = (bf16[2,64,1024]{2,1,0:T(8,128)(2,1)S(1)}, bf16[2,64,1024]{2,1,0:T(8,128)(2,1)S(1)}, u32[]{:S(2)}, u32[]{:S(2)}) collective-permute-start(bf16[2,64,1024]{2,1,0:T(8,128)(2,1)S(1)} %slice.170), channel_id=1, source_target_pairs={{0,64},{1,9},{8,72},{9,17},{16,80},{17,25},{24,88},{25,1},{64,128}... | collective-permute-start | bytes 786440 | tf_op jit(solution)/shard_map/ppermute | solution.py:38
  171.9 6.7 %collective-permute-start.31 = (bf16[2,64,1024]{2,1,0:T(8,128)(2,1)S(1)}, bf16[2,64,1024]{2,1,0:T(8,128)(2,1)S(1)}, u32[]{:S(2)}, u32[]{:S(2)}) collective-permute-start(bf16[2,64,1024]{2,1,0:T(8,128)(2,1)S(1)} %slice.171), channel_id=1, source_target_pairs={{0,192},{1,25},{8,200},{9,1},{16,208},{17,9},{24,216},{25,17},{64,... | collective-permute-start | bytes 786440 | tf_op jit(solution)/shard_map/ppermute | solution.py:38
  180.0 2.4 %collective-permute-start.37 = (f32[256,256]{1,0:T(8,128)S(1)}, f32[256,256]{1,0:T(8,128)S(1)}, u32[]{:S(2)}, u32[]{:S(2)}) collective-permute-start(f32[256,256]{1,0:T(8,128)S(1)} %get-tuple-element.47.own), channel_id=1, source_target_pairs={{0,1},{1,0},{2,3},{3,2},{4,5},{5,4},{6,7},{7,6},{8,9},{9,8},{10,11... | collective-permute-start | bytes 786440 | tf_op jit(solution)/shard_map/ppermute | solution.py:42
  182.4 2.3 %copy-start = (bf16[128,8192]{1,0:T(8,128)(2,1)S(1)}, bf16[128,8192]{1,0:T(8,128)(2,1)}, u32[]{:S(2)}) copy-start(bf16[128,8192]{1,0:T(8,128)(2,1)} %first_ref.3) | copy-start | bytes 6291460
  182.4 2.3 %copy-start.1 = (bf16[128,8192]{1,0:T(8,128)(2,1)S(1)}, bf16[128,8192]{1,0:T(8,128)(2,1)}, u32[]{:S(2)}) copy-start(bf16[128,8192]{1,0:T(8,128)(2,1)} %second_ref.3) | copy-start | bytes 6291460
  184.3 3.9 %collective-permute-start.38 = (bf16[128,4096]{1,0:T(8,128)(2,1)S(1)}, bf16[128,4096]{1,0:T(8,128)(2,1)S(1)}, u32[]{:S(2)}, u32[]{:S(2)}) collective-permute-start(bf16[128,4096]{1,0:T(8,128)(2,1)S(1)} %get-tuple-element.52), channel_id=1, source_target_pairs={{0,1},{1,0},{2,3},{3,2},{4,5},{5,4},{6,7},{7,6},{8,9},{9,8},{10,11... | collective-permute-start | bytes 3145736 | tf_op jit(solution)/shard_map/ppermute | solution.py:42
